TPU v7x, 256 devices: a whole 4x4x8 slice. The times are simulated.
256 devices in a mesh: seq: 32 (over z, x), row: 4 (over y), col: 2 (over core).
Axes of the slice: x: 4, y: 4, z: 8, core: 2. Of those that a mesh axis runs over, the one named last changes fastest.
Arguments:
- tokens: bfloat16 [16384, 4608], P(('seq', 'row'), 'col')
- norm_gain: float32 [4608], replicated, may hold values from 0.5 to 2
- w_query: bfloat16 [4608, 2048], P('row', 'col'), may hold values from -0.09375 to 0.09375
- w_keyval: bfloat16 [4608, 2, 1024], P('row', None, 'col'), may hold values from -0.09375 to 0.09375
- active: int32 [32], replicated, may hold values from 64 to 512, as said below
Outputs:
- attended: bfloat16 [16384, 2048], P(('seq', 'row'), 'col')
Inputs may be any that keep to these rules, and one draw needn't show every extreme that they name: active tokens of each shard form a prefix of it; in every draw one shard is wholly active.
All inputs are finite; a program needn't handle non-finite values.
Results may differ from a plain program's by a relative error of at most 0.0084.
Values may be sent and summed in bfloat16 or wider, within the bound.
No kernel may reach another device: no remote copies, remote signals or barrier semaphores. Data moves between devices by JAX's collectives and lax.ppermute only.
A program may use at most 192 MiB of HBM per device.

v0:
```python
import jax
import jax.numpy as jnp
from jax import lax
from jax.sharding import PartitionSpec as P

HEAD = 128
WINDOW = 4096
SEQ_MAX = 8192


SCALE = 1.0 / 12.0
SOFTCAP = 50.0
EPSILON = 1e-06


def shifted(value, axis, steps):
    count = lax.axis_size(axis)
    leading, last = (max(0, -steps), min(count, count - steps))
    return lax.ppermute(value, axis, [(source, source + steps) for source in range(leading, last)])


def rotate(vectors, positions):
    half_width = vectors.shape[-1] // 2
    freqs = 10000.0 ** (-2.0 * jnp.arange(half_width, dtype=jnp.float32) / vectors.shape[-1])
    angles = positions.astype(jnp.float32)[:, None] * freqs[None, :]
    cosine = jnp.cos(angles)[:, None, :]
    sine = jnp.sin(angles)[:, None, :]
    first = vectors[..., :half_width]
    second = vectors[..., half_width:]
    return jnp.concatenate([first * cosine - second * sine, second * cosine + first * sine], -1)


def on_device(tokens, norm_gain, w_query, w_keyval, active):
    row_count = tokens.shape[0]
    shard_count = lax.axis_size("seq")
    row_groups = lax.axis_size("row")
    tok_shard = row_count * row_groups
    seq_length = min(SEQ_MAX, tok_shard * shard_count)
    seq_index = lax.axis_index("seq")
    row_index = lax.axis_index("row")
    head_size = HEAD
    query_cols = w_query.shape[1]
    keyval_cols = w_keyval.shape[2]
    local_heads = query_cols // head_size
    local_kv = keyval_cols // head_size
    positions = (
        seq_index * tok_shard + row_index * row_count + jnp.arange(row_count, dtype=jnp.int32)
    )
    in_sequence = positions % seq_length
    query_seq = jnp.floor_divide(positions, seq_length)
    shard_ids = jnp.arange(shard_count, dtype=jnp.int32)

    def limit_of(where_at):
        shard_of = jnp.floor_divide(where_at, tok_shard)
        return jnp.sum(jnp.where(shard_of[:, None] == shard_ids[None, :], active[None, :], 0), 1)

    whole = lax.all_gather(tokens, "col", axis=1, tiled=True)
    floated = whole.astype(jnp.float32)
    meansq = jnp.mean(floated * floated, -1, keepdims=True)
    normed = (floated * lax.rsqrt(meansq + EPSILON) * norm_gain).astype(jnp.bfloat16)
    slab_width = w_query.shape[0]
    shard_normed = lax.all_gather(normed, "row", axis=0, tiled=True)
    own_slab = lax.dynamic_slice_in_dim(shard_normed, row_index * slab_width, slab_width, 1)
    flat_keyval = w_keyval.reshape(slab_width, 2 * keyval_cols)
    summed = lax.psum_scatter(
        jnp.concatenate(
            [
                jnp.dot(own_slab, w_query, preferred_element_type=jnp.float32),
                jnp.dot(own_slab, flat_keyval, preferred_element_type=jnp.float32),
            ],
            1,
        ),
        "row",
        scatter_dimension=0,
        tiled=True,
    )
    query_raw = summed[:, :query_cols]
    keyval_raw = summed[:, query_cols:].reshape(row_count, 2, keyval_cols)
    query = rotate(query_raw.reshape(row_count, local_heads, head_size), in_sequence).astype(
        jnp.bfloat16
    )
    rotated_keys = rotate(keyval_raw[:, 0].reshape(row_count, local_kv, head_size), in_sequence)
    keyval = jnp.stack([rotated_keys.reshape(row_count, keyval_cols), keyval_raw[:, 1]], 1).astype(
        jnp.bfloat16
    )
    shard_kv = lax.all_gather(keyval, "row", axis=0, tiled=True)
    query_groups = query.reshape(row_count, local_kv, local_heads // local_kv, head_size)
    query_live = positions % tok_shard < limit_of(positions)

    def attend(carry, kv_piece, key_start):
        key_count = kv_piece.shape[0]
        key_pos = key_start + jnp.arange(key_count, dtype=jnp.int32)
        key_live = (key_pos >= 0) & (key_pos % tok_shard < limit_of(key_pos))
        key_seq = jnp.floor_divide(key_pos + seq_length * 4096, seq_length) - 4096
        mask = (
            key_live[None, :]
            & (key_seq[None, :] == query_seq[:, None])
            & (key_pos[None, :] <= positions[:, None])
            & (key_pos[None, :] > positions[:, None] - WINDOW)
        )
        key_heads = kv_piece[:, 0].reshape(key_count, local_kv, head_size)
        value_heads = kv_piece[:, 1].reshape(key_count, local_kv, head_size)
        scores = (
            jnp.einsum(
                "rgjd,kgd->rgjk", query_groups, key_heads, preferred_element_type=jnp.float32
            )
            * SCALE
        )
        scores = SOFTCAP * jnp.tanh(scores / SOFTCAP)
        weights = jnp.where(mask[:, None, None, :], jnp.exp(scores), 0.0).astype(jnp.bfloat16)
        numer = carry[0] + jnp.einsum(
            "rgjk,kgd->rgjd", weights, value_heads, preferred_element_type=jnp.float32
        )
        denom = carry[1] + jnp.sum(weights.astype(jnp.float32), -1)
        return (numer, denom)

    initial_sums = (
        jnp.zeros((row_count, local_kv, local_heads // local_kv, head_size), jnp.float32),
        jnp.zeros((row_count, local_kv, local_heads // local_kv), jnp.float32),
    )
    span_count = WINDOW // tok_shard
    doublings = span_count.bit_length() - 1
    carried = shard_kv
    for section_index in range(doublings + 1):
        moved = shifted(carried, "seq", 1 if section_index == 0 else 2 ** (section_index - 1))
        carried = moved if section_index == 0 else jnp.concatenate([moved, carried], 0)
    block_count = carried.shape[0] // tok_shard
    stacked = carried.reshape(block_count, tok_shard, 2, keyval_cols)
    starts = (seq_index - span_count) * tok_shard + tok_shard * jnp.arange(
        block_count, dtype=jnp.int32
    )

    def step_block(state, inputs):
        return (attend(state, inputs[0], inputs[1]), None)

    result, unused = lax.scan(step_block, initial_sums, (stacked, starts))
    partial_sums = result
    numer, denom = attend(partial_sums, shard_kv, seq_index * tok_shard)
    safe = jnp.where(query_live[:, None, None], denom, 1.0)
    result = numer / safe[..., None]
    result = jnp.where(query_live[:, None, None, None], result, 0.0)
    return result.reshape(row_count, query_cols).astype(jnp.bfloat16)


def solution(mesh):
    placed = (P(("seq", "row"), "col"), P(), P("row", "col"), P("row", None, "col"), P())
    return jax.shard_map(
        on_device, mesh=mesh, in_specs=placed, out_specs=P(("seq", "row"), "col"), check_vma=False
    )
```

profile of v0, /device:TPU:64, one launch (start us, length us, event | category | flops | bytes accessed | tf_op | source)
XLA Modules:
  0.0 471.6 jit_solution(12263841838949607252)
XLA Ops:
  7.3 18.7 %all-gather.4.cloned.1.call-done = bf16[128,4608]{1,0:T(8,128)(2,1)} async-done(((bf16[128,2304]{1,0:T(8,128)(2,1)}), bf16[128,4608]{1,0:T(8,128)(2,1)}) %all-gather.4.cloned.1.call-update) | async-done | bytes 1179664 | tf_op jit(solution)/shard_map/all_gather | solution.py:57
  27.6 2.7 fusion.21
  30.3 3.7 copy.50
  34.1 52.9 %all-gather.6.cloned.1.call-done = bf16[512,4608]{1,0:T(8,128)(2,1)} async-done(((bf16[128,4608]{1,0:T(8,128)(2,1)}), bf16[512,4608]{1,0:T(8,128)(2,1)}) %all-gather.6.cloned.1.call-update) | async-done | bytes 4718608 | tf_op jit(solution)/shard_map/all_gather | solution.py:62
  86.9 3.6 fusion.27
  90.5 2.8 fusion.29
  93.3 2.5 pad_maximum_fusion.1
  96.1 49.7 %reduce-scatter.2.cloned.1.call-done = f32[128,2048]{1,0:T(8,128)} async-done(((f32[512,2048]{1,0:T(8,128)}), f32[128,2048]{1,0:T(8,128)}) %reduce-scatter.2.cloned.1.call-update) | async-done | bytes 1048592 | tf_op jit(solution)/shard_map/reduce_scatter | solution.py:65
  149.1 28.3 %all-gather.8.cloned.1.call-done = bf16[512,2,512]{0,2,1:T(8,128)(2,1)} async-done(((bf16[128,2,512]{0,2,1:T(8,128)(2,1)}), bf16[512,2,512]{0,2,1:T(8,128)(2,1)}) %all-gather.8.cloned.1.call-update) | async-done | bytes 1048592 | tf_op jit(solution)/shard_map/all_gather | solution.py:86
  177.4 3.4 collective-permute-start
  180.8 24.9 %collective-permute-done = bf16[512,2,512]{0,2,1:T(8,128)(2,1)S(1)} collective-permute-done((bf16[512,2,512]{0,2,1:T(8,128)(2,1)}, bf16[512,2,512]{0,2,1:T(8,128)(2,1)S(1)}, u32[]{:S(2)}, u32[]{:S(2)}) %collective-permute-start) | collective-permute-done | bytes 1048608 | tf_op jit(solution)/shard_map/ppermute | solution.py:19
  205.7 1.9 collective-permute-start.1
  207.6 25.2 %collective-permute-done.1 = bf16[512,2,512]{0,2,1:T(8,128)(2,1)S(1)} collective-permute-done((bf16[512,2,512]{0,2,1:T(8,128)(2,1)S(1)}, bf16[512,2,512]{0,2,1:T(8,128)(2,1)S(1)}, u32[]{:S(2)}, u32[]{:S(2)}) %collective-permute-start.1) | collective-permute-done | bytes 1048608 | tf_op jit(solution)/shard_map/ppermute | solution.py:19
  233.1 1.9 collective-permute-start.2
  235.0 47.0 %collective-permute-done.2 = bf16[1024,2,512]{0,2,1:T(8,128)(2,1)S(1)} collective-permute-done((bf16[1024,2,512]{0,2,1:T(8,128)(2,1)S(1)}, bf16[1024,2,512]{0,2,1:T(8,128)(2,1)S(1)}, u32[]{:S(2)}, u32[]{:S(2)}) %collective-permute-start.2) | collective-permute-done | bytes 2097184 | tf_op jit(solution)/shard_map/ppermute | solution.py:19
  282.0 2.4 pad_maximum_fusion.2
  284.6 3.5 collective-permute-start.3
  290.5 1.9 convert_reduce_fusion.1
  292.3 83.2 %collective-permute-done.3 = bf16[2048,2,512]{0,2,1:T(8,128)(2,1)} collective-permute-done((bf16[2048,2,512]{0,2,1:T(8,128)(2,1)}, bf16[2048,2,512]{0,2,1:T(8,128)(2,1)}, u32[]{:S(2)}, u32[]{:S(2)}) %collective-permute-start.3) | collective-permute-done | bytes 4194336 | tf_op jit(solution)/shard_map/ppermute | solution.py:19
  375.5 6.1 %pad_maximum_fusion = bf16[4096,2,512]{0,2,1:T(8,128)(2,1)} fusion(bf16[512,2,512]{0,2,1:T(8,128)(2,1)S(1)} %collective-permute-done, bf16[512,2,512]{0,2,1:T(8,128)(2,1)S(1)} %collective-permute-done.1, bf16[1024,2,512]{0,2,1:T(8,128)(2,1)S(1)} %copy-done.3, bf16[2048,2,512]{0,2,1:T(8,128)(2,1)} %collective-permute-done.3), kind=kLoop, calls=%fused_computation.42 | loop fusion | flops 33554432 | bytes 16777216 | tf_op jit(solution)/shard_map/concatenate | solution.py:126
  381.6 12.0 %copy.29 = bf16[4096,2,512]{2,0,1:T(8,128)(2,1)} copy(bf16[4096,2,512]{0,2,1:T(8,128)(2,1)} %pad_maximum_fusion) | data formatting | bytes 16777216 | tf_op jit(solution)/shard_map/concatenate | solution.py:126
  393.6 68.6 %while.18 = (s32[]{:T(128)}, f32[128,4,2,128]{0,3,2,1:T(8,128)}, f32[128,4,2]{0,2,1:T(2,128)S(1)}, bf16[8,512,2,512]{3,1,0,2:T(8,128)(2,1)}, s32[8]{0:T(128)S(1)...) while((s32[]{:T(128)}, f32[128,4,2,128]{0,3,2,1:T(8,128)}, ...), condition=%wide.region_6.7_spmd.clone.clone.clone, body=%wide.region_3.6_spmd.clone.clone.clone.sunk | while | flops 272313600 | bytes 10916116 | solution.py:136
  405.9 1.9 convert_reduce_fusion.3
  407.8 2.2 fusion.71
  416.5 2.2 fusion.71
  423.3 1.9 convert_reduce_fusion.3
  425.2 2.2 fusion.71
  433.9 2.2 fusion.71
  442.6 2.2 fusion.71
  451.3 2.2 fusion.71
  460.0 2.2 fusion.71
  462.2 2.0 fusion.26
  (162 shorter events, 58.6 us)
Async XLA Ops:
  6.5 84.0 %copy-start = (bf16[1152,1024]{1,0:T(8,128)(2,1)S(1)}, bf16[1152,1024]{1,0:T(8,128)(2,1)}, u32[]{:S(2)}) copy-start(bf16[1152,1024]{1,0:T(8,128)(2,1)} %param.9) | copy-start | bytes 7077892
  6.5 19.5 %all-gather.4.cloned.1.call-start = ((), (), s32[]{:S(2)}) async-start(), calls=%async_computation.1 | async-start | bytes 1769472 | tf_op jit(solution)/shard_map/all_gather | solution.py:57
  7.3 79.7 %all-gather.6.cloned.1.call-start = ((), (), s32[]{:S(2)}) async-start(), calls=%async_computation.2 | async-start | bytes 5898240 | tf_op jit(solution)/shard_map/all_gather | solution.py:62
  30.3 115.5 %reduce-scatter.2.cloned.1.call-start = ((), (), s32[]{:S(2)}) async-start(), calls=%async_computation.3 | async-start | bytes 5242880 | tf_op jit(solution)/shard_map/reduce_scatter | solution.py:65
  95.8 81.7 %all-gather.8.cloned.1.call-start = ((), (), s32[]{:S(2)}) async-start(), calls=%async_computation.4 | async-start | bytes 1310720 | tf_op jit(solution)/shard_map/all_gather | solution.py:86
  177.4 28.2 %collective-permute-start = (bf16[512,2,512]{0,2,1:T(8,128)(2,1)}, bf16[512,2,512]{0,2,1:T(8,128)(2,1)S(1)}, u32[]{:S(2)}, u32[]{:S(2)}) collective-permute-start(bf16[512,2,512]{0,2,1:T(8,128)(2,1)} %all-gather.8.cloned.1.call-done), channel_id=1, source_target_pairs={{0,8},{8,16},{16,24},{24,32},{32,40},{40,48},{48,56},{56,64},{64,7... | collective-permute-start | bytes 3145736 | tf_op jit(solution)/shard_map/ppermute | solution.py:19
  205.7 27.1 %collective-permute-start.1 = (bf16[512,2,512]{0,2,1:T(8,128)(2,1)S(1)}, bf16[512,2,512]{0,2,1:T(8,128)(2,1)S(1)}, u32[]{:S(2)}, u32[]{:S(2)}) collective-permute-start(bf16[512,2,512]{0,2,1:T(8,128)(2,1)S(1)} %collective-permute-done), channel_id=1, source_target_pairs={{0,8},{8,16},{16,24},{24,32},{32,40},{40,48},{48,56},{56,64},{64,7... | collective-permute-start | bytes 3145736 | tf_op jit(solution)/shard_map/ppermute | solution.py:19
  233.0 55.4 %copy-start.6 = (s32[32]{0:T(128)S(1)}, s32[32]{0:T(128)}, u32[]{:S(2)}) copy-start(s32[32]{0:T(128)} %param.11) | copy-start | bytes 388
  233.1 49.0 %collective-permute-start.2 = (bf16[1024,2,512]{0,2,1:T(8,128)(2,1)S(1)}, bf16[1024,2,512]{0,2,1:T(8,128)(2,1)S(1)}, u32[]{:S(2)}, u32[]{:S(2)}) collective-permute-start(bf16[1024,2,512]{0,2,1:T(8,128)(2,1)S(1)} %pad_maximum_fusion.3), channel_id=1, source_target_pairs={{0,16},{8,24},{16,32},{24,40},{32,48},{40,56},{48,64},{56,72},{64,... | collective-permute-start | bytes 6291464 | tf_op jit(solution)/shard_map/ppermute | solution.py:19
  282.0 2.6 copy-start.2
  284.6 90.9 %collective-permute-start.3 = (bf16[2048,2,512]{0,2,1:T(8,128)(2,1)}, bf16[2048,2,512]{0,2,1:T(8,128)(2,1)}, u32[]{:S(2)}, u32[]{:S(2)}) collective-permute-start(bf16[2048,2,512]{0,2,1:T(8,128)(2,1)} %pad_maximum_fusion.2), channel_id=1, source_target_pairs={{0,32},{8,40},{16,48},{24,56},{32,64},{40,72},{48,80},{56,88},{64,... | collective-permute-start | bytes 12582920 | tf_op jit(solution)/shard_map/ppermute | solution.py:19
  288.3 1.2 copy-start.4
  289.5 2.8 copy-start.5
  290.5 85.1 %copy-start.3 = (bf16[1024,2,512]{0,2,1:T(8,128)(2,1)S(1)}, bf16[1024,2,512]{0,2,1:T(8,128)(2,1)}, u32[]{:S(2)}) copy-start(bf16[1024,2,512]{0,2,1:T(8,128)(2,1)} %copy-done.2) | copy-start | bytes 6291460
  462.2 2.9 copy-start.1
Sparse Core Ops, SparseCore 0:
  9.2 16.7 all-gather.3
  30.4 56.4 all-gather.5
  95.9 49.7 reduce-scatter.1
  149.2 28.1 all-gather.7
where the time goes:
time: 478 us; the launch traced here: 472 us
  waiting for transfers between devices  331 us (69%)
  matrix products  41.5 us (9%)
  local copies, waits for them, and re-layouts  40.5 us (8%)
  other arithmetic  34.3 us (7%)
  between operations  13.4 us (3%)
  starting transfers between devices  10.8 us (2%)
    ppermute x4, waiting for transfers between devices, shifted(): lax.ppermute(value, axis, [(source, source + steps) for source in range(l...  180 us
    all_gather x1, waiting for transfers between devices, on_device(): shard_normed = lax.all_gather(normed, 'row', axis=0, tiled=True)  52.9 us
    reduce_scatter x1, waiting for transfers between devices, on_device(): lax.psum_scatter(jnp.concatenate([jnp.dot(own_slab, w_query, preferred_el...  49.7 us
    all_gather x1, waiting for transfers between devices, on_device(): shard_kv = lax.all_gather(keyval, 'row', axis=0, tiled=True)  28.3 us
    dynamic_slice x24, local copies, waits for them, and re-layouts, on_device(): result, unused = lax.scan(step_block, initial_sums, (stacked, starts))  19.4 us
    all_gather x1, waiting for transfers between devices, on_device(): whole = lax.all_gather(tokens, 'col', axis=1, tiled=True)  18.7 us
    dot_general x9, matrix products, attend(): jnp.einsum('rgjk,kgd->rgjd', weights, value_heads, preferred_element_type...  18.4 us
    dot_general x9, matrix products, attend(): jnp.einsum('rgjd,kgd->rgjk', query_groups, key_heads, preferred_element_t...  16.7 us
  transfers between devices with their start and end apart: 8, of which 8 were waited for; matrix products, arithmetic and copies ran while one was open for 2% of the time, Pallas kernels for 0%

commit v1 on v0

v1 whole, which is shorter than its diff:
```python
import functools
import math

import jax
import jax.numpy as jnp
from jax import lax
from jax.experimental import pallas as pl
from jax.experimental.pallas import tpu as pltpu
from jax.sharding import Mesh, PartitionSpec as P

SCALE = 1.0 / 12.0
SOFTCAP = 50.0
EPSILON = 1e-06

HEAD = 128
SHARD = 512
SEQ_SHARDS = 16
PLANE = 4
ROWS = 4
BLOCK = SHARD // ROWS
HALF = BLOCK // 2
MODEL = 4608
SLAB = MODEL // ROWS
CHUNK = 256
DEN_ROWS = 16
PIECE = BLOCK + DEN_ROWS
SEQ = ("z", "xh", "xl")

TO_TANH = SCALE / SOFTCAP
TO_EXP2 = SOFTCAP * math.log2(math.e)

bf16 = jnp.bfloat16
f32 = jnp.float32
VMEM = pl.BlockSpec(memory_space=pltpu.VMEM)
SMEM = pl.BlockSpec(memory_space=pltpu.SMEM)


def local(body, operands, out_shapes, name, scratch=(), flops=0, limit=40 * 2**20):
    return pl.pallas_call(
        body,
        out_shape=out_shapes,
        in_specs=[SMEM] + [VMEM] * (len(operands) - 1),
        out_specs=jax.tree.map(lambda _: VMEM, out_shapes),
        scratch_shapes=list(scratch),
        compiler_params=pltpu.CompilerParams(vmem_limit_bytes=limit),
        cost_estimate=pl.CostEstimate(flops=flops, bytes_accessed=2**20, transcendentals=0),
        name=name,
    )(*operands)


def scalars(ids):
    return ids[0], ids[1], ids[2]


def live_of(ids, shard):
    return ids[3 + shard]


def norm_body(ids, tokens, received, gain, out):
    _, _, core = scalars(ids)
    kept = tokens[pl.ds(pl.multiple_of(core * HALF, HALF), HALF), :].astype(f32)
    other = received[...].astype(f32)
    total = jnp.sum(kept * kept, -1, keepdims=True) + jnp.sum(other * other, -1, keepdims=True)
    inverse = lax.rsqrt(total * (1.0 / MODEL) + EPSILON)
    for part in range(2):
        span = slice(part * SLAB, (part + 1) * SLAB)
        mine, theirs = 2 * core + part, 2 * (1 - core) + part
        out[mine] = (kept[:, span] * inverse * gain[mine]).astype(bf16)
        out[theirs] = (other[:, span] * inverse * gain[theirs]).astype(bf16)


def keyval_partial_body(ids, mine, theirs, weights, out, joined):
    _, _, core = scalars(ids)
    for block in range(ROWS):
        joined[block, core] = mine[block]
        joined[block, 1 - core] = theirs[block]
    slab = joined[...].reshape(SHARD, SLAB)
    for target in range(ROWS):
        for part in range(2):
            start = part * ROWS * HEAD + target * HEAD
            out[target, :, part * HEAD : (part + 1) * HEAD] = jnp.dot(
                slab, weights[:, start : start + HEAD], preferred_element_type=f32
            ).astype(bf16)


def query_partial_body(ids, joined, weights, out):
    slab = joined[...].reshape(SHARD, SLAB)
    for target in range(ROWS):
        out[target] = jnp.dot(
            slab,
            weights[:, target * 2 * HEAD : (target + 1) * 2 * HEAD],
            preferred_element_type=f32,
        ).astype(bf16)


def rotate_body(rotated, ids, parts, cosine, sine, out):
    for block in range(ROWS):
        rows = slice(block * BLOCK, (block + 1) * BLOCK)
        total = parts[0, rows].astype(f32)
        for source in range(1, ROWS):
            total = total + parts[source, rows].astype(f32)
        for half in range(2):
            span = slice(half * HEAD, (half + 1) * HEAD)
            value = total[:, span]
            if half < rotated:
                value = value * cosine[rows] + pltpu.roll(value, HEAD // 2, 1) * sine[rows]
            out[rows, span] = value.astype(bf16)


def key_shards(shard):
    plane, place = shard >> 2, shard & 3
    mirror = PLANE - 1 - place
    chosen = jnp.where(place < 2, plane - 2, plane)
    return (
        shard,
        shard - PLANE,
        (plane - 1) * PLANE + mirror,
        shard - 2 * PLANE,
        chosen * PLANE + mirror,
    )


def mask_values(ids, key_shard, keyval, masked):
    shard = ids[0]
    first = (shard >> 4) << 4
    count = jnp.where(key_shard >= first, live_of(ids, jnp.maximum(key_shard, 0)), 0)
    for start in range(0, SHARD, CHUNK):

        @pl.when(start < count)
        def _():
            alive = (
                lax.broadcasted_iota(jnp.int32, (CHUNK, HEAD), 0) + start < count
            )
            rows = slice(start, start + CHUNK)
            values = keyval[rows, HEAD:].astype(f32)
            masked[rows, :HEAD] = jnp.where(alive, values, 0.0).astype(bf16)
            masked[rows, HEAD:] = jnp.where(alive, 1.0, 0.0).astype(bf16)

    return count


def accumulate(query, query_shard, query_count, blocks, sums, fresh):
    for start in range(0, SHARD, CHUNK):
        tokens = slice(start, start + CHUNK)
        place = start // CHUNK

        @pl.when(start < query_count)
        def _(tokens=tokens, place=place):
            if fresh:
                for head in range(2):
                    sums[head, tokens] = jnp.zeros((CHUNK, 2 * HEAD), f32)
            for key_shard, count, keyval, masked in blocks:
                back = query_shard - key_shard
                chunks = (count + (CHUNK - 1)) // CHUNK
                low = jnp.where(back == 2 * PLANE, place, 0)
                high = jnp.where(back == 0, jnp.minimum(chunks, place + 1), chunks)
                high = jnp.where((back >= 0) & (back <= 2 * PLANE), high, 0)
                edge = (back == 0) | (back == 2 * PLANE)

                def step(chunk, carry, keyval=keyval, masked=masked, back=back, edge=edge):
                    rows = pl.ds(pl.multiple_of(chunk * CHUNK, CHUNK), CHUNK)

                    def work(with_mask):
                        keys = keyval[rows, :HEAD]
                        values = masked[rows, :]
                        if with_mask:
                            key_at = lax.broadcasted_iota(jnp.int32, (CHUNK, CHUNK), 1)
                            query_at = lax.broadcasted_iota(jnp.int32, (CHUNK, CHUNK), 0)
                            ahead = jnp.where(key_at <= query_at, 1, 0)
                            seen = ahead == jnp.where(back == 0, 1, 0)
                        for head in range(2):
                            scores = lax.dot_general(
                                query[tokens, head * HEAD : (head + 1) * HEAD],
                                keys,
                                (((1,), (1,)), ((), ())),
                                preferred_element_type=f32,
                            )
                            weights = jnp.exp2(jnp.tanh(scores * TO_TANH) * TO_EXP2)
                            if with_mask:
                                weights = jnp.where(seen, weights, 0.0)
                            sums[head, tokens] += jnp.dot(
                                weights.astype(bf16), values, preferred_element_type=f32
                            )

                    masked_step = edge & (chunk == place)

                    @pl.when(masked_step)
                    def _():
                        work(True)

                    @pl.when(jnp.logical_not(masked_step))
                    def _():
                        work(False)

                    return carry

                lax.fori_loop(low, high, step, 0)


def early_body(ids, query, own, back1, mirror1, back2, sums, *masked):
    shard, _, _ = scalars(ids)
    shards = key_shards(shard)
    held = (own, back1, mirror1, back2)
    blocks = [
        (shards[i], mask_values(ids, shards[i], held[i], masked[i]), held[i], masked[i])
        for i in range(len(held))
    ]
    accumulate(query, shard, live_of(ids, shard), blocks, sums, True)


def late_body(ids, query, pair, own, back1, mirror1, back2, chosen, before, out, sums, pair_sums, *masked):
    shard, _, _ = scalars(ids)
    side = shard & 1
    partner = shard + 1 - 2 * side
    shards = key_shards(shard)
    held = (own, back1, mirror1, back2, chosen)
    blocks = [
        (shards[i], mask_values(ids, shards[i], held[i], masked[i]), held[i], masked[i])
        for i in range(len(held))
    ]
    count, pair_count = live_of(ids, shard), live_of(ids, partner)
    for start in range(0, SHARD, CHUNK):

        @pl.when(start < count)
        def _(start=start):
            for head in range(2):
                sums[head, start : start + CHUNK] = before[head, start : start + CHUNK]

    accumulate(query, shard, count, blocks[4:], sums, False)
    accumulate(pair, partner, pair_count, blocks, pair_sums, True)
    for held_sums, live, owner in ((sums, count, side), (pair_sums, pair_count, 1 - side)):
        for block in range(ROWS):
            start = block * BLOCK

            @pl.when(start < live)
            def _(held_sums=held_sums, owner=owner, block=block, start=start):
                target = owner * ROWS + block
                for head in range(2):
                    span = slice(head * HEAD, (head + 1) * HEAD)
                    out[target, :BLOCK, span] = held_sums[head, start : start + BLOCK, :HEAD].astype(bf16)
                    turned = held_sums[head, start : start + BLOCK, HEAD:].T[:8]
                    coarse = turned.astype(bf16).astype(f32)
                    out[target, BLOCK:, span] = jnp.concatenate([coarse, turned - coarse], 0).astype(bf16)


def finish_body(ids, pieces, out):
    shard, row, _ = scalars(ids)
    alive = lax.broadcasted_iota(jnp.int32, (BLOCK, HEAD), 0) + row * BLOCK < live_of(ids, shard)
    for group in range(ROWS):
        for head in range(2):
            span = slice(head * HEAD, (head + 1) * HEAD)
            numer = pieces[group, :BLOCK, span].astype(f32) + pieces[ROWS + group, :BLOCK, span].astype(f32)
            both = pieces[group, BLOCK:, span].astype(f32) + pieces[ROWS + group, BLOCK:, span].astype(f32)
            flat = both[0:1] + both[8:9]
            denom = jnp.broadcast_to(flat, (BLOCK, HEAD)).T
            result = jnp.where(alive, numer / jnp.where(alive, denom, 1.0), 0.0)
            start = group * 2 * HEAD + head * HEAD
            out[:, start : start + HEAD] = result.astype(bf16)


def along_seq(value, target):
    pairs = []
    for shard in range(32):
        to = target(shard // PLANE, shard % PLANE)
        if to is not None:
            pairs.append((shard, to[0] * PLANE + to[1]))
    return lax.ppermute(value, SEQ, pairs)


def hop(value):
    planes = SEQ_SHARDS // PLANE
    return along_seq(value, lambda z, x: (z + 1, x) if z % planes != planes - 1 else None)


def mirrored(value):
    return along_seq(value, lambda z, x: (z, PLANE - 1 - x))


def paired(value):
    return along_seq(value, lambda z, x: (z, x ^ 1))


def swapped(value):
    return lax.ppermute(value, "col", [(0, 1), (1, 0)])


def on_device(tokens, norm_gain, w_query, w_keyval, active):
    core = lax.axis_index("col")
    row = lax.axis_index("row")
    shard = lax.axis_index(SEQ)
    ids = jnp.concatenate([jnp.stack([shard, row, core]).astype(jnp.int32), active])
    sds = jax.ShapeDtypeStruct

    outgoing = lax.dynamic_slice_in_dim(tokens, (1 - core) * HALF, HALF, 0)
    received = swapped(outgoing)
    gain = norm_gain.reshape(ROWS, 1, SLAB)
    normed = local(
        norm_body, (ids, tokens, received, gain), sds((ROWS, HALF, SLAB), bf16), "norm"
    )
    mine = lax.all_to_all(normed, "row", 0, 0)
    theirs = swapped(mine)

    half = HEAD // 2
    positions = (shard % SEQ_SHARDS) * SHARD + jnp.arange(SHARD, dtype=jnp.int32)
    freqs = 10000.0 ** (-2.0 * jnp.arange(half, dtype=f32) / HEAD)
    angles = positions.astype(f32)[:, None] * freqs[None, :]
    cosine, sine = jnp.cos(angles), jnp.sin(angles)
    cosine = jnp.concatenate([cosine, cosine], 1)
    sine = jnp.concatenate([-sine, sine], 1)

    flat = w_keyval.reshape(SLAB, 2 * ROWS * HEAD)
    part = sds((ROWS, SHARD, 2 * HEAD), bf16)
    joined_shape = sds((ROWS, 2, HALF, SLAB), bf16)
    flops = 2 * SHARD * SLAB * 8 * HEAD
    keyval_part, joined = local(
        keyval_partial_body, (ids, mine, theirs, flat), (part, joined_shape), "keyval_partial", flops=flops
    )
    keyval_parts = lax.all_to_all(keyval_part, "row", 0, 0)
    query_part = local(query_partial_body, (ids, joined, w_query), part, "query_partial", flops=flops)
    held = sds((SHARD, 2 * HEAD), bf16)
    own = local(
        functools.partial(rotate_body, 1), (ids, keyval_parts, cosine, sine), held, "keyval_rotate"
    )
    query_parts = lax.all_to_all(query_part, "row", 0, 0)

    back1 = hop(own)
    back2 = hop(back1)
    mirror1 = mirrored(back1)
    chosen = mirrored(jnp.where(lax.axis_index("xh") == 0, own, back2))

    query = local(
        functools.partial(rotate_body, 2), (ids, query_parts, cosine, sine), held, "query_rotate"
    )
    pair = paired(query)

    sums_shape = (2, SHARD, 2 * HEAD)
    masked = pltpu.VMEM((SHARD, 2 * HEAD), bf16)
    before = local(
        early_body,
        (ids, query, own, back1, mirror1, back2),
        sds(sums_shape, f32),
        "attend_early",
        scratch=[masked] * 4,
        flops=2**31,
    )
    pieces = local(
        late_body,
        (ids, query, pair, own, back1, mirror1, back2, chosen, before),
        sds((2 * ROWS, PIECE, 2 * HEAD), bf16),
        "attend_late",
        scratch=[pltpu.VMEM(sums_shape, f32), pltpu.VMEM(sums_shape, f32)] + [masked] * 5,
        flops=2**31,
    )
    returned = lax.all_to_all(pieces, ("xl", "row"), 0, 0)
    return local(finish_body, (ids, returned), sds((BLOCK, ROWS * 2 * HEAD), bf16), "finish")


def solution(mesh):
    fine = Mesh(mesh.devices.reshape(8, 2, 2, ROWS, 2), SEQ + ("row", "col"))
    tokens_spec = P(SEQ + ("row",), "col")
    placed = (tokens_spec, P(), P("row", "col"), P("row", None, "col"), P())
    return jax.shard_map(
        on_device, mesh=fine, in_specs=placed, out_specs=tokens_spec, check_vma=False
    )
```

time: 478 us -> 100 us (0.21); the launches traced: 472 us -> 101 us
  waiting for transfers between devices: 331 us -> 23.4 us
  matrix products: 41.5 us -> 0 us
  local copies, waits for them, and re-layouts: 40.5 us -> 6.68 us
  other arithmetic: 34.3 us -> 1.98 us
  blocking collectives: 0 us -> 28.2 us
  Pallas kernels: 0 us -> 18.9 us
  between operations: 13.4 us -> 0.21 us
  starting transfers between devices: 10.8 us -> 21.3 us
    ppermute x4 -> x7, waiting for transfers between devices: 180 us -> 12.1 us  [the longest x5 10.7 us: along_seq(): return lax.ppermute(value, SEQ, pairs)]
    all_gather x3 -> x0, waiting for transfers between devices: 99.9 us -> none  [the longest x1 52.9 us: on_device(): shard_normed = lax.all_gather(normed, 'row', axis=0, tiled=True)]
    reduce_scatter x1 -> x0, waiting for transfers between devices: 49.7 us -> none  [on_device(): lax.psum_scatter(jnp.concatenate([jnp.dot(own_slab, w_query, preferred_el...]
    dot_general x20 -> x0, matrix products: 41.5 us -> none  [the longest x9 18.4 us: attend(): jnp.einsum('rgjk,kgd->rgjd', weights, value_heads, preferred_element_type...]
    all_to_all x0 -> x2, blocking collectives: none -> 28.2 us  [the longest x1 15.1 us: on_device(): mine = lax.all_to_all(normed, 'row', 0, 0)]
    pallas_call x0 -> x8, Pallas kernels: none -> 18.9 us  [local(): pl.pallas_call(body, out_shape=out_shapes, in_specs=[SMEM] + [VMEM] * (le...]
    dynamic_slice x24 -> x1, local copies, waits for them, and re-layouts: 19.4 us -> 0.98 us  [on_device(): outgoing = lax.dynamic_slice_in_dim(tokens, (1 - core) * HALF, HALF, 0)]
    concatenate x1 -> x0, local copies, waits for them, and re-layouts: 12 us -> none  [on_device(): jnp.concatenate([moved, carried], 0)]
  transfers between devices with their start and end apart: 8 -> 9, of which waited for: 8 -> 6; matrix products, arithmetic and copies ran while one was open for 2% -> 3% of each run, Pallas kernels for 0% -> 9%
where the time goes in v1:
time: 100 us; the launch traced here: 101 us
  blocking collectives  28.2 us (28%)
  waiting for transfers between devices  23.4 us (23%)
  starting transfers between devices  21.3 us (21%)
  Pallas kernels  18.9 us (19%)
  local copies, waits for them, and re-layouts  6.68 us (7%)
  other arithmetic  1.98 us (2%)
    pallas_call x8, Pallas kernels, local(): pl.pallas_call(body, out_shape=out_shapes, in_specs=[SMEM] + [VMEM] * (le...  18.9 us
    all_to_all x1, blocking collectives, on_device(): mine = lax.all_to_all(normed, 'row', 0, 0)  15.1 us
    ppermute x5, starting transfers between devices, along_seq(): return lax.ppermute(value, SEQ, pairs)  14.2 us
    all_to_all x1, blocking collectives, on_device(): returned = lax.all_to_all(pieces, ('xl', 'row'), 0, 0)  13.2 us
    all_to_all x1, waiting for transfers between devices, on_device(): keyval_parts = lax.all_to_all(keyval_part, 'row', 0, 0)  11.3 us
    ppermute x5, waiting for transfers between devices, along_seq(): return lax.ppermute(value, SEQ, pairs)  10.7 us
    unnamed x13, local copies, waits for them, and re-layouts  4.95 us
    all_to_all x1, starting transfers between devices, on_device(): query_parts = lax.all_to_all(query_part, 'row', 0, 0)  3.52 us
  transfers between devices with their start and end apart: 9, of which 6 were waited for; matrix products, arithmetic and copies ran while one was open for 3% of the time, Pallas kernels for 9%

profile of v1, /device:TPU:64, one launch (start us, length us, event | category | flops | bytes accessed | tf_op | source)
XLA Modules:
  0.0 100.7 jit_solution(3378386560925820907)
XLA Ops:
  0.0 1.0 constant_dynamic-slice_fusion
  1.1 0.7 reshape.16.gain
  1.9 0.7 pad_add_fusion.ids
  2.7 1.1 %copy-done.1 = bf16[128,2304]{1,0:T(8,128)(2,1)S(1)} copy-done((bf16[128,2304]{1,0:T(8,128)(2,1)S(1)}, bf16[128,2304]{1,0:T(8,128)(2,1)}, u32[]{:S(2)}) %copy-start.1) | copy-done | bytes 589848
  3.7 0.8 norm.1
  4.6 15.1 %all_to_all.20.mine = bf16[4,64,1152]{2,1,0:T(8,128)(2,1)S(1)} all-to-all(bf16[4,64,1152]{2,1,0:T(8,128)(2,1)S(1)} %norm.1), channel_id=1, replica_groups=mesh['z'=8,'xh'=2,'xl'=2,'row'=4,'col'=2] {'row'}, dimensions={0} | all-to-all | bytes 1179648 | tf_op jit(solution)/shard_map/all_to_all | solution.py:300
  19.6 0.6 copy.6
  20.2 1.4 %collective-permute-done.1.theirs = bf16[4,64,1152]{2,1,0:T(8,128)(2,1)S(1)} collective-permute-done((bf16[4,64,1152]{2,1,0:T(8,128)(2,1)S(1)}, bf16[4,64,1152]{2,1,0:T(8,128)(2,1)S(1)}, u32[]{:S(2)}, u32[]{:S(2)}) %collective-permute-start.1) | collective-permute-done | bytes 589856 | tf_op jit(solution)/shard_map/ppermute | solution.py:284
  21.6 3.2 %keyval_partial.1 = (bf16[4,512,256]{2,1,0:T(8,128)(2,1)S(1)}, bf16[4,2,64,1152]{3,2,1,0:T(8,128)(2,1)S(1)}) custom-call(s32[35]{0:T(128)S(1)} %pad_add_fusion.ids, bf16[4,64,1152]{2,1,0:T(8,128)(2,1)S(1)} %all_to_all.20.mine, bf16[4,64,1152]{2,1,0:T(8,128)(2,1)S(1)} %collective-permute-done.1.theirs, bf16[1152,1024]{1,0:T(8,128)(2,1)S(1)} %bitcast.5), custom_call_target="tpu_custom_call" | custom-call | flops 1207959552 | bytes 1048576 | tf_op jit(solution)/shard_map/keyval_partial/pallas_call | solution.py:39
  24.9 1.0 %copy-done.2 = bf16[4,2,64,1152]{3,2,1,0:T(8,128)(2,1)} copy-done((bf16[4,2,64,1152]{3,2,1,0:T(8,128)(2,1)}, bf16[4,2,64,1152]{3,2,1,0:T(8,128)(2,1)S(1)}, u32[]{:S(2)}) %copy-start.2) | copy-done | bytes 1179672
  25.9 0.9 copy-done.4
  26.9 3.5 %all-to-all-start.2 = ((bf16[4,512,256]{2,1,0:T(8,128)(2,1)}), bf16[4,512,256]{2,1,0:T(8,128)(2,1)S(1)}, u32[]{:S(2)}, u32[]{:S(2)}) async-start(bf16[4,512,256]{2,1,0:T(8,128)(2,1)} %copy-done.4), calls=%async_computation.2 | async-start | bytes 2097152 | tf_op jit(solution)/shard_map/all_to_all | solution.py:318
  30.4 1.3 %copy-done.3 = bf16[4,2,64,1152]{3,2,1,0:T(8,128)(2,1)S(1)} copy-done((bf16[4,2,64,1152]{3,2,1,0:T(8,128)(2,1)S(1)}, bf16[4,2,64,1152]{3,2,1,0:T(8,128)(2,1)}, u32[]{:S(2)}) %copy-start.3) | copy-done | bytes 1179672
  31.7 3.0 %query_partial.1 = bf16[4,512,256]{2,1,0:T(8,128)(2,1)} custom-call(s32[35]{0:T(128)S(1)} %pad_add_fusion.ids, bf16[4,2,64,1152]{3,2,1,0:T(8,128)(2,1)S(1)} %copy-done.3, bf16[1152,1024]{1,0:T(8,128)(2,1)S(1)} %copy-done), custom_call_target="tpu_custom_call" | custom-call | flops 1207959552 | bytes 1048576 | tf_op jit(solution)/shard_map/query_partial/pallas_call | solution.py:39
  34.7 11.3 %all-to-all-done.2.parts = bf16[4,512,256]{2,1,0:T(8,128)(2,1)S(1)} async-done(((bf16[4,512,256]{2,1,0:T(8,128)(2,1)}), bf16[4,512,256]{2,1,0:T(8,128)(2,1)S(1)}, u32[]{:S(2)}, u32[]{:S(2)}) %all-to-all-start.2) | async-done | bytes 1048608 | tf_op jit(solution)/shard_map/all_to_all | solution.py:318
  46.0 3.5 %all-to-all-start.1 = ((bf16[4,512,256]{2,1,0:T(8,128)(2,1)}), bf16[4,512,256]{2,1,0:T(8,128)(2,1)S(1)}, u32[]{:S(2)}, u32[]{:S(2)}) async-start(bf16[4,512,256]{2,1,0:T(8,128)(2,1)} %query_partial.1), calls=%async_computation.1 | async-start | bytes 2097152 | tf_op jit(solution)/shard_map/all_to_all | solution.py:324
  49.5 1.0 fusion
  50.5 0.2 pad_maximum_fusion
  50.8 0.7 keyval_rotate.1.own
  51.5 3.8 %collective-permute-start.3 = (bf16[512,256]{1,0:T(8,128)(2,1)S(1)}, bf16[512,256]{1,0:T(8,128)(2,1)S(1)}, u32[]{:S(2)}, u32[]{:S(2)}) collective-permute-start(bf16[512,256]{1,0:T(8,128)(2,1)S(1)} %keyval_rotate.1.own), channel_id=1, source_target_pairs={{0,32},{8,40},{16,48},{24,56},{32,64},{40,72},{48,80},{56,88},{64,... | collective-permute-start | bytes 786440 | tf_op jit(solution)/shard_map/ppermute | solution.py:267
  55.3 5.6 %collective-permute-done.3.back1 = bf16[512,256]{1,0:T(8,128)(2,1)S(1)} collective-permute-done((bf16[512,256]{1,0:T(8,128)(2,1)S(1)}, bf16[512,256]{1,0:T(8,128)(2,1)S(1)}, u32[]{:S(2)}, u32[]{:S(2)}) %collective-permute-start.3) | collective-permute-done | bytes 262176 | tf_op jit(solution)/shard_map/ppermute | solution.py:267
  60.9 3.8 %collective-permute-start.5 = (bf16[512,256]{1,0:T(8,128)(2,1)S(1)}, bf16[512,256]{1,0:T(8,128)(2,1)S(1)}, u32[]{:S(2)}, u32[]{:S(2)}) collective-permute-start(bf16[512,256]{1,0:T(8,128)(2,1)S(1)} %collective-permute-done.3.back1), channel_id=1, source_target_pairs={{0,32},{8,40},{16,48},{24,56},{32,64},{40,72},{48,80},{56,88},{64,... | collective-permute-start | bytes 786440 | tf_op jit(solution)/shard_map/ppermute | solution.py:267
  64.7 0.8 query_rotate.1.query
  65.5 1.6 %collective-permute-start.2 = (bf16[512,256]{1,0:T(8,128)(2,1)S(1)}, bf16[512,256]{1,0:T(8,128)(2,1)S(1)}, u32[]{:S(2)}, u32[]{:S(2)}) collective-permute-start(bf16[512,256]{1,0:T(8,128)(2,1)S(1)} %query_rotate.1.query), channel_id=1, source_target_pairs={{0,8},{8,0},{16,24},{24,16},{32,40},{40,32},{48,56},{56,48},{64,72... | collective-permute-start | bytes 786440 | tf_op jit(solution)/shard_map/ppermute | solution.py:267
  67.1 2.1 %collective-permute-start.4 = (bf16[512,256]{1,0:T(8,128)(2,1)S(1)}, bf16[512,256]{1,0:T(8,128)(2,1)S(1)}, u32[]{:S(2)}, u32[]{:S(2)}) collective-permute-start(bf16[512,256]{1,0:T(8,128)(2,1)S(1)} %collective-permute-done.3.back1), channel_id=1, source_target_pairs={{0,24},{8,16},{16,8},{24,0},{32,56},{40,48},{48,40},{56,32},{64,88... | collective-permute-start | bytes 786440 | tf_op jit(solution)/shard_map/ppermute | solution.py:267
  69.2 0.2 collective-permute-done.5.back2
  69.4 2.8 %collective-permute-start.6 = (bf16[512,256]{1,0:T(8,128)(2,1)S(1)}, bf16[512,256]{1,0:T(8,128)(2,1)S(1)}, u32[]{:S(2)}, u32[]{:S(2)}) collective-permute-start(bf16[512,256]{1,0:T(8,128)(2,1)S(1)} %broadcast_select_fusion), channel_id=1, source_target_pairs={{0,24},{8,16},{16,8},{24,0},{32,56},{40,48},{48,40},{56,32},{64,88... | collective-permute-start | bytes 786440 | tf_op jit(solution)/shard_map/ppermute | solution.py:267
  72.3 4.9 %collective-permute-done.4.mirror1 = bf16[512,256]{1,0:T(8,128)(2,1)S(1)} collective-permute-done((bf16[512,256]{1,0:T(8,128)(2,1)S(1)}, bf16[512,256]{1,0:T(8,128)(2,1)S(1)}, u32[]{:S(2)}, u32[]{:S(2)}) %collective-permute-start.4) | collective-permute-done | bytes 262176 | tf_op jit(solution)/shard_map/ppermute | solution.py:267
  77.2 4.5 %attend_early.1.before = f32[2,512,256]{2,1,0:T(8,128)S(1)} custom-call(s32[35]{0:T(128)S(1)} %pad_add_fusion.ids, bf16[512,256]{1,0:T(8,128)(2,1)S(1)} %query_rotate.1.query, bf16[512,256]{1,0:T(8,128)(2,1)S(1)} %keyval_rotate.1.own, bf16[512,256]{1,0:T(8,128)(2,1)S(1)} %collective-permute-done.3.back1, ...), custom_call_target="tpu_custom_call" | custom-call | flops 2147483648 | bytes 1048576 | tf_op jit(solution)/shard_map/attend_early/pallas_call | solution.py:39
  81.7 4.4 %attend_late.1 = bf16[8,144,256]{2,1,0:T(8,128)(2,1)S(1)} custom-call(s32[35]{0:T(128)S(1)} %pad_add_fusion.ids, bf16[512,256]{1,0:T(8,128)(2,1)S(1)} %query_rotate.1.query, bf16[512,256]{1,0:T(8,128)(2,1)S(1)} %collective-permute-done.2.pair, bf16[512,256]{1,0:T(8,128)(2,1)S(1)} %keyval_rotate.1.own, bf16[512,256]{1,0:T(8,128)(2,1)S(1)} %collective-permute-done.3.back1, ...), custom_call_target="tpu_custom_call" | custom-call | flops 2147483648 | bytes 1048576 | tf_op jit(solution)/shard_map/attend_late/pallas_call | solution.py:39
  86.1 13.2 %all_to_all.21.pieces = bf16[8,144,256]{2,1,0:T(8,128)(2,1)S(1)} all-to-all(bf16[8,144,256]{2,1,0:T(8,128)(2,1)S(1)} %attend_late.1), channel_id=1, replica_groups=mesh['z'=8,'xh'=2,'xl'=2,'row'=4,'col'=2] {'xl','row'}, dimensions={0} | all-to-all | bytes 1179648 | tf_op jit(solution)/shard_map/all_to_all | solution.py:354
  99.2 1.5 %finish.1 = bf16[128,1024]{1,0:T(8,128)(2,1)} custom-call(s32[35]{0:T(128)S(1)} %pad_add_fusion.ids, bf16[8,144,256]{2,1,0:T(8,128)(2,1)S(1)} %all_to_all.21.pieces), custom_call_target="tpu_custom_call" | custom-call | bytes 1048576 | tf_op jit(solution)/shard_map/finish/pallas_call | solution.py:39
  (17 shorter events, 0.2 us)
Async XLA Ops:
  1.0 1.7 %collective-permute-start = (bf16[64,2304]{1,0:T(8,128)(2,1)S(1)}, bf16[64,2304]{1,0:T(8,128)(2,1)S(1)}, u32[]{:S(2)}, u32[]{:S(2)}) collective-permute-start(bf16[64,2304]{1,0:T(8,128)(2,1)S(1)} %constant_dynamic-slice_fusion), channel_id=1, source_target_pairs={{0,1},{1,0},{2,3},{3,2},{4,5},{5,4},{6,7},{7,6},{8,9},{9,8},{10,11... | collective-permute-start | bytes 884744 | tf_op jit(solution)/shard_map/ppermute | solution.py:284
  2.7 1.1 %copy-start.1 = (bf16[128,2304]{1,0:T(8,128)(2,1)S(1)}, bf16[128,2304]{1,0:T(8,128)(2,1)}, u32[]{:S(2)}) copy-start(bf16[128,2304]{1,0:T(8,128)(2,1)} %tokens.1) | copy-start | bytes 1769476
  3.7 15.9 %copy-start.5 = (bf16[1152,2,512]{2,1,0:T(2,128)(2,1)S(1)}, bf16[1152,2,512]{2,1,0:T(2,128)(2,1)}, u32[]{:S(2)}) copy-start(bf16[1152,2,512]{2,1,0:T(2,128)(2,1)} %param.8) | copy-start | bytes 7077892
  19.6 2.0 %collective-permute-start.1 = (bf16[4,64,1152]{2,1,0:T(8,128)(2,1)S(1)}, bf16[4,64,1152]{2,1,0:T(8,128)(2,1)S(1)}, u32[]{:S(2)}, u32[]{:S(2)}) collective-permute-start(bf16[4,64,1152]{2,1,0:T(8,128)(2,1)S(1)} %all_to_all.20.mine), channel_id=1, source_target_pairs={{0,1},{1,0},{2,3},{3,2},{4,5},{5,4},{6,7},{7,6},{8,9},{9,8},{10,11... | collective-permute-start | bytes 1769480 | tf_op jit(solution)/shard_map/ppermute | solution.py:284
  21.6 8.8 %copy-start = (bf16[1152,1024]{1,0:T(8,128)(2,1)S(1)}, bf16[1152,1024]{1,0:T(8,128)(2,1)}, u32[]{:S(2)}) copy-start(bf16[1152,1024]{1,0:T(8,128)(2,1)} %weights.1) | copy-start | bytes 7077892
  24.9 1.1 %copy-start.2 = (bf16[4,2,64,1152]{3,2,1,0:T(8,128)(2,1)}, bf16[4,2,64,1152]{3,2,1,0:T(8,128)(2,1)S(1)}, u32[]{:S(2)}) copy-start(bf16[4,2,64,1152]{3,2,1,0:T(8,128)(2,1)S(1)} %get-tuple-element.7.joined) | copy-start | bytes 3538948
  25.9 0.9 copy-start.4
  26.9 19.2 %all-to-all-start.2 = ((bf16[4,512,256]{2,1,0:T(8,128)(2,1)}), bf16[4,512,256]{2,1,0:T(8,128)(2,1)S(1)}, u32[]{:S(2)}, u32[]{:S(2)}) async-start(bf16[4,512,256]{2,1,0:T(8,128)(2,1)} %copy-done.4), calls=%async_computation.2 | async-start | bytes 2097152 | tf_op jit(solution)/shard_map/all_to_all | solution.py:318
  30.4 1.3 %copy-start.3 = (bf16[4,2,64,1152]{3,2,1,0:T(8,128)(2,1)S(1)}, bf16[4,2,64,1152]{3,2,1,0:T(8,128)(2,1)}, u32[]{:S(2)}) copy-start(bf16[4,2,64,1152]{3,2,1,0:T(8,128)(2,1)} %copy-done.2) | copy-start | bytes 3538948
  46.0 18.7 %all-to-all-start.1 = ((bf16[4,512,256]{2,1,0:T(8,128)(2,1)}), bf16[4,512,256]{2,1,0:T(8,128)(2,1)S(1)}, u32[]{:S(2)}, u32[]{:S(2)}) async-start(bf16[4,512,256]{2,1,0:T(8,128)(2,1)} %query_partial.1), calls=%async_computation.1 | async-start | bytes 2097152 | tf_op jit(solution)/shard_map/all_to_all | solution.py:324
  51.5 9.4 %collective-permute-start.3 = (bf16[512,256]{1,0:T(8,128)(2,1)S(1)}, bf16[512,256]{1,0:T(8,128)(2,1)S(1)}, u32[]{:S(2)}, u32[]{:S(2)}) collective-permute-start(bf16[512,256]{1,0:T(8,128)(2,1)S(1)} %keyval_rotate.1.own), channel_id=1, source_target_pairs={{0,32},{8,40},{16,48},{24,56},{32,64},{40,72},{48,80},{56,88},{64,... | collective-permute-start | bytes 786440 | tf_op jit(solution)/shard_map/ppermute | solution.py:267
  60.9 8.5 %collective-permute-start.5 = (bf16[512,256]{1,0:T(8,128)(2,1)S(1)}, bf16[512,256]{1,0:T(8,128)(2,1)S(1)}, u32[]{:S(2)}, u32[]{:S(2)}) collective-permute-start(bf16[512,256]{1,0:T(8,128)(2,1)S(1)} %collective-permute-done.3.back1), channel_id=1, source_target_pairs={{0,32},{8,40},{16,48},{24,56},{32,64},{40,72},{48,80},{56,88},{64,... | collective-permute-start | bytes 786440 | tf_op jit(solution)/shard_map/ppermute | solution.py:267
  65.5 16.1 %collective-permute-start.2 = (bf16[512,256]{1,0:T(8,128)(2,1)S(1)}, bf16[512,256]{1,0:T(8,128)(2,1)S(1)}, u32[]{:S(2)}, u32[]{:S(2)}) collective-permute-start(bf16[512,256]{1,0:T(8,128)(2,1)S(1)} %query_rotate.1.query), channel_id=1, source_target_pairs={{0,8},{8,0},{16,24},{24,16},{32,40},{40,32},{48,56},{56,48},{64,72... | collective-permute-start | bytes 786440 | tf_op jit(solution)/shard_map/ppermute | solution.py:267
  67.1 10.1 %collective-permute-start.4 = (bf16[512,256]{1,0:T(8,128)(2,1)S(1)}, bf16[512,256]{1,0:T(8,128)(2,1)S(1)}, u32[]{:S(2)}, u32[]{:S(2)}) collective-permute-start(bf16[512,256]{1,0:T(8,128)(2,1)S(1)} %collective-permute-done.3.back1), channel_id=1, source_target_pairs={{0,24},{8,16},{16,8},{24,0},{32,56},{40,48},{48,40},{56,32},{64,88... | collective-permute-start | bytes 786440 | tf_op jit(solution)/shard_map/ppermute | solution.py:267
  69.4 12.2 %collective-permute-start.6 = (bf16[512,256]{1,0:T(8,128)(2,1)S(1)}, bf16[512,256]{1,0:T(8,128)(2,1)S(1)}, u32[]{:S(2)}, u32[]{:S(2)}) collective-permute-start(bf16[512,256]{1,0:T(8,128)(2,1)S(1)} %broadcast_select_fusion), channel_id=1, source_target_pairs={{0,24},{8,16},{16,8},{24,0},{32,56},{40,48},{48,40},{56,32},{64,88... | collective-permute-start | bytes 786440 | tf_op jit(solution)/shard_map/ppermute | solution.py:267

commit v2 on v1

--- a/solution.py
+++ b/solution.py
@@ -22,6 +22,8 @@
 MODEL = 4608
 SLAB = MODEL // ROWS
 CHUNK = 256
+TILE = 128
+LISTED = 4 * SHARD + 4 * TILE
 DEN_ROWS = 16
 PIECE = BLOCK + DEN_ROWS
 SEQ = ("z", "xh", "xl")
@@ -33,13 +35,14 @@
 f32 = jnp.float32
 VMEM = pl.BlockSpec(memory_space=pltpu.VMEM)
 SMEM = pl.BlockSpec(memory_space=pltpu.SMEM)
-
-
-def local(body, operands, out_shapes, name, scratch=(), flops=0, limit=40 * 2**20):
+FAR = pl.BlockSpec(memory_space=pltpu.HBM)
+
+
+def local(body, operands, out_shapes, name, scratch=(), flops=0, limit=8 * 2**20, apart=()):
     return pl.pallas_call(
         body,
         out_shape=out_shapes,
-        in_specs=[SMEM] + [VMEM] * (len(operands) - 1),
+        in_specs=[SMEM] + [FAR if i in apart else VMEM for i in range(1, len(operands))],
         out_specs=jax.tree.map(lambda _: VMEM, out_shapes),
         scratch_shapes=list(scratch),
         compiler_params=pltpu.CompilerParams(vmem_limit_bytes=limit),
@@ -56,49 +59,53 @@
     return ids[3 + shard]
 
 
-def norm_body(ids, tokens, received, gain, out):
+def norm_body(ids, tokens, received, gain, out, held, arrived):
     _, _, core = scalars(ids)
-    kept = tokens[pl.ds(pl.multiple_of(core * HALF, HALF), HALF), :].astype(f32)
-    other = received[...].astype(f32)
-    total = jnp.sum(kept * kept, -1, keepdims=True) + jnp.sum(other * other, -1, keepdims=True)
+    half = pl.ds(pl.multiple_of(core * HALF, HALF), HALF)
+    copy = pltpu.make_async_copy(tokens.at[half, :], held, arrived)
+    copy.start()
+    other = received[half, :].astype(f32)
+    total = jnp.sum(other * other, -1, keepdims=True)
+    copy.wait()
+    kept = held[...].astype(f32)
+    total = total + jnp.sum(kept * kept, -1, keepdims=True)
     inverse = lax.rsqrt(total * (1.0 / MODEL) + EPSILON)
     for part in range(2):
         span = slice(part * SLAB, (part + 1) * SLAB)
-        mine, theirs = 2 * core + part, 2 * (1 - core) + part
-        out[mine] = (kept[:, span] * inverse * gain[mine]).astype(bf16)
-        out[theirs] = (other[:, span] * inverse * gain[theirs]).astype(bf16)
-
-
-def keyval_partial_body(ids, mine, theirs, weights, out, joined):
-    _, _, core = scalars(ids)
-    for block in range(ROWS):
-        joined[block, core] = mine[block]
-        joined[block, 1 - core] = theirs[block]
-    slab = joined[...].reshape(SHARD, SLAB)
-    for target in range(ROWS):
-        for part in range(2):
-            start = part * ROWS * HEAD + target * HEAD
-            out[target, :, part * HEAD : (part + 1) * HEAD] = jnp.dot(
-                slab, weights[:, start : start + HEAD], preferred_element_type=f32
-            ).astype(bf16)
-
-
-def query_partial_body(ids, joined, weights, out):
-    slab = joined[...].reshape(SHARD, SLAB)
-    for target in range(ROWS):
-        out[target] = jnp.dot(
-            slab,
-            weights[:, target * 2 * HEAD : (target + 1) * 2 * HEAD],
-            preferred_element_type=f32,
-        ).astype(bf16)
-
-
-def rotate_body(rotated, ids, parts, cosine, sine, out):
+        for value, slab in ((kept, 2 * core + part), (other, 2 * (1 - core) + part)):
+            scale = gain[:, pl.ds(pl.multiple_of(slab * SLAB, HEAD), SLAB)]
+            out[slab] = (value[:, span] * inverse * scale).astype(bf16)
+
+
+def partial_body(steps, split, ids, mine, theirs, weights, *outs):
+    _, row, core = scalars(ids)
+    for step, out in zip(steps, outs):
+        target = (row + step) & (ROWS - 1)
+        if split:
+            columns = [
+                weights[:, pl.ds(pl.multiple_of((part * ROWS + target) * HEAD, HEAD), HEAD)]
+                for part in range(2)
+            ]
+            columns = jnp.concatenate(columns, 1)
+        else:
+            columns = weights[:, pl.ds(pl.multiple_of(target * 2 * HEAD, 2 * HEAD), 2 * HEAD)]
+        for slab, side in ((mine, core), (theirs, 1 - core)):
+            rows = slab[...].reshape(ROWS * HALF, SLAB)
+            sums = jnp.dot(rows, columns, preferred_element_type=f32).astype(bf16)
+            for block in range(ROWS):
+                value = sums[block * HALF : (block + 1) * HALF]
+                out[block, side] = value
+
+
+def rotate_body(rotated, ids, *refs):
+    parts, (cosine, sine, out) = refs[:-3], refs[-3:]
+    if len(parts) == 1:
+        parts = [parts[0].at[source] for source in range(ROWS)]
     for block in range(ROWS):
         rows = slice(block * BLOCK, (block + 1) * BLOCK)
-        total = parts[0, rows].astype(f32)
-        for source in range(1, ROWS):
-            total = total + parts[source, rows].astype(f32)
+        total = parts[0][rows].astype(f32)
+        for part in parts[1:]:
+            total = total + part[rows].astype(f32)
         for half in range(2):
             span = slice(half * HEAD, (half + 1) * HEAD)
             value = total[:, span]
@@ -208,52 +215,107 @@
     accumulate(query, shard, live_of(ids, shard), blocks, sums, True)
 
 
-def late_body(ids, query, pair, own, back1, mirror1, back2, chosen, before, out, sums, pair_sums, *masked):
+def late_body(
+    ids, query, pair, own, back1, mirror1, back2, chosen, before, out, sums, pair_sums, keys, values
+):
     shard, _, _ = scalars(ids)
     side = shard & 1
     partner = shard + 1 - 2 * side
-    shards = key_shards(shard)
-    held = (own, back1, mirror1, back2, chosen)
-    blocks = [
-        (shards[i], mask_values(ids, shards[i], held[i], masked[i]), held[i], masked[i])
-        for i in range(len(held))
-    ]
+    own_shard, back1_shard, mirror1_shard, back2_shard, chosen_shard = key_shards(shard)
+    first = (shard >> 4) << 4
+    used = 0
+    listed = (
+        (own, own_shard, side == 0),
+        (back2, back2_shard, side == 1),
+        (back1, back1_shard, True),
+        (mirror1, mirror1_shard, True),
+        (chosen, chosen_shard, True),
+    )
+    for keyval, key_shard, seen in listed:
+        before_this = used
+        counted = (key_shard >= first) & seen
+        count = jnp.where(counted, live_of(ids, jnp.maximum(key_shard, 0)), 0)
+        for start in range(0, SHARD, TILE):
+
+            @pl.when(start < count)
+            def _(keyval=keyval, start=start, used=used, count=count):
+                alive = lax.broadcasted_iota(jnp.int32, (TILE, HEAD), 0) + start < count
+                rows = pl.ds(pl.multiple_of(used * TILE + start, TILE), TILE)
+                keys[rows, :] = keyval[start : start + TILE, :HEAD]
+                value = keyval[start : start + TILE, HEAD:].astype(f32)
+                values[rows, :HEAD] = jnp.where(alive, value, 0.0).astype(bf16)
+                values[rows, HEAD:] = jnp.where(alive, 1.0, 0.0).astype(bf16)
+
+        used = used + ((count + (TILE - 1)) >> 7)
+    rows = pl.ds(pl.multiple_of(used * TILE, TILE), 3 * TILE)
+    keys[rows, :] = jnp.zeros((3 * TILE, HEAD), bf16)
+    values[rows, :] = jnp.zeros((3 * TILE, 2 * HEAD), bf16)
+
+    def attend(query, live, low, width, sums):
+        for start in range(0, SHARD, CHUNK):
+            tokens = slice(start, start + CHUNK)
+
+            @pl.when(start < live)
+            def _(tokens=tokens):
+                heads = [query[tokens, :HEAD], query[tokens, HEAD:]]
+                stacked = jnp.concatenate(heads, 0)
+                for head in range(2):
+                    sums[head, tokens] = jnp.zeros((CHUNK, 2 * HEAD), f32)
+
+                def step(index, carry):
+                    at = pl.ds(pl.multiple_of((low + index * width) * TILE, TILE), width * TILE)
+                    scores = lax.dot_general(
+                        stacked, keys[at, :], (((1,), (1,)), ((), ())), preferred_element_type=f32
+                    )
+                    weights = jnp.exp2(jnp.tanh(scores * TO_TANH) * TO_EXP2).astype(bf16)
+                    added = jnp.dot(weights, values[at, :], preferred_element_type=f32)
+                    for head in range(2):
+                        sums[head, tokens] += added[head * CHUNK : (head + 1) * CHUNK]
+                    return carry
+
+                lax.fori_loop(0, (used - low + (width - 1)) // width, step, 0)
+
     count, pair_count = live_of(ids, shard), live_of(ids, partner)
-    for start in range(0, SHARD, CHUNK):
-
-        @pl.when(start < count)
-        def _(start=start):
-            for head in range(2):
-                sums[head, start : start + CHUNK] = before[head, start : start + CHUNK]
-
-    accumulate(query, shard, count, blocks[4:], sums, False)
-    accumulate(pair, partner, pair_count, blocks, pair_sums, True)
-    for held_sums, live, owner in ((sums, count, side), (pair_sums, pair_count, 1 - side)):
+    attend(query, count, before_this, 2, sums)
+    attend(pair, pair_count, 0, 4, pair_sums)
+    same = lax.broadcasted_iota(jnp.int32, (BLOCK, HEAD), 0) == lax.broadcasted_iota(
+        jnp.int32, (BLOCK, HEAD), 1
+    )
+    for held, live, owner, earlier in (
+        (sums, count, side, before),
+        (pair_sums, pair_count, 1 - side, None),
+    ):
         for block in range(ROWS):
             start = block * BLOCK
 
             @pl.when(start < live)
-            def _(held_sums=held_sums, owner=owner, block=block, start=start):
+            def _(held=held, owner=owner, earlier=earlier, block=block, start=start):
                 target = owner * ROWS + block
                 for head in range(2):
                     span = slice(head * HEAD, (head + 1) * HEAD)
-                    out[target, :BLOCK, span] = held_sums[head, start : start + BLOCK, :HEAD].astype(bf16)
-                    turned = held_sums[head, start : start + BLOCK, HEAD:].T[:8]
-                    coarse = turned.astype(bf16).astype(f32)
-                    out[target, BLOCK:, span] = jnp.concatenate([coarse, turned - coarse], 0).astype(bf16)
+                    total = held[head, start : start + BLOCK]
+                    if earlier is not None:
+                        total = total + earlier[head, start : start + BLOCK]
+                    out[target, :BLOCK, span] = total[:, :HEAD].astype(bf16)
+                    line = jnp.sum(jnp.where(same, total[:, HEAD:], 0.0), 0, keepdims=True)
+                    line = jnp.broadcast_to(line, (8, HEAD))
+                    coarse = line.astype(bf16).astype(f32)
+                    out[target, BLOCK:, span] = jnp.concatenate([coarse, line - coarse], 0).astype(bf16)
 
 
 def finish_body(ids, pieces, out):
     shard, row, _ = scalars(ids)
-    alive = lax.broadcasted_iota(jnp.int32, (BLOCK, HEAD), 0) + row * BLOCK < live_of(ids, shard)
+    at = lax.broadcasted_iota(jnp.int32, (BLOCK, HEAD), 0)
+    same = at == lax.broadcasted_iota(jnp.int32, (BLOCK, HEAD), 1)
+    alive = at + row * BLOCK < live_of(ids, shard)
     for group in range(ROWS):
         for head in range(2):
             span = slice(head * HEAD, (head + 1) * HEAD)
             numer = pieces[group, :BLOCK, span].astype(f32) + pieces[ROWS + group, :BLOCK, span].astype(f32)
             both = pieces[group, BLOCK:, span].astype(f32) + pieces[ROWS + group, BLOCK:, span].astype(f32)
-            flat = both[0:1] + both[8:9]
-            denom = jnp.broadcast_to(flat, (BLOCK, HEAD)).T
-            result = jnp.where(alive, numer / jnp.where(alive, denom, 1.0), 0.0)
+            line = both[0:1] + both[8:9]
+            denom = jnp.sum(jnp.where(same, line, 0.0), 1, keepdims=True)
+            result = jnp.where(alive, numer * (1.0 / denom), 0.0)
             start = group * 2 * HEAD + head * HEAD
             out[:, start : start + HEAD] = result.astype(bf16)
 
@@ -280,6 +342,10 @@
     return along_seq(value, lambda z, x: (z, x ^ 1))
 
 
+def onward(value, step):
+    return lax.ppermute(value, "row", [(row, (row + step) % ROWS) for row in range(ROWS)])
+
+
 def swapped(value):
     return lax.ppermute(value, "col", [(0, 1), (1, 0)])
 
@@ -291,17 +357,22 @@
     ids = jnp.concatenate([jnp.stack([shard, row, core]).astype(jnp.int32), active])
     sds = jax.ShapeDtypeStruct
 
-    outgoing = lax.dynamic_slice_in_dim(tokens, (1 - core) * HALF, HALF, 0)
-    received = swapped(outgoing)
-    gain = norm_gain.reshape(ROWS, 1, SLAB)
+    received = swapped(tokens)
+    gain = norm_gain.reshape(1, MODEL)
     normed = local(
-        norm_body, (ids, tokens, received, gain), sds((ROWS, HALF, SLAB), bf16), "norm"
+        norm_body,
+        (ids, tokens, received, gain),
+        sds((ROWS, HALF, SLAB), bf16),
+        "norm",
+        scratch=[pltpu.VMEM((HALF, ROWS * SLAB // 2), bf16), pltpu.SemaphoreType.DMA],
+        apart=(1,),
     )
     mine = lax.all_to_all(normed, "row", 0, 0)
+    mine, place = lax.optimization_barrier((mine, shard))
     theirs = swapped(mine)
 
     half = HEAD // 2
-    positions = (shard % SEQ_SHARDS) * SHARD + jnp.arange(SHARD, dtype=jnp.int32)
+    positions = (place % SEQ_SHARDS) * SHARD + jnp.arange(SHARD, dtype=jnp.int32)
     freqs = 10000.0 ** (-2.0 * jnp.arange(half, dtype=f32) / HEAD)
     angles = positions.astype(f32)[:, None] * freqs[None, :]
     cosine, sine = jnp.cos(angles), jnp.sin(angles)
@@ -309,27 +380,41 @@
     sine = jnp.concatenate([-sine, sine], 1)
 
     flat = w_keyval.reshape(SLAB, 2 * ROWS * HEAD)
-    part = sds((ROWS, SHARD, 2 * HEAD), bf16)
-    joined_shape = sds((ROWS, 2, HALF, SLAB), bf16)
+    held = sds((SHARD, 2 * HEAD), bf16)
+    split = (ROWS, 2, HALF, 2 * HEAD)
     flops = 2 * SHARD * SLAB * 8 * HEAD
-    keyval_part, joined = local(
-        keyval_partial_body, (ids, mine, theirs, flat), (part, joined_shape), "keyval_partial", flops=flops
-    )
-    keyval_parts = lax.all_to_all(keyval_part, "row", 0, 0)
-    query_part = local(query_partial_body, (ids, joined, w_query), part, "query_partial", flops=flops)
-    held = sds((SHARD, 2 * HEAD), bf16)
+
+    def partial_sums(mine, theirs, weights, split_columns, steps, name):
+        parts = local(
+            functools.partial(partial_body, steps, split_columns),
+            (ids, mine, theirs, weights),
+            [sds(split, bf16)] * len(steps),
+            name,
+            flops=flops * len(steps) // ROWS,
+        )
+        return [value.reshape(SHARD, 2 * HEAD) for value in parts]
+
+    (far,) = partial_sums(mine, theirs, flat, True, (2,), "keyval_far")
+    mine, theirs, far = lax.optimization_barrier((mine, theirs, far))
+    up, down, kept = partial_sums(mine, theirs, flat, True, (1, 3, 0), "keyval_near")
+    mine, theirs, kept, cosine, sine = lax.optimization_barrier((mine, theirs, kept, cosine, sine))
+    keyval_sums = (kept, onward(up, 1), onward(down, 3), onward(far, 2))
+    steps = (2, 1, 3, 0)
+    query_sums = partial_sums(mine, theirs, w_query, False, steps, "query_partial")
     own = local(
-        functools.partial(rotate_body, 1), (ids, keyval_parts, cosine, sine), held, "keyval_rotate"
-    )
-    query_parts = lax.all_to_all(query_part, "row", 0, 0)
+        functools.partial(rotate_body, 1), (ids, *keyval_sums, cosine, sine), held, "keyval_rotate"
+    )
+    query_sums, own = lax.optimization_barrier((query_sums, own))
+    query_sums = [onward(value, step) if step else value for value, step in zip(query_sums, steps)]
 
     back1 = hop(own)
     back2 = hop(back1)
     mirror1 = mirrored(back1)
     chosen = mirrored(jnp.where(lax.axis_index("xh") == 0, own, back2))
 
+    query_sums, back2_here = lax.optimization_barrier((query_sums, back2))
     query = local(
-        functools.partial(rotate_body, 2), (ids, query_parts, cosine, sine), held, "query_rotate"
+        functools.partial(rotate_body, 2), (ids, *query_sums, cosine, sine), held, "query_rotate"
     )
     pair = paired(query)
 
@@ -337,7 +422,7 @@
     masked = pltpu.VMEM((SHARD, 2 * HEAD), bf16)
     before = local(
         early_body,
-        (ids, query, own, back1, mirror1, back2),
+        (ids, query, own, back1, mirror1, back2_here),
         sds(sums_shape, f32),
         "attend_early",
         scratch=[masked] * 4,
@@ -345,11 +430,17 @@
     )
     pieces = local(
         late_body,
-        (ids, query, pair, own, back1, mirror1, back2, chosen, before),
+        (ids, query, pair, own, back1, mirror1, back2_here, chosen, before),
         sds((2 * ROWS, PIECE, 2 * HEAD), bf16),
         "attend_late",
-        scratch=[pltpu.VMEM(sums_shape, f32), pltpu.VMEM(sums_shape, f32)] + [masked] * 5,
+        scratch=[
+            pltpu.VMEM(sums_shape, f32),
+            pltpu.VMEM(sums_shape, f32),
+            pltpu.VMEM((LISTED, HEAD), bf16),
+            pltpu.VMEM((LISTED, 2 * HEAD), bf16),
+        ],
         flops=2**31,
+        limit=16 * 2**20,
     )
     returned = lax.all_to_all(pieces, ("xl", "row"), 0, 0)
     return local(finish_body, (ids, returned), sds((BLOCK, ROWS * 2 * HEAD), bf16), "finish")

time: 100 us -> 87.3 us (0.87); the launches traced: 101 us -> 86.4 us
  waiting for transfers between devices: 23.4 us -> 17.9 us
  local copies, waits for them, and re-layouts: 6.68 us -> 2.44 us
  Pallas kernels: 18.9 us -> 14.7 us
    all_to_all x2 -> x0, waiting for transfers between devices: 11.3 us -> none  [the longest x1 11.3 us: on_device(): keyval_parts = lax.all_to_all(keyval_part, 'row', 0, 0)]
    ppermute x0 -> x6, waiting for transfers between devices: none -> 10.5 us  [onward(): lax.ppermute(value, 'row', [(row, (row + step) % ROWS) for row in range(R...]
    ppermute x0 -> x6, starting transfers between devices: none -> 7.48 us  [onward(): lax.ppermute(value, 'row', [(row, (row + step) % ROWS) for row in range(R...]
    all_to_all x2 -> x0, starting transfers between devices: 7.03 us -> none  [the longest x1 3.52 us: on_device(): query_parts = lax.all_to_all(query_part, 'row', 0, 0)]
    ppermute x5, waiting for transfers between devices: 10.7 us -> 5.4 us  [along_seq(): return lax.ppermute(value, SEQ, pairs)]
    pallas_call x8 -> x9, Pallas kernels: 18.9 us -> 14.7 us  [local(): pl.pallas_call(body, out_shape=out_shapes, in_specs=[SMEM] + [FAR if i in...]
    unnamed x13 -> x7, local copies, waits for them, and re-layouts: 4.95 us -> 1.7 us
  transfers between devices with their start and end apart: 9 -> 13, of which waited for: 6 -> 7; matrix products, arithmetic and copies ran while one was open for 3% -> 4% of each run, Pallas kernels for 9% -> 7%
where the time goes in v2:
time: 87.3 us; the launch traced here: 86.4 us
  blocking collectives  27.3 us (31%)
  starting transfers between devices  21.9 us (25%)
  waiting for transfers between devices  17.9 us (21%)
  Pallas kernels  14.7 us (17%)
  local copies, waits for them, and re-layouts  2.44 us (3%)
  other arithmetic  1.97 us (2%)
    all_to_all x1, blocking collectives, on_device(): mine = lax.all_to_all(normed, 'row', 0, 0)  14.7 us
    pallas_call x9, Pallas kernels, local(): pl.pallas_call(body, out_shape=out_shapes, in_specs=[SMEM] + [FAR if i in...  14.7 us
    ppermute x5, starting transfers between devices, along_seq(): return lax.ppermute(value, SEQ, pairs)  14.4 us
    all_to_all x1, blocking collectives, on_device(): returned = lax.all_to_all(pieces, ('xl', 'row'), 0, 0)  12.6 us
    ppermute x6, waiting for transfers between devices, onward(): lax.ppermute(value, 'row', [(row, (row + step) % ROWS) for row in range(R...  10.5 us
    ppermute x6, starting transfers between devices, onward(): lax.ppermute(value, 'row', [(row, (row + step) % ROWS) for row in range(R...  7.48 us
    ppermute x5, waiting for transfers between devices, along_seq(): return lax.ppermute(value, SEQ, pairs)  5.4 us
    ppermute x2, waiting for transfers between devices, swapped(): return lax.ppermute(value, 'col', [(0, 1), (1, 0)])  2.05 us
  transfers between devices with their start and end apart: 13, of which 7 were waited for; matrix products, arithmetic and copies ran while one was open for 4% of the time, Pallas kernels for 7%

profile of v2, /device:TPU:64, one launch (start us, length us, event | category | flops | bytes accessed | tf_op | source)
XLA Modules:
  0.0 86.4 jit_solution(8269738519671248990)
XLA Ops:
  0.0 0.7 reshape.40.gain
  0.8 0.7 pad_add_fusion.ids
  1.5 0.7 collective-permute-done.received
  2.2 1.1 %copy-done = bf16[128,2304]{1,0:T(8,128)(2,1)S(1)} copy-done((bf16[128,2304]{1,0:T(8,128)(2,1)S(1)}, bf16[128,2304]{1,0:T(8,128)(2,1)}, u32[]{:S(2)}) %copy-start) | copy-done | bytes 589848
  3.3 1.0 %norm.1 = bf16[4,64,1152]{2,1,0:T(8,128)(2,1)S(1)} custom-call(s32[35]{0:T(128)S(1)} %pad_add_fusion.ids, bf16[128,2304]{1,0:T(8,128)(2,1)S(1)} %copy-done, bf16[128,2304]{1,0:T(8,128)(2,1)S(1)} %collective-permute-done.received, f32[1,4608]{1,0:T(1,128)S(1)} %reshape.40.gain), custom_call_target="tpu_custom_call" | custom-call | bytes 1048576 | tf_op jit(solution)/shard_map/norm/pallas_call | solution.py:42
  4.3 14.7 %all_to_all.10.mine = bf16[4,64,1152]{2,1,0:T(8,128)(2,1)S(1)} all-to-all(bf16[4,64,1152]{2,1,0:T(8,128)(2,1)S(1)} %norm.1), channel_id=1, replica_groups=mesh['z'=8,'xh'=2,'xl'=2,'row'=4,'col'=2] {'row'}, dimensions={0} | all-to-all | bytes 1179648 | tf_op jit(solution)/shard_map/all_to_all | solution.py:370
  19.0 0.6 copy.6
  19.7 1.3 %collective-permute-done.1.theirs = bf16[4,64,1152]{2,1,0:T(8,128)(2,1)S(1)} collective-permute-done((bf16[4,64,1152]{2,1,0:T(8,128)(2,1)S(1)}, bf16[4,64,1152]{2,1,0:T(8,128)(2,1)S(1)}, u32[]{:S(2)}, u32[]{:S(2)}) %collective-permute-start.1) | collective-permute-done | bytes 589856 | tf_op jit(solution)/shard_map/ppermute | solution.py:350
  21.0 1.1 %keyval_far.1 = bf16[4,2,64,256]{3,2,1,0:T(8,128)(2,1)S(1)} custom-call(s32[35]{0:T(128)S(1)} %pad_add_fusion.ids, bf16[4,64,1152]{2,1,0:T(8,128)(2,1)S(1)} %all_to_all.10.mine, bf16[4,64,1152]{2,1,0:T(8,128)(2,1)S(1)} %collective-permute-done.1.theirs, bf16[1152,1024]{1,0:T(8,128)(2,1)S(1)} %bitcast.13), custom_call_target="tpu_custom_call" | custom-call | flops 301989888 | bytes 1048576 | tf_op jit(solution)/shard_map/keyval_far/pallas_call | solution.py:42
  22.1 1.8 %keyval_near.1 = (bf16[4,2,64,256]{3,2,1,0:T(8,128)(2,1)S(1)}, bf16[4,2,64,256]{3,2,1,0:T(8,128)(2,1)S(1)}, bf16[4,2,64,256]{3,2,1,0:T(8,128)(2,1)S(1)}) custom-call(s32[35]{0:T(128)S(1)} %pad_add_fusion.ids, bf16[4,64,1152]{2,1,0:T(8,128)(2,1)S(1)} %all_to_all.10.mine, bf16[4,64,1152]{2,1,0:T(8,128)(2,1)S(1)} %collective-permute-done.1.theirs, ...), custom_call_target="tpu_custom_call" | custom-call | flops 905969664 | bytes 1048576 | tf_op jit(solution)/shard_map/keyval_near/pallas_call | solution.py:42
  23.9 0.6 collective-permute-start.2
  24.6 2.7 %collective-permute-start.3 = (bf16[512,256]{1,0:T(8,128)(2,1)S(1)}, bf16[512,256]{1,0:T(8,128)(2,1)S(1)}, u32[]{:S(2)}, u32[]{:S(2)}) collective-permute-start(bf16[512,256]{1,0:T(8,128)(2,1)S(1)} %bitcast.18), channel_id=1, source_target_pairs={{0,6},{2,0},{4,2},{6,4},{1,7},{3,1},{5,3},{7,5},{8,14},{10,8},{12,... | collective-permute-start | bytes 786440 | tf_op jit(solution)/shard_map/ppermute | solution.py:346
  27.2 1.0 %fusion = (f32[512,64]{1,0:T(8,128)S(1)}, f32[512,64]{1,0:T(8,128)S(1)}, f32[512,64]{1,0:T(8,128)S(1)}) fusion(f32[64]{0:T(128)S(1)} %multiply_power_fusion, f32[512]{0:T(512)S(1)} %add_convert_fusion), kind=kLoop, calls=%fused_computation.5 | loop fusion | flops 65536 | bytes 395520 | tf_op jit(solution)/shard_map/neg | solution.py:380
  28.5 2.7 %query_partial.1 = (bf16[4,2,64,256]{3,2,1,0:T(8,128)(2,1)}, bf16[4,2,64,256]{3,2,1,0:T(8,128)(2,1)}, bf16[4,2,64,256]{3,2,1,0:T(8,128)(2,1)}, bf16[4,2,64,256]{3,2,1,0:T(8,128)(2,1)S(1)}) custom-call(s32[35]{0:T(128)S(1)} %pad_add_fusion.ids, bf16[4,64,1152]{2,1,0:T(8,128)(2,1)S(1)} %all_to_all.10.mine, ...), custom_call_target="tpu_custom_call" | custom-call | flops 1207959552 | bytes 1048576 | tf_op jit(solution)/shard_map/query_partial/pallas_call | solution.py:42
  31.2 8.0 %collective-permute-done.2.refs_1_ = bf16[512,256]{1,0:T(8,128)(2,1)S(1)} collective-permute-done((bf16[512,256]{1,0:T(8,128)(2,1)S(1)}, bf16[512,256]{1,0:T(8,128)(2,1)S(1)}, u32[]{:S(2)}, u32[]{:S(2)}) %collective-permute-start.2) | collective-permute-done | bytes 262176 | tf_op jit(solution)/shard_map/ppermute | solution.py:346
  39.2 0.8 keyval_rotate.1.own
  39.9 3.8 %collective-permute-start.8 = (bf16[512,256]{1,0:T(8,128)(2,1)S(1)}, bf16[512,256]{1,0:T(8,128)(2,1)S(1)}, u32[]{:S(2)}, u32[]{:S(2)}) collective-permute-start(bf16[512,256]{1,0:T(8,128)(2,1)S(1)} %keyval_rotate.1.own), channel_id=1, source_target_pairs={{0,32},{8,40},{16,48},{24,56},{32,64},{40,72},{48,80},{56,88},{64,... | collective-permute-start | bytes 786440 | tf_op jit(solution)/shard_map/ppermute | solution.py:329
  43.8 0.9 %collective-permute-start.5 = (bf16[512,256]{1,0:T(8,128)(2,1)}, bf16[512,256]{1,0:T(8,128)(2,1)S(1)}, u32[]{:S(2)}, u32[]{:S(2)}) collective-permute-start(bf16[512,256]{1,0:T(8,128)(2,1)} %bitcast.5), channel_id=1, source_target_pairs={{0,4},{2,6},{4,0},{6,2},{1,5},{3,7},{5,1},{7,3},{8,12},{10,14},{12... | collective-permute-start | bytes 786440 | tf_op jit(solution)/shard_map/ppermute | solution.py:346
  44.7 3.0 %collective-permute-start.6 = (bf16[512,256]{1,0:T(8,128)(2,1)}, bf16[512,256]{1,0:T(8,128)(2,1)S(1)}, u32[]{:S(2)}, u32[]{:S(2)}) collective-permute-start(bf16[512,256]{1,0:T(8,128)(2,1)} %bitcast.6), channel_id=1, source_target_pairs={{0,2},{2,4},{4,6},{6,0},{1,3},{3,5},{5,7},{7,1},{8,10},{10,12},{12... | collective-permute-start | bytes 786440 | tf_op jit(solution)/shard_map/ppermute | solution.py:346
  47.9 0.9 collective-permute-done.8.back1
  48.8 3.8 %collective-permute-start.9 = (bf16[512,256]{1,0:T(8,128)(2,1)S(1)}, bf16[512,256]{1,0:T(8,128)(2,1)S(1)}, u32[]{:S(2)}, u32[]{:S(2)}) collective-permute-start(bf16[512,256]{1,0:T(8,128)(2,1)S(1)} %collective-permute-done.8.back1), channel_id=1, source_target_pairs={{0,32},{8,40},{16,48},{24,56},{32,64},{40,72},{48,80},{56,88},{64,... | collective-permute-start | bytes 786440 | tf_op jit(solution)/shard_map/ppermute | solution.py:329
  52.6 2.8 %collective-permute-start.11 = (bf16[512,256]{1,0:T(8,128)(2,1)S(1)}, bf16[512,256]{1,0:T(8,128)(2,1)S(1)}, u32[]{:S(2)}, u32[]{:S(2)}) collective-permute-start(bf16[512,256]{1,0:T(8,128)(2,1)S(1)} %collective-permute-done.8.back1), channel_id=1, source_target_pairs={{0,24},{8,16},{16,8},{24,0},{32,56},{40,48},{48,40},{56,32},{64,88... | collective-permute-start | bytes 786440 | tf_op jit(solution)/shard_map/ppermute | solution.py:329
  55.5 2.4 %collective-permute-done.6.refs_1_ = bf16[512,256]{1,0:T(8,128)(2,1)S(1)} collective-permute-done((bf16[512,256]{1,0:T(8,128)(2,1)}, bf16[512,256]{1,0:T(8,128)(2,1)S(1)}, u32[]{:S(2)}, u32[]{:S(2)}) %collective-permute-start.6) | collective-permute-done | bytes 262176 | tf_op jit(solution)/shard_map/ppermute | solution.py:346
  57.9 0.8 query_rotate.1.query
  58.7 1.5 %collective-permute-start.10 = (bf16[512,256]{1,0:T(8,128)(2,1)S(1)}, bf16[512,256]{1,0:T(8,128)(2,1)S(1)}, u32[]{:S(2)}, u32[]{:S(2)}) collective-permute-start(bf16[512,256]{1,0:T(8,128)(2,1)S(1)} %query_rotate.1.query), channel_id=1, source_target_pairs={{0,8},{8,0},{16,24},{24,16},{32,40},{40,32},{48,56},{56,48},{64,72... | collective-permute-start | bytes 786440 | tf_op jit(solution)/shard_map/ppermute | solution.py:329
  60.2 2.4 %collective-permute-start.12 = (bf16[512,256]{1,0:T(8,128)(2,1)S(1)}, bf16[512,256]{1,0:T(8,128)(2,1)S(1)}, u32[]{:S(2)}, u32[]{:S(2)}) collective-permute-start(bf16[512,256]{1,0:T(8,128)(2,1)S(1)} %broadcast_select_fusion), channel_id=1, source_target_pairs={{0,24},{8,16},{16,8},{24,0},{32,56},{40,48},{48,40},{56,32},{64,88... | collective-permute-start | bytes 786440 | tf_op jit(solution)/shard_map/ppermute | solution.py:329
  62.6 2.5 %attend_early.1.before = f32[2,512,256]{2,1,0:T(8,128)S(1)} custom-call(s32[35]{0:T(128)S(1)} %pad_add_fusion.ids, bf16[512,256]{1,0:T(8,128)(2,1)S(1)} %query_rotate.1.query, bf16[512,256]{1,0:T(8,128)(2,1)S(1)} %keyval_rotate.1.own, bf16[512,256]{1,0:T(8,128)(2,1)S(1)} %collective-permute-done.8.back1, ...), custom_call_target="tpu_custom_call" | custom-call | flops 2147483648 | bytes 1048576 | tf_op jit(solution)/shard_map/attend_early/pallas_call | solution.py:42
  65.1 1.9 %collective-permute-done.10.pair = bf16[512,256]{1,0:T(8,128)(2,1)S(1)} collective-permute-done((bf16[512,256]{1,0:T(8,128)(2,1)S(1)}, bf16[512,256]{1,0:T(8,128)(2,1)S(1)}, u32[]{:S(2)}, u32[]{:S(2)}) %collective-permute-start.10) | collective-permute-done | bytes 262176 | tf_op jit(solution)/shard_map/ppermute | solution.py:329
  67.0 2.7 %collective-permute-done.12.chosen = bf16[512,256]{1,0:T(8,128)(2,1)S(1)} collective-permute-done((bf16[512,256]{1,0:T(8,128)(2,1)S(1)}, bf16[512,256]{1,0:T(8,128)(2,1)S(1)}, u32[]{:S(2)}, u32[]{:S(2)}) %collective-permute-start.12) | collective-permute-done | bytes 262176 | tf_op jit(solution)/shard_map/ppermute | solution.py:329
  69.7 2.6 %attend_late.1 = bf16[8,144,256]{2,1,0:T(8,128)(2,1)S(1)} custom-call(s32[35]{0:T(128)S(1)} %pad_add_fusion.ids, bf16[512,256]{1,0:T(8,128)(2,1)S(1)} %query_rotate.1.query, bf16[512,256]{1,0:T(8,128)(2,1)S(1)} %collective-permute-done.10.pair, bf16[512,256]{1,0:T(8,128)(2,1)S(1)} %keyval_rotate.1.own, bf16[512,256]{1,0:T(8,128)(2,1)S(1)} %collective-permute-done.8.back1, ...), custom_call_target="tpu_custom_call" | custom-call | flops 2147483648 | bytes 1048576 | tf_op jit(solution)/shard_map/attend_late/pallas_call | solution.py:42
  72.3 12.6 %all_to_all.11.pieces = bf16[8,144,256]{2,1,0:T(8,128)(2,1)S(1)} all-to-all(bf16[8,144,256]{2,1,0:T(8,128)(2,1)S(1)} %attend_late.1), channel_id=1, replica_groups=mesh['z'=8,'xh'=2,'xl'=2,'row'=4,'col'=2] {'xl','row'}, dimensions={0} | all-to-all | bytes 1179648 | tf_op jit(solution)/shard_map/all_to_all | solution.py:445
  84.9 1.5 %finish.1 = bf16[128,1024]{1,0:T(8,128)(2,1)} custom-call(s32[35]{0:T(128)S(1)} %pad_add_fusion.ids, bf16[8,144,256]{2,1,0:T(8,128)(2,1)S(1)} %all_to_all.11.pieces), custom_call_target="tpu_custom_call" | custom-call | bytes 1048576 | tf_op jit(solution)/shard_map/finish/pallas_call | solution.py:42
  (19 shorter events, 0.6 us)
Async XLA Ops:
  0.0 2.2 %collective-permute-start = (bf16[128,2304]{1,0:T(8,128)(2,1)}, bf16[128,2304]{1,0:T(8,128)(2,1)S(1)}, u32[]{:S(2)}, u32[]{:S(2)}) collective-permute-start(bf16[128,2304]{1,0:T(8,128)(2,1)} %tokens.1), channel_id=1, source_target_pairs={{0,1},{1,0},{2,3},{3,2},{4,5},{5,4},{6,7},{7,6},{8,9},{9,8},{10,11... | collective-permute-start | bytes 1769480 | tf_op jit(solution)/shard_map/ppermute | solution.py:350
  2.2 1.1 %copy-start = (bf16[128,2304]{1,0:T(8,128)(2,1)S(1)}, bf16[128,2304]{1,0:T(8,128)(2,1)}, u32[]{:S(2)}) copy-start(bf16[128,2304]{1,0:T(8,128)(2,1)} %tokens.1) | copy-start | bytes 1769476
  3.3 15.8 %copy-start.2 = (bf16[1152,2,512]{2,1,0:T(2,128)(2,1)S(1)}, bf16[1152,2,512]{2,1,0:T(2,128)(2,1)}, u32[]{:S(2)}) copy-start(bf16[1152,2,512]{2,1,0:T(2,128)(2,1)} %param.8) | copy-start | bytes 7077892
  19.0 2.0 %collective-permute-start.1 = (bf16[4,64,1152]{2,1,0:T(8,128)(2,1)S(1)}, bf16[4,64,1152]{2,1,0:T(8,128)(2,1)S(1)}, u32[]{:S(2)}, u32[]{:S(2)}) collective-permute-start(bf16[4,64,1152]{2,1,0:T(8,128)(2,1)S(1)} %all_to_all.10.mine), channel_id=1, source_target_pairs={{0,1},{1,0},{2,3},{3,2},{4,5},{5,4},{6,7},{7,6},{8,9},{9,8},{10,11... | collective-permute-start | bytes 1769480 | tf_op jit(solution)/shard_map/ppermute | solution.py:350
  22.1 6.3 %copy-start.1 = (bf16[1152,1024]{1,0:T(8,128)(2,1)S(1)}, bf16[1152,1024]{1,0:T(8,128)(2,1)}, u32[]{:S(2)}) copy-start(bf16[1152,1024]{1,0:T(8,128)(2,1)} %weights.1) | copy-start | bytes 7077892
  23.9 15.3 %collective-permute-start.2 = (bf16[512,256]{1,0:T(8,128)(2,1)S(1)}, bf16[512,256]{1,0:T(8,128)(2,1)S(1)}, u32[]{:S(2)}, u32[]{:S(2)}) collective-permute-start(bf16[512,256]{1,0:T(8,128)(2,1)S(1)} %bitcast.19), channel_id=1, source_target_pairs={{0,2},{2,4},{4,6},{6,0},{1,3},{3,5},{5,7},{7,1},{8,10},{10,12},{12... | collective-permute-start | bytes 786440 | tf_op jit(solution)/shard_map/ppermute | solution.py:346
  24.6 14.6 %collective-permute-start.3 = (bf16[512,256]{1,0:T(8,128)(2,1)S(1)}, bf16[512,256]{1,0:T(8,128)(2,1)S(1)}, u32[]{:S(2)}, u32[]{:S(2)}) collective-permute-start(bf16[512,256]{1,0:T(8,128)(2,1)S(1)} %bitcast.18), channel_id=1, source_target_pairs={{0,6},{2,0},{4,2},{6,4},{1,7},{3,1},{5,3},{7,5},{8,14},{10,8},{12,... | collective-permute-start | bytes 786440 | tf_op jit(solution)/shard_map/ppermute | solution.py:346
  27.2 11.9 %collective-permute-start.4 = (bf16[512,256]{1,0:T(8,128)(2,1)S(1)}, bf16[512,256]{1,0:T(8,128)(2,1)S(1)}, u32[]{:S(2)}, u32[]{:S(2)}) collective-permute-start(bf16[512,256]{1,0:T(8,128)(2,1)S(1)} %bitcast.15), channel_id=1, source_target_pairs={{0,4},{2,6},{4,0},{6,2},{1,5},{3,7},{5,1},{7,3},{8,12},{10,14},{12... | collective-permute-start | bytes 786440 | tf_op jit(solution)/shard_map/ppermute | solution.py:346
  39.9 8.9 %collective-permute-start.8 = (bf16[512,256]{1,0:T(8,128)(2,1)S(1)}, bf16[512,256]{1,0:T(8,128)(2,1)S(1)}, u32[]{:S(2)}, u32[]{:S(2)}) collective-permute-start(bf16[512,256]{1,0:T(8,128)(2,1)S(1)} %keyval_rotate.1.own), channel_id=1, source_target_pairs={{0,32},{8,40},{16,48},{24,56},{32,64},{40,72},{48,80},{56,88},{64,... | collective-permute-start | bytes 786440 | tf_op jit(solution)/shard_map/ppermute | solution.py:329
  43.8 11.7 %collective-permute-start.5 = (bf16[512,256]{1,0:T(8,128)(2,1)}, bf16[512,256]{1,0:T(8,128)(2,1)S(1)}, u32[]{:S(2)}, u32[]{:S(2)}) collective-permute-start(bf16[512,256]{1,0:T(8,128)(2,1)} %bitcast.5), channel_id=1, source_target_pairs={{0,4},{2,6},{4,0},{6,2},{1,5},{3,7},{5,1},{7,3},{8,12},{10,14},{12... | collective-permute-start | bytes 786440 | tf_op jit(solution)/shard_map/ppermute | solution.py:346
  44.7 13.2 %collective-permute-start.6 = (bf16[512,256]{1,0:T(8,128)(2,1)}, bf16[512,256]{1,0:T(8,128)(2,1)S(1)}, u32[]{:S(2)}, u32[]{:S(2)}) collective-permute-start(bf16[512,256]{1,0:T(8,128)(2,1)} %bitcast.6), channel_id=1, source_target_pairs={{0,2},{2,4},{4,6},{6,0},{1,3},{3,5},{5,7},{7,1},{8,10},{10,12},{12... | collective-permute-start | bytes 786440 | tf_op jit(solution)/shard_map/ppermute | solution.py:346
  47.7 10.2 %collective-permute-start.7 = (bf16[512,256]{1,0:T(8,128)(2,1)}, bf16[512,256]{1,0:T(8,128)(2,1)S(1)}, u32[]{:S(2)}, u32[]{:S(2)}) collective-permute-start(bf16[512,256]{1,0:T(8,128)(2,1)} %bitcast.7), channel_id=1, source_target_pairs={{0,6},{2,0},{4,2},{6,4},{1,7},{3,1},{5,3},{7,5},{8,14},{10,8},{12,... | collective-permute-start | bytes 786440 | tf_op jit(solution)/shard_map/ppermute | solution.py:346
  48.8 9.1 %collective-permute-start.9 = (bf16[512,256]{1,0:T(8,128)(2,1)S(1)}, bf16[512,256]{1,0:T(8,128)(2,1)S(1)}, u32[]{:S(2)}, u32[]{:S(2)}) collective-permute-start(bf16[512,256]{1,0:T(8,128)(2,1)S(1)} %collective-permute-done.8.back1), channel_id=1, source_target_pairs={{0,32},{8,40},{16,48},{24,56},{32,64},{40,72},{48,80},{56,88},{64,... | collective-permute-start | bytes 786440 | tf_op jit(solution)/shard_map/ppermute | solution.py:329
  52.6 10.0 %collective-permute-start.11 = (bf16[512,256]{1,0:T(8,128)(2,1)S(1)}, bf16[512,256]{1,0:T(8,128)(2,1)S(1)}, u32[]{:S(2)}, u32[]{:S(2)}) collective-permute-start(bf16[512,256]{1,0:T(8,128)(2,1)S(1)} %collective-permute-done.8.back1), channel_id=1, source_target_pairs={{0,24},{8,16},{16,8},{24,0},{32,56},{40,48},{48,40},{56,32},{64,88... | collective-permute-start | bytes 786440 | tf_op jit(solution)/shard_map/ppermute | solution.py:329
  58.7 8.3 %collective-permute-start.10 = (bf16[512,256]{1,0:T(8,128)(2,1)S(1)}, bf16[512,256]{1,0:T(8,128)(2,1)S(1)}, u32[]{:S(2)}, u32[]{:S(2)}) collective-permute-start(bf16[512,256]{1,0:T(8,128)(2,1)S(1)} %query_rotate.1.query), channel_id=1, source_target_pairs={{0,8},{8,0},{16,24},{24,16},{32,40},{40,32},{48,56},{56,48},{64,72... | collective-permute-start | bytes 786440 | tf_op jit(solution)/shard_map/ppermute | solution.py:329
  60.2 9.4 %collective-permute-start.12 = (bf16[512,256]{1,0:T(8,128)(2,1)S(1)}, bf16[512,256]{1,0:T(8,128)(2,1)S(1)}, u32[]{:S(2)}, u32[]{:S(2)}) collective-permute-start(bf16[512,256]{1,0:T(8,128)(2,1)S(1)} %broadcast_select_fusion), channel_id=1, source_target_pairs={{0,24},{8,16},{16,8},{24,0},{32,56},{40,48},{48,40},{56,32},{64,88... | collective-permute-start | bytes 786440 | tf_op jit(solution)/shard_map/ppermute | solution.py:329

commit v3 on v2

--- a/solution.py
+++ b/solution.py
@@ -38,11 +38,11 @@
 FAR = pl.BlockSpec(memory_space=pltpu.HBM)
 
 
-def local(body, operands, out_shapes, name, scratch=(), flops=0, limit=8 * 2**20, apart=()):
+def local(body, operands, out_shapes, name, scratch=(), flops=0, limit=8 * 2**20, specs=None):
     return pl.pallas_call(
         body,
         out_shape=out_shapes,
-        in_specs=[SMEM] + [FAR if i in apart else VMEM for i in range(1, len(operands))],
+        in_specs=specs or [SMEM] + [VMEM] * (len(operands) - 1),
         out_specs=jax.tree.map(lambda _: VMEM, out_shapes),
         scratch_shapes=list(scratch),
         compiler_params=pltpu.CompilerParams(vmem_limit_bytes=limit),
@@ -59,16 +59,21 @@
     return ids[3 + shard]
 
 
-def norm_body(ids, tokens, received, gain, out, held, arrived):
+def fetch_body(tokens, outgoing, kept, arrived):
+    core = lax.axis_index("col")
+    copies = []
+    for index, (side, to) in enumerate(((1 - core, outgoing), (core, kept))):
+        rows = pl.ds(pl.multiple_of(side * HALF, HALF), HALF)
+        copies.append(pltpu.make_async_copy(tokens.at[rows, :], to, arrived.at[index]))
+        copies[-1].start()
+    for copy in copies:
+        copy.wait()
+
+
+def norm_body(ids, own, received, gain, out):
     _, _, core = scalars(ids)
-    half = pl.ds(pl.multiple_of(core * HALF, HALF), HALF)
-    copy = pltpu.make_async_copy(tokens.at[half, :], held, arrived)
-    copy.start()
-    other = received[half, :].astype(f32)
-    total = jnp.sum(other * other, -1, keepdims=True)
-    copy.wait()
-    kept = held[...].astype(f32)
-    total = total + jnp.sum(kept * kept, -1, keepdims=True)
+    kept, other = own[...].astype(f32), received[...].astype(f32)
+    total = jnp.sum(kept * kept, -1, keepdims=True) + jnp.sum(other * other, -1, keepdims=True)
     inverse = lax.rsqrt(total * (1.0 / MODEL) + EPSILON)
     for part in range(2):
         span = slice(part * SLAB, (part + 1) * SLAB)
@@ -91,10 +96,21 @@
             columns = weights[:, pl.ds(pl.multiple_of(target * 2 * HEAD, 2 * HEAD), 2 * HEAD)]
         for slab, side in ((mine, core), (theirs, 1 - core)):
             rows = slab[...].reshape(ROWS * HALF, SLAB)
-            sums = jnp.dot(rows, columns, preferred_element_type=f32).astype(bf16)
+            sums = jnp.dot(rows, columns, preferred_element_type=f32)
             for block in range(ROWS):
                 value = sums[block * HALF : (block + 1) * HALF]
-                out[block, side] = value
+                if len(outs) == 2:
+                    outs[block // 2][block % 2, side] = value.astype(bf16)
+                else:
+                    out[block, side] = value.astype(out.dtype)
+
+
+def join_body(ids, up, down, first, second, up_out, down_out):
+    middle = SHARD // 2
+    up_out[:middle] = (up[:middle] + first[...].astype(f32)).astype(bf16)
+    up_out[middle:] = up[middle:].astype(bf16)
+    down_out[:middle] = down[:middle].astype(bf16)
+    down_out[middle:] = (down[middle:] + second[...].astype(f32)).astype(bf16)
 
 
 def rotate_body(rotated, ids, *refs):
@@ -231,8 +247,9 @@
         (mirror1, mirror1_shard, True),
         (chosen, chosen_shard, True),
     )
-    for keyval, key_shard, seen in listed:
-        before_this = used
+    for place, (keyval, key_shard, seen) in enumerate(listed):
+        if place == 4:
+            common = used
         counted = (key_shard >= first) & seen
         count = jnp.where(counted, live_of(ids, jnp.maximum(key_shard, 0)), 0)
         for start in range(0, SHARD, TILE):
@@ -276,7 +293,7 @@
                 lax.fori_loop(0, (used - low + (width - 1)) // width, step, 0)
 
     count, pair_count = live_of(ids, shard), live_of(ids, partner)
-    attend(query, count, before_this, 2, sums)
+    attend(query, count, common, 2, sums)
     attend(pair, pair_count, 0, 4, pair_sums)
     same = lax.broadcasted_iota(jnp.int32, (BLOCK, HEAD), 0) == lax.broadcasted_iota(
         jnp.int32, (BLOCK, HEAD), 1
@@ -338,6 +355,17 @@
     return along_seq(value, lambda z, x: (z, PLANE - 1 - x))
 
 
+def turned(value):
+    planes = SEQ_SHARDS // PLANE
+
+    def target(z, x):
+        if x < PLANE // 2:
+            return z, PLANE - 1 - x
+        return (z + 1, PLANE - 1 - x) if z % planes != planes - 1 else None
+
+    return along_seq(value, target)
+
+
 def paired(value):
     return along_seq(value, lambda z, x: (z, x ^ 1))
 
@@ -357,16 +385,18 @@
     ids = jnp.concatenate([jnp.stack([shard, row, core]).astype(jnp.int32), active])
     sds = jax.ShapeDtypeStruct
 
-    received = swapped(tokens)
+    half_shape = sds((HALF, MODEL // 2), bf16)
+    outgoing, kept = local(
+        fetch_body,
+        (tokens,),
+        (half_shape, half_shape),
+        "fetch",
+        scratch=[pltpu.SemaphoreType.DMA((2,))],
+        specs=[FAR],
+    )
+    received = swapped(outgoing)
     gain = norm_gain.reshape(1, MODEL)
-    normed = local(
-        norm_body,
-        (ids, tokens, received, gain),
-        sds((ROWS, HALF, SLAB), bf16),
-        "norm",
-        scratch=[pltpu.VMEM((HALF, ROWS * SLAB // 2), bf16), pltpu.SemaphoreType.DMA],
-        apart=(1,),
-    )
+    normed = local(norm_body, (ids, kept, received, gain), sds((ROWS, HALF, SLAB), bf16), "norm")
     mine = lax.all_to_all(normed, "row", 0, 0)
     mine, place = lax.optimization_barrier((mine, shard))
     theirs = swapped(mine)
@@ -384,25 +414,31 @@
     split = (ROWS, 2, HALF, 2 * HEAD)
     flops = 2 * SHARD * SLAB * 8 * HEAD
 
-    def partial_sums(mine, theirs, weights, split_columns, steps, name):
+    def sums_across(mine, theirs, weights, split_columns, steps, kind, name, count=1):
         parts = local(
             functools.partial(partial_body, steps, split_columns),
             (ids, mine, theirs, weights),
-            [sds(split, bf16)] * len(steps),
+            [sds((ROWS // count,) + split[1:], kind)] * (len(steps) * count),
             name,
             flops=flops * len(steps) // ROWS,
         )
-        return [value.reshape(SHARD, 2 * HEAD) for value in parts]
-
-    (far,) = partial_sums(mine, theirs, flat, True, (2,), "keyval_far")
-    mine, theirs, far = lax.optimization_barrier((mine, theirs, far))
-    up, down, kept = partial_sums(mine, theirs, flat, True, (1, 3, 0), "keyval_near")
+        return [value.reshape(SHARD // count, 2 * HEAD) for value in parts]
+
+    def joined(up, down, first, second, name):
+        return local(join_body, (ids, up, down, first, second), [held, held], name)
+
+    first, second = sums_across(mine, theirs, flat, True, (2,), bf16, "keyval_far", 2)
+    mine, theirs, first, second = lax.optimization_barrier((mine, theirs, first, second))
+    first, second = onward(first, 1), onward(second, 3)
+    up, down, kept = sums_across(mine, theirs, flat, True, (1, 3, 0), f32, "keyval_near")
     mine, theirs, kept, cosine, sine = lax.optimization_barrier((mine, theirs, kept, cosine, sine))
-    keyval_sums = (kept, onward(up, 1), onward(down, 3), onward(far, 2))
+    up, down = joined(up, down, first, second, "keyval_join")
+    mine, theirs, up, down = lax.optimization_barrier((mine, theirs, up, down))
+    up, down = onward(up, 1), onward(down, 3)
     steps = (2, 1, 3, 0)
-    query_sums = partial_sums(mine, theirs, w_query, False, steps, "query_partial")
+    query_sums = sums_across(mine, theirs, w_query, False, steps, bf16, "query_partial")
     own = local(
-        functools.partial(rotate_body, 1), (ids, *keyval_sums, cosine, sine), held, "keyval_rotate"
+        functools.partial(rotate_body, 1), (ids, kept, up, down, cosine, sine), held, "keyval_rotate"
     )
     query_sums, own = lax.optimization_barrier((query_sums, own))
     query_sums = [onward(value, step) if step else value for value, step in zip(query_sums, steps)]
@@ -410,9 +446,9 @@
     back1 = hop(own)
     back2 = hop(back1)
     mirror1 = mirrored(back1)
-    chosen = mirrored(jnp.where(lax.axis_index("xh") == 0, own, back2))
-
-    query_sums, back2_here = lax.optimization_barrier((query_sums, back2))
+    chosen = turned(jnp.where(lax.axis_index("xh") == 0, own, back1))
+
+    query_sums, back2 = lax.optimization_barrier((query_sums, back2))
     query = local(
         functools.partial(rotate_body, 2), (ids, *query_sums, cosine, sine), held, "query_rotate"
     )
@@ -422,7 +458,7 @@
     masked = pltpu.VMEM((SHARD, 2 * HEAD), bf16)
     before = local(
         early_body,
-        (ids, query, own, back1, mirror1, back2_here),
+        (ids, query, own, back1, mirror1, back2),
         sds(sums_shape, f32),
         "attend_early",
         scratch=[masked] * 4,
@@ -430,7 +466,7 @@
     )
     pieces = local(
         late_body,
-        (ids, query, pair, own, back1, mirror1, back2_here, chosen, before),
+        (ids, query, pair, own, back1, mirror1, back2, chosen, before),
         sds((2 * ROWS, PIECE, 2 * HEAD), bf16),
         "attend_late",
         scratch=[

time: 87.3 us -> 84.9 us (0.973)
  waiting for transfers between devices: 17.9 us -> 7.89 us
  starting transfers between devices: 21.9 us -> 26.4 us
  blocking collectives: 27.3 us -> 29.2 us
  local copies, waits for them, and re-layouts: 2.44 us -> 3.51 us
    ppermute x6 -> x7, waiting for transfers between devices: 10.5 us -> 3.9 us  [onward(): lax.ppermute(value, 'row', [(row, (row + step) % ROWS) for row in range(R...]
    ppermute x6 -> x7, starting transfers between devices: 7.48 us -> 12.5 us  [onward(): lax.ppermute(value, 'row', [(row, (row + step) % ROWS) for row in range(R...]
    ppermute x5, waiting for transfers between devices: 5.4 us -> 3.65 us  [along_seq(): return lax.ppermute(value, SEQ, pairs)]
    ppermute x2, waiting for transfers between devices: 2.05 us -> 0.33 us  [swapped(): return lax.ppermute(value, 'col', [(0, 1), (1, 0)])]
    all_to_all x1, blocking collectives: 12.6 us -> 14.1 us  [on_device(): returned = lax.all_to_all(pieces, ('xl', 'row'), 0, 0)]
    unnamed x7 -> x13, local copies, waits for them, and re-layouts: 1.7 us -> 2.76 us
    pallas_call x9 -> x11, Pallas kernels: 14.7 us -> 14.7 us  [local(): pl.pallas_call(body, out_shape=out_shapes, in_specs=specs or [SMEM] + [VM...]
  transfers between devices with their start and end apart: 13 -> 14, of which waited for: 7 -> 6; matrix products, arithmetic and copies ran while one was open for 4% -> 4% of each run, Pallas kernels for 7% -> 9%
where the time goes in v3:
time: 84.9 us; the launch traced here: 84.2 us
  blocking collectives  29.2 us (34%)
  starting transfers between devices  26.4 us (31%)
  Pallas kernels  14.7 us (17%)
  waiting for transfers between devices  7.89 us (9%)
  local copies, waits for them, and re-layouts  3.51 us (4%)
  other arithmetic  2.12 us (2%)
    all_to_all x1, blocking collectives, on_device(): mine = lax.all_to_all(normed, 'row', 0, 0)  15.1 us
    pallas_call x11, Pallas kernels, local(): pl.pallas_call(body, out_shape=out_shapes, in_specs=specs or [SMEM] + [VM...  14.7 us
    all_to_all x1, blocking collectives, on_device(): returned = lax.all_to_all(pieces, ('xl', 'row'), 0, 0)  14.1 us
    ppermute x5, starting transfers between devices, along_seq(): return lax.ppermute(value, SEQ, pairs)  13.8 us
    ppermute x7, starting transfers between devices, onward(): lax.ppermute(value, 'row', [(row, (row + step) % ROWS) for row in range(R...  12.5 us
    ppermute x7, waiting for transfers between devices, onward(): lax.ppermute(value, 'row', [(row, (row + step) % ROWS) for row in range(R...  3.9 us
    ppermute x5, waiting for transfers between devices, along_seq(): return lax.ppermute(value, SEQ, pairs)  3.65 us
    unnamed x13, local copies, waits for them, and re-layouts  2.76 us
  transfers between devices with their start and end apart: 14, of which 6 were waited for; matrix products, arithmetic and copies ran while one was open for 4% of the time, Pallas kernels for 9%

profile of v3, /device:TPU:64, one launch (start us, length us, event | category | flops | bytes accessed | tf_op | source)
XLA Modules:
  0.0 84.2 jit_solution(1783646547323434145)
XLA Ops:
  0.0 1.1 %copy-done.3 = bf16[128,2304]{1,0:T(8,128)(2,1)S(1)} copy-done((bf16[128,2304]{1,0:T(8,128)(2,1)S(1)}, bf16[128,2304]{1,0:T(8,128)(2,1)}, u32[]{:S(2)}) %copy-start.3) | copy-done | bytes 589848
  1.3 0.7 reshape.43.gain
  2.1 0.9 %pad_add_fusion.ids = s32[35]{0:T(128)S(1)} fusion(s32[32]{0:T(128)} %param.9, s32[1]{0:T(128)} %bitcast.2, s32[1]{0:T(128)} %bitcast.1, s32[1]{0:T(128)} %bitcast), kind=kLoop, calls=%fused_computation.7 | loop fusion | flops 105 | bytes 280 | tf_op jit(solution)/shard_map/concatenate | solution.py:385
  3.0 0.8 %norm.1 = bf16[4,64,1152]{2,1,0:T(8,128)(2,1)S(1)} custom-call(s32[35]{0:T(128)S(1)} %pad_add_fusion.ids, bf16[64,2304]{1,0:T(8,128)(2,1)S(1)} %get-tuple-element.43.own, bf16[64,2304]{1,0:T(8,128)(2,1)S(1)} %collective-permute-done.received, f32[1,4608]{1,0:T(1,128)S(1)} %reshape.43.gain), custom_call_target="tpu_custom_call" | custom-call | bytes 1048576 | tf_op jit(solution)/shard_map/norm/pallas_call | solution.py:42
  3.8 15.1 %all_to_all.10.mine = bf16[4,64,1152]{2,1,0:T(8,128)(2,1)S(1)} all-to-all(bf16[4,64,1152]{2,1,0:T(8,128)(2,1)S(1)} %norm.1), channel_id=1, replica_groups=mesh['z'=8,'xh'=2,'xl'=2,'row'=4,'col'=2] {'row'}, dimensions={0} | all-to-all | bytes 1179648 | tf_op jit(solution)/shard_map/all_to_all | solution.py:400
  18.9 0.6 copy.6
  19.6 1.0 %fusion = (f32[512,64]{1,0:T(8,128)S(1)}, f32[512,64]{1,0:T(8,128)S(1)}, f32[512,64]{1,0:T(8,128)S(1)}) fusion(f32[64]{0:T(128)S(1)} %multiply_power_fusion, f32[512]{0:T(512)S(1)} %add_convert_fusion), kind=kLoop, calls=%fused_computation.5 | loop fusion | flops 65536 | bytes 395520 | tf_op jit(solution)/shard_map/neg | solution.py:410
  20.9 1.1 %keyval_far.1 = (bf16[2,2,64,256]{3,2,1,0:T(8,128)(2,1)S(1)}, bf16[2,2,64,256]{3,2,1,0:T(8,128)(2,1)S(1)}) custom-call(s32[35]{0:T(128)S(1)} %pad_add_fusion.ids, bf16[4,64,1152]{2,1,0:T(8,128)(2,1)S(1)} %all_to_all.10.mine, bf16[4,64,1152]{2,1,0:T(8,128)(2,1)S(1)} %collective-permute-done.1.theirs, bf16[1152,1024]{1,0:T(8,128)(2,1)S(1)} %bitcast.14), custom_call_target="tpu_custom_call" | custom-call | flops 301989888 | bytes 1048576 | tf_op jit(solution)/shard_map/keyval_far/pallas_call | solution.py:42
  22.0 0.6 collective-permute-start.2
  22.7 2.7 %collective-permute-start.3 = (bf16[256,256]{1,0:T(8,128)(2,1)S(1)}, bf16[256,256]{1,0:T(8,128)(2,1)S(1)}, u32[]{:S(2)}, u32[]{:S(2)}) collective-permute-start(bf16[256,256]{1,0:T(8,128)(2,1)S(1)} %bitcast.22), channel_id=1, source_target_pairs={{0,6},{2,0},{4,2},{6,4},{1,7},{3,1},{5,3},{7,5},{8,14},{10,8},{12,... | collective-permute-start | bytes 393224 | tf_op jit(solution)/shard_map/ppermute | solution.py:374
  25.5 1.1 %copy-done.1 = bf16[4,64,1152]{2,1,0:T(8,128)(2,1)S(1)} copy-done((bf16[4,64,1152]{2,1,0:T(8,128)(2,1)S(1)}, bf16[4,64,1152]{2,1,0:T(8,128)(2,1)}, u32[]{:S(2)}) %copy-start.1) | copy-done | bytes 589848
  26.6 1.8 %keyval_near.1 = (f32[4,2,64,256]{3,2,1,0:T(8,128)S(1)}, f32[4,2,64,256]{3,2,1,0:T(8,128)S(1)}, f32[4,2,64,256]{3,2,1,0:T(8,128)S(1)}) custom-call(s32[35]{0:T(128)S(1)} %pad_add_fusion.ids, bf16[4,64,1152]{2,1,0:T(8,128)(2,1)S(1)} %all_to_all.10.mine, bf16[4,64,1152]{2,1,0:T(8,128)(2,1)S(1)} %copy-done.1, bf16[1152,1024]{1,0:T(8,128)(2,1)S(1)} %bitcast.15), custom_call_target="tpu_custom_call" | custom-call | flops 905969664 | bytes 1048576 | tf_op jit(solution)/shard_map/keyval_near/pallas_call | solution.py:42
  28.9 0.6 keyval_join.1
  29.6 3.2 %collective-permute-start.5 = (bf16[512,256]{1,0:T(8,128)(2,1)S(1)}, bf16[512,256]{1,0:T(8,128)(2,1)S(1)}, u32[]{:S(2)}, u32[]{:S(2)}) collective-permute-start(bf16[512,256]{1,0:T(8,128)(2,1)S(1)} %get-tuple-element.68), channel_id=1, source_target_pairs={{0,6},{2,0},{4,2},{6,4},{1,7},{3,1},{5,3},{7,5},{8,14},{10,8},{12,... | collective-permute-start | bytes 786440 | tf_op jit(solution)/shard_map/ppermute | solution.py:374
  32.8 2.1 %query_partial.1 = (bf16[4,2,64,256]{3,2,1,0:T(8,128)(2,1)}, bf16[4,2,64,256]{3,2,1,0:T(8,128)(2,1)S(1)}, bf16[4,2,64,256]{3,2,1,0:T(8,128)(2,1)S(1)}, bf16[4,2,64,256]{3,2,1,0:T(8,128)(2,1)S(1)}) custom-call(s32[35]{0:T(128)S(1)} %pad_add_fusion.ids, bf16[4,64,1152]{2,1,0:T(8,128)(2,1)S(1)} %all_to_all.10.mine, bf16[4,64,1152]{2,1,0:T(8,128)(2,1)S(1)} %copy-done.2, ...), custom_call_target="tpu_custom_call" | custom-call | flops 1207959552 | bytes 1048576 | tf_op jit(solution)/shard_map/query_partial/pallas_call | solution.py:42
  35.0 3.4 %collective-permute-done.4.refs_1_ = bf16[512,256]{1,0:T(8,128)(2,1)S(1)} collective-permute-done((bf16[512,256]{1,0:T(8,128)(2,1)S(1)}, bf16[512,256]{1,0:T(8,128)(2,1)S(1)}, u32[]{:S(2)}, u32[]{:S(2)}) %collective-permute-start.4) | collective-permute-done | bytes 262176 | tf_op jit(solution)/shard_map/ppermute | solution.py:374
  38.4 0.7 keyval_rotate.1.own
  39.1 3.8 %collective-permute-start.9 = (bf16[512,256]{1,0:T(8,128)(2,1)S(1)}, bf16[512,256]{1,0:T(8,128)(2,1)S(1)}, u32[]{:S(2)}, u32[]{:S(2)}) collective-permute-start(bf16[512,256]{1,0:T(8,128)(2,1)S(1)} %keyval_rotate.1.own), channel_id=1, source_target_pairs={{0,32},{8,40},{16,48},{24,56},{32,64},{40,72},{48,80},{56,88},{64,... | collective-permute-start | bytes 786440 | tf_op jit(solution)/shard_map/ppermute | solution.py:346
  43.0 2.7 %collective-permute-start.6 = (bf16[512,256]{1,0:T(8,128)(2,1)}, bf16[512,256]{1,0:T(8,128)(2,1)S(1)}, u32[]{:S(2)}, u32[]{:S(2)}) collective-permute-start(bf16[512,256]{1,0:T(8,128)(2,1)} %bitcast.8), channel_id=1, source_target_pairs={{0,4},{2,6},{4,0},{6,2},{1,5},{3,7},{5,1},{7,3},{8,12},{10,14},{12... | collective-permute-start | bytes 786440 | tf_op jit(solution)/shard_map/ppermute | solution.py:374
  45.6 1.2 %collective-permute-start.7 = (bf16[512,256]{1,0:T(8,128)(2,1)S(1)}, bf16[512,256]{1,0:T(8,128)(2,1)S(1)}, u32[]{:S(2)}, u32[]{:S(2)}) collective-permute-start(bf16[512,256]{1,0:T(8,128)(2,1)S(1)} %bitcast.21), channel_id=1, source_target_pairs={{0,2},{2,4},{4,6},{6,0},{1,3},{3,5},{5,7},{7,1},{8,10},{10,12},{12... | collective-permute-start | bytes 786440 | tf_op jit(solution)/shard_map/ppermute | solution.py:374
  46.9 2.0 %collective-permute-start.8 = (bf16[512,256]{1,0:T(8,128)(2,1)S(1)}, bf16[512,256]{1,0:T(8,128)(2,1)S(1)}, u32[]{:S(2)}, u32[]{:S(2)}) collective-permute-start(bf16[512,256]{1,0:T(8,128)(2,1)S(1)} %bitcast.20), channel_id=1, source_target_pairs={{0,6},{2,0},{4,2},{6,4},{1,7},{3,1},{5,3},{7,5},{8,14},{10,8},{12,... | collective-permute-start | bytes 786440 | tf_op jit(solution)/shard_map/ppermute | solution.py:374
  48.9 2.6 %collective-permute-start.10 = (bf16[512,256]{1,0:T(8,128)(2,1)S(1)}, bf16[512,256]{1,0:T(8,128)(2,1)S(1)}, u32[]{:S(2)}, u32[]{:S(2)}) collective-permute-start(bf16[512,256]{1,0:T(8,128)(2,1)S(1)} %collective-permute-done.9.back1), channel_id=1, source_target_pairs={{0,32},{8,40},{16,48},{24,56},{32,64},{40,72},{48,80},{56,88},{64,... | collective-permute-start | bytes 786440 | tf_op jit(solution)/shard_map/ppermute | solution.py:346
  51.5 3.0 %collective-permute-start.12 = (bf16[512,256]{1,0:T(8,128)(2,1)S(1)}, bf16[512,256]{1,0:T(8,128)(2,1)S(1)}, u32[]{:S(2)}, u32[]{:S(2)}) collective-permute-start(bf16[512,256]{1,0:T(8,128)(2,1)S(1)} %collective-permute-done.9.back1), channel_id=1, source_target_pairs={{0,24},{8,16},{16,8},{24,0},{32,56},{40,48},{48,40},{56,32},{64,88... | collective-permute-start | bytes 786440 | tf_op jit(solution)/shard_map/ppermute | solution.py:346
  54.6 4.0 %collective-permute-start.13 = (bf16[512,256]{1,0:T(8,128)(2,1)S(1)}, bf16[512,256]{1,0:T(8,128)(2,1)S(1)}, u32[]{:S(2)}, u32[]{:S(2)}) collective-permute-start(bf16[512,256]{1,0:T(8,128)(2,1)S(1)} %broadcast_select_fusion), channel_id=1, source_target_pairs={{0,24},{8,16},{16,40},{24,32},{32,56},{40,48},{48,72},{56,64},{64,... | collective-permute-start | bytes 786440 | tf_op jit(solution)/shard_map/ppermute | solution.py:346
  58.6 0.8 query_rotate.1.query
  59.7 0.8 collective-permute-done.12.mirror1
  60.5 2.5 %attend_early.1.before = f32[2,512,256]{2,1,0:T(8,128)S(1)} custom-call(s32[35]{0:T(128)S(1)} %pad_add_fusion.ids, bf16[512,256]{1,0:T(8,128)(2,1)S(1)} %query_rotate.1.query, bf16[512,256]{1,0:T(8,128)(2,1)S(1)} %keyval_rotate.1.own, bf16[512,256]{1,0:T(8,128)(2,1)S(1)} %collective-permute-done.9.back1, ...), custom_call_target="tpu_custom_call" | custom-call | flops 2147483648 | bytes 1048576 | tf_op jit(solution)/shard_map/attend_early/pallas_call | solution.py:42
  63.0 2.0 %collective-permute-done.13.chosen = bf16[512,256]{1,0:T(8,128)(2,1)S(1)} collective-permute-done((bf16[512,256]{1,0:T(8,128)(2,1)S(1)}, bf16[512,256]{1,0:T(8,128)(2,1)S(1)}, u32[]{:S(2)}, u32[]{:S(2)}) %collective-permute-start.13) | collective-permute-done | bytes 262176 | tf_op jit(solution)/shard_map/ppermute | solution.py:346
  65.0 0.9 %collective-permute-done.11.pair = bf16[512,256]{1,0:T(8,128)(2,1)S(1)} collective-permute-done((bf16[512,256]{1,0:T(8,128)(2,1)S(1)}, bf16[512,256]{1,0:T(8,128)(2,1)S(1)}, u32[]{:S(2)}, u32[]{:S(2)}) %collective-permute-start.11) | collective-permute-done | bytes 262176 | tf_op jit(solution)/shard_map/ppermute | solution.py:346
  65.9 2.7 %attend_late.1 = bf16[8,144,256]{2,1,0:T(8,128)(2,1)S(1)} custom-call(s32[35]{0:T(128)S(1)} %pad_add_fusion.ids, bf16[512,256]{1,0:T(8,128)(2,1)S(1)} %query_rotate.1.query, bf16[512,256]{1,0:T(8,128)(2,1)S(1)} %collective-permute-done.11.pair, bf16[512,256]{1,0:T(8,128)(2,1)S(1)} %keyval_rotate.1.own, bf16[512,256]{1,0:T(8,128)(2,1)S(1)} %collective-permute-done.9.back1, ...), custom_call_target="tpu_custom_call" | custom-call | flops 2147483648 | bytes 1048576 | tf_op jit(solution)/shard_map/attend_late/pallas_call | solution.py:42
  68.6 14.1 %all_to_all.11.pieces = bf16[8,144,256]{2,1,0:T(8,128)(2,1)S(1)} all-to-all(bf16[8,144,256]{2,1,0:T(8,128)(2,1)S(1)} %attend_late.1), channel_id=1, replica_groups=mesh['z'=8,'xh'=2,'xl'=2,'row'=4,'col'=2] {'xl','row'}, dimensions={0} | all-to-all | bytes 1179648 | tf_op jit(solution)/shard_map/all_to_all | solution.py:481
  82.7 1.5 %finish.1 = bf16[128,1024]{1,0:T(8,128)(2,1)} custom-call(s32[35]{0:T(128)S(1)} %pad_add_fusion.ids, bf16[8,144,256]{2,1,0:T(8,128)(2,1)S(1)} %all_to_all.11.pieces), custom_call_target="tpu_custom_call" | custom-call | bytes 1048576 | tf_op jit(solution)/shard_map/finish/pallas_call | solution.py:42
  (29 shorter events, 1.7 us)
Async XLA Ops:
  0.0 1.1 %copy-start.3 = (bf16[128,2304]{1,0:T(8,128)(2,1)S(1)}, bf16[128,2304]{1,0:T(8,128)(2,1)}, u32[]{:S(2)}) copy-start(bf16[128,2304]{1,0:T(8,128)(2,1)} %tokens.1) | copy-start | bytes 1769476
  1.2 1.8 %collective-permute-start = (bf16[64,2304]{1,0:T(8,128)(2,1)S(1)}, bf16[64,2304]{1,0:T(8,128)(2,1)S(1)}, u32[]{:S(2)}, u32[]{:S(2)}) collective-permute-start(bf16[64,2304]{1,0:T(8,128)(2,1)S(1)} %get-tuple-element.44), channel_id=1, source_target_pairs={{0,1},{1,0},{2,3},{3,2},{4,5},{5,4},{6,7},{7,6},{8,9},{9,8},{10,11... | collective-permute-start | bytes 884744 | tf_op jit(solution)/shard_map/ppermute | solution.py:378
  2.1 16.9 %copy-start.5 = (bf16[1152,2,512]{2,1,0:T(2,128)(2,1)S(1)}, bf16[1152,2,512]{2,1,0:T(2,128)(2,1)}, u32[]{:S(2)}) copy-start(bf16[1152,2,512]{2,1,0:T(2,128)(2,1)} %param.8) | copy-start | bytes 7077892
  18.9 2.0 %collective-permute-start.1 = (bf16[4,64,1152]{2,1,0:T(8,128)(2,1)S(1)}, bf16[4,64,1152]{2,1,0:T(8,128)(2,1)S(1)}, u32[]{:S(2)}, u32[]{:S(2)}) collective-permute-start(bf16[4,64,1152]{2,1,0:T(8,128)(2,1)S(1)} %all_to_all.10.mine), channel_id=1, source_target_pairs={{0,1},{1,0},{2,3},{3,2},{4,5},{5,4},{6,7},{7,6},{8,9},{9,8},{10,11... | collective-permute-start | bytes 1769480 | tf_op jit(solution)/shard_map/ppermute | solution.py:378
  20.9 4.4 %copy-start = (bf16[4,64,1152]{2,1,0:T(8,128)(2,1)}, bf16[4,64,1152]{2,1,0:T(8,128)(2,1)S(1)}, u32[]{:S(2)}) copy-start(bf16[4,64,1152]{2,1,0:T(8,128)(2,1)S(1)} %collective-permute-done.1.theirs) | copy-start | bytes 1769476
  22.0 6.9 %collective-permute-start.2 = (bf16[256,256]{1,0:T(8,128)(2,1)S(1)}, bf16[256,256]{1,0:T(8,128)(2,1)S(1)}, u32[]{:S(2)}, u32[]{:S(2)}) collective-permute-start(bf16[256,256]{1,0:T(8,128)(2,1)S(1)} %bitcast.23), channel_id=1, source_target_pairs={{0,2},{2,4},{4,6},{6,0},{1,3},{3,5},{5,7},{7,1},{8,10},{10,12},{12... | collective-permute-start | bytes 393224 | tf_op jit(solution)/shard_map/ppermute | solution.py:374
  22.7 6.2 %collective-permute-start.3 = (bf16[256,256]{1,0:T(8,128)(2,1)S(1)}, bf16[256,256]{1,0:T(8,128)(2,1)S(1)}, u32[]{:S(2)}, u32[]{:S(2)}) collective-permute-start(bf16[256,256]{1,0:T(8,128)(2,1)S(1)} %bitcast.22), channel_id=1, source_target_pairs={{0,6},{2,0},{4,2},{6,4},{1,7},{3,1},{5,3},{7,5},{8,14},{10,8},{12,... | collective-permute-start | bytes 393224 | tf_op jit(solution)/shard_map/ppermute | solution.py:374
  25.5 1.1 %copy-start.1 = (bf16[4,64,1152]{2,1,0:T(8,128)(2,1)S(1)}, bf16[4,64,1152]{2,1,0:T(8,128)(2,1)}, u32[]{:S(2)}) copy-start(bf16[4,64,1152]{2,1,0:T(8,128)(2,1)} %copy-done) | copy-start | bytes 1769476
  26.6 6.2 %copy-start.2 = (bf16[4,64,1152]{2,1,0:T(8,128)(2,1)S(1)}, bf16[4,64,1152]{2,1,0:T(8,128)(2,1)}, u32[]{:S(2)}) copy-start(bf16[4,64,1152]{2,1,0:T(8,128)(2,1)} %copy-done) | copy-start | bytes 1769476
  26.6 6.2 %copy-start.4 = (bf16[1152,1024]{1,0:T(8,128)(2,1)S(1)}, bf16[1152,1024]{1,0:T(8,128)(2,1)}, u32[]{:S(2)}) copy-start(bf16[1152,1024]{1,0:T(8,128)(2,1)} %weights.1) | copy-start | bytes 7077892
  29.5 8.9 %collective-permute-start.4 = (bf16[512,256]{1,0:T(8,128)(2,1)S(1)}, bf16[512,256]{1,0:T(8,128)(2,1)S(1)}, u32[]{:S(2)}, u32[]{:S(2)}) collective-permute-start(bf16[512,256]{1,0:T(8,128)(2,1)S(1)} %get-tuple-element.67), channel_id=1, source_target_pairs={{0,2},{2,4},{4,6},{6,0},{1,3},{3,5},{5,7},{7,1},{8,10},{10,12},{12... | collective-permute-start | bytes 786440 | tf_op jit(solution)/shard_map/ppermute | solution.py:374
  29.6 8.8 %collective-permute-start.5 = (bf16[512,256]{1,0:T(8,128)(2,1)S(1)}, bf16[512,256]{1,0:T(8,128)(2,1)S(1)}, u32[]{:S(2)}, u32[]{:S(2)}) collective-permute-start(bf16[512,256]{1,0:T(8,128)(2,1)S(1)} %get-tuple-element.68), channel_id=1, source_target_pairs={{0,6},{2,0},{4,2},{6,4},{1,7},{3,1},{5,3},{7,5},{8,14},{10,8},{12,... | collective-permute-start | bytes 786440 | tf_op jit(solution)/shard_map/ppermute | solution.py:374
  39.1 9.8 %collective-permute-start.9 = (bf16[512,256]{1,0:T(8,128)(2,1)S(1)}, bf16[512,256]{1,0:T(8,128)(2,1)S(1)}, u32[]{:S(2)}, u32[]{:S(2)}) collective-permute-start(bf16[512,256]{1,0:T(8,128)(2,1)S(1)} %keyval_rotate.1.own), channel_id=1, source_target_pairs={{0,32},{8,40},{16,48},{24,56},{32,64},{40,72},{48,80},{56,88},{64,... | collective-permute-start | bytes 786440 | tf_op jit(solution)/shard_map/ppermute | solution.py:346
  43.0 11.6 %collective-permute-start.6 = (bf16[512,256]{1,0:T(8,128)(2,1)}, bf16[512,256]{1,0:T(8,128)(2,1)S(1)}, u32[]{:S(2)}, u32[]{:S(2)}) collective-permute-start(bf16[512,256]{1,0:T(8,128)(2,1)} %bitcast.8), channel_id=1, source_target_pairs={{0,4},{2,6},{4,0},{6,2},{1,5},{3,7},{5,1},{7,3},{8,12},{10,14},{12... | collective-permute-start | bytes 786440 | tf_op jit(solution)/shard_map/ppermute | solution.py:374
  45.6 13.0 %collective-permute-start.7 = (bf16[512,256]{1,0:T(8,128)(2,1)S(1)}, bf16[512,256]{1,0:T(8,128)(2,1)S(1)}, u32[]{:S(2)}, u32[]{:S(2)}) collective-permute-start(bf16[512,256]{1,0:T(8,128)(2,1)S(1)} %bitcast.21), channel_id=1, source_target_pairs={{0,2},{2,4},{4,6},{6,0},{1,3},{3,5},{5,7},{7,1},{8,10},{10,12},{12... | collective-permute-start | bytes 786440 | tf_op jit(solution)/shard_map/ppermute | solution.py:374
  46.9 11.8 %collective-permute-start.8 = (bf16[512,256]{1,0:T(8,128)(2,1)S(1)}, bf16[512,256]{1,0:T(8,128)(2,1)S(1)}, u32[]{:S(2)}, u32[]{:S(2)}) collective-permute-start(bf16[512,256]{1,0:T(8,128)(2,1)S(1)} %bitcast.20), channel_id=1, source_target_pairs={{0,6},{2,0},{4,2},{6,4},{1,7},{3,1},{5,3},{7,5},{8,14},{10,8},{12,... | collective-permute-start | bytes 786440 | tf_op jit(solution)/shard_map/ppermute | solution.py:374
  48.9 9.7 %collective-permute-start.10 = (bf16[512,256]{1,0:T(8,128)(2,1)S(1)}, bf16[512,256]{1,0:T(8,128)(2,1)S(1)}, u32[]{:S(2)}, u32[]{:S(2)}) collective-permute-start(bf16[512,256]{1,0:T(8,128)(2,1)S(1)} %collective-permute-done.9.back1), channel_id=1, source_target_pairs={{0,32},{8,40},{16,48},{24,56},{32,64},{40,72},{48,80},{56,88},{64,... | collective-permute-start | bytes 786440 | tf_op jit(solution)/shard_map/ppermute | solution.py:346
  51.5 9.0 %collective-permute-start.12 = (bf16[512,256]{1,0:T(8,128)(2,1)S(1)}, bf16[512,256]{1,0:T(8,128)(2,1)S(1)}, u32[]{:S(2)}, u32[]{:S(2)}) collective-permute-start(bf16[512,256]{1,0:T(8,128)(2,1)S(1)} %collective-permute-done.9.back1), channel_id=1, source_target_pairs={{0,24},{8,16},{16,8},{24,0},{32,56},{40,48},{48,40},{56,32},{64,88... | collective-permute-start | bytes 786440 | tf_op jit(solution)/shard_map/ppermute | solution.py:346
  54.6 10.4 %collective-permute-start.13 = (bf16[512,256]{1,0:T(8,128)(2,1)S(1)}, bf16[512,256]{1,0:T(8,128)(2,1)S(1)}, u32[]{:S(2)}, u32[]{:S(2)}) collective-permute-start(bf16[512,256]{1,0:T(8,128)(2,1)S(1)} %broadcast_select_fusion), channel_id=1, source_target_pairs={{0,24},{8,16},{16,40},{24,32},{32,56},{40,48},{48,72},{56,64},{64,... | collective-permute-start | bytes 786440 | tf_op jit(solution)/shard_map/ppermute | solution.py:346
  59.4 6.5 %collective-permute-start.11 = (bf16[512,256]{1,0:T(8,128)(2,1)S(1)}, bf16[512,256]{1,0:T(8,128)(2,1)S(1)}, u32[]{:S(2)}, u32[]{:S(2)}) collective-permute-start(bf16[512,256]{1,0:T(8,128)(2,1)S(1)} %query_rotate.1.query), channel_id=1, source_target_pairs={{0,8},{8,0},{16,24},{24,16},{32,40},{40,32},{48,56},{56,48},{64,72... | collective-permute-start | bytes 786440 | tf_op jit(solution)/shard_map/ppermute | solution.py:346

commit v4 on v3

--- a/solution.py
+++ b/solution.py
@@ -70,8 +70,9 @@
         copy.wait()
 
 
-def norm_body(ids, own, received, gain, out):
-    _, _, core = scalars(ids)
+def norm_body(ids, own, received, gain, *refs):
+    outs, whole = refs[:ROWS], refs[ROWS]
+    _, row, core = scalars(ids)
     kept, other = own[...].astype(f32), received[...].astype(f32)
     total = jnp.sum(kept * kept, -1, keepdims=True) + jnp.sum(other * other, -1, keepdims=True)
     inverse = lax.rsqrt(total * (1.0 / MODEL) + EPSILON)
@@ -79,10 +80,13 @@
         span = slice(part * SLAB, (part + 1) * SLAB)
         for value, slab in ((kept, 2 * core + part), (other, 2 * (1 - core) + part)):
             scale = gain[:, pl.ds(pl.multiple_of(slab * SLAB, HEAD), SLAB)]
-            out[slab] = (value[:, span] * inverse * scale).astype(bf16)
-
-
-def partial_body(steps, split, ids, mine, theirs, weights, *outs):
+            whole[slab] = (value[:, span] * inverse * scale).astype(bf16)
+    for step in range(ROWS):
+        outs[step][...] = whole[(row + step) & (ROWS - 1)]
+
+
+def partial_body(steps, split, ids, *refs):
+    mine, theirs, weights, outs = refs[:ROWS], refs[ROWS : 2 * ROWS], refs[2 * ROWS], refs[2 * ROWS + 1 :]
     _, row, core = scalars(ids)
     for step, out in zip(steps, outs):
         target = (row + step) & (ROWS - 1)
@@ -94,15 +98,20 @@
             columns = jnp.concatenate(columns, 1)
         else:
             columns = weights[:, pl.ds(pl.multiple_of(target * 2 * HEAD, 2 * HEAD), 2 * HEAD)]
-        for slab, side in ((mine, core), (theirs, 1 - core)):
-            rows = slab[...].reshape(ROWS * HALF, SLAB)
-            sums = jnp.dot(rows, columns, preferred_element_type=f32)
-            for block in range(ROWS):
-                value = sums[block * HALF : (block + 1) * HALF]
-                if len(outs) == 2:
-                    outs[block // 2][block % 2, side] = value.astype(bf16)
+        for pieces, side in ((mine, core), (theirs, 1 - core)):
+            rows = jnp.concatenate([piece[...] for piece in pieces], 0)
+            sums = jnp.dot(rows, columns, preferred_element_type=f32).astype(out.dtype)
+            for back in range(ROWS):
+                block = (row - back) & (ROWS - 1)
+                value = sums[back * HALF : (back + 1) * HALF]
+                if len(outs) == len(steps):
+                    out[block, side] = value
                 else:
-                    out[block, side] = value.astype(out.dtype)
+                    for half in range(2):
+
+                        @pl.when(block >> 1 == half)
+                        def _(half=half, block=block, side=side, value=value):
+                            outs[half][block & 1, side] = value
 
 
 def join_body(ids, up, down, first, second, up_out, down_out):
@@ -396,10 +405,18 @@
     )
     received = swapped(outgoing)
     gain = norm_gain.reshape(1, MODEL)
-    normed = local(norm_body, (ids, kept, received, gain), sds((ROWS, HALF, SLAB), bf16), "norm")
-    mine = lax.all_to_all(normed, "row", 0, 0)
+    piece = sds((HALF, SLAB), bf16)
+    normed = local(
+        norm_body,
+        (ids, kept, received, gain),
+        [piece] * ROWS,
+        "norm",
+        scratch=[pltpu.VMEM((ROWS, HALF, SLAB), bf16)],
+    )
+    far_piece = onward(normed[2], 2)
+    mine = [normed[0], onward(normed[1], 1), far_piece, onward(normed[3], 3)]
+    theirs = [swapped(value) for value in mine]
     mine, place = lax.optimization_barrier((mine, shard))
-    theirs = swapped(mine)
 
     half = HEAD // 2
     positions = (place % SEQ_SHARDS) * SHARD + jnp.arange(SHARD, dtype=jnp.int32)
@@ -417,7 +434,7 @@
     def sums_across(mine, theirs, weights, split_columns, steps, kind, name, count=1):
         parts = local(
             functools.partial(partial_body, steps, split_columns),
-            (ids, mine, theirs, weights),
+            (ids, *mine, *theirs, weights),
             [sds((ROWS // count,) + split[1:], kind)] * (len(steps) * count),
             name,
             flops=flops * len(steps) // ROWS,

time: 84.9 us -> 81.6 us (0.961)
  blocking collectives: 29.2 us -> 14.1 us
  starting transfers between devices: 26.4 us -> 32.8 us
  waiting for transfers between devices: 7.89 us -> 11.6 us
  local copies, waits for them, and re-layouts: 3.51 us -> 5.01 us
    all_to_all x1 -> x0, blocking collectives: 15.1 us -> none  [on_device(): mine = lax.all_to_all(normed, 'row', 0, 0)]
    ppermute x7 -> x10, starting transfers between devices: 12.5 us -> 18.5 us  [onward(): lax.ppermute(value, 'row', [(row, (row + step) % ROWS) for row in range(R...]
    ppermute x7 -> x10, waiting for transfers between devices: 3.9 us -> 7.68 us  [onward(): lax.ppermute(value, 'row', [(row, (row + step) % ROWS) for row in range(R...]
    unnamed x13 -> x11, local copies, waits for them, and re-layouts: 2.76 us -> 4.26 us
  transfers between devices with their start and end apart: 14 -> 20, of which waited for: 6 -> 8; matrix products, arithmetic and copies ran while one was open for 4% -> 6% of each run, Pallas kernels for 9% -> 9%
where the time goes in v4:
time: 81.6 us; the launch traced here: 81.2 us
  starting transfers between devices  32.8 us (40%)
  Pallas kernels  15.3 us (19%)
  blocking collectives  14.1 us (17%)
  waiting for transfers between devices  11.6 us (14%)
  local copies, waits for them, and re-layouts  5.01 us (6%)
  other arithmetic  1.97 us (2%)
    ppermute x10, starting transfers between devices, onward(): lax.ppermute(value, 'row', [(row, (row + step) % ROWS) for row in range(R...  18.5 us
    pallas_call x11, Pallas kernels, local(): pl.pallas_call(body, out_shape=out_shapes, in_specs=specs or [SMEM] + [VM...  15.3 us
    all_to_all x1, blocking collectives, on_device(): returned = lax.all_to_all(pieces, ('xl', 'row'), 0, 0)  14.1 us
    ppermute x5, starting transfers between devices, along_seq(): return lax.ppermute(value, SEQ, pairs)  13.6 us
    ppermute x10, waiting for transfers between devices, onward(): lax.ppermute(value, 'row', [(row, (row + step) % ROWS) for row in range(R...  7.68 us
    unnamed x11, local copies, waits for them, and re-layouts  4.26 us
    ppermute x5, waiting for transfers between devices, along_seq(): return lax.ppermute(value, SEQ, pairs)  3.65 us
  transfers between devices with their start and end apart: 20, of which 8 were waited for; matrix products, arithmetic and copies ran while one was open for 6% of the time, Pallas kernels for 9%

profile of v4, /device:TPU:64, one launch (start us, length us, event | category | flops | bytes accessed | tf_op | source)
XLA Modules:
  0.0 81.2 jit_solution(5931442335203639802)
XLA Ops:
  0.0 1.1 %copy-done = bf16[128,2304]{1,0:T(8,128)(2,1)S(1)} copy-done((bf16[128,2304]{1,0:T(8,128)(2,1)S(1)}, bf16[128,2304]{1,0:T(8,128)(2,1)}, u32[]{:S(2)}) %copy-start) | copy-done | bytes 589848
  2.9 0.9 %norm.1 = (bf16[64,1152]{1,0:T(8,128)(2,1)S(1)}, bf16[64,1152]{1,0:T(8,128)(2,1)S(1)}, bf16[64,1152]{1,0:T(8,128)(2,1)S(1)}, bf16[64,1152]{1,0:T(8,128)(2,1)S(1)}) custom-call(s32[35]{0:T(128)S(1)} %pad_add_fusion.ids, bf16[64,2304]{1,0:T(8,128)(2,1)S(1)} %get-tuple-element.68.own, bf16[64,2304]{1,0:T(8,128)(2,1)S(1)} %collective-permute-done.received, ...), custom_call_target="tpu_custom_call" | custom-call | bytes 1048576 | tf_op jit(solution)/shard_map/norm/pallas_call | solution.py:42
  3.8 1.7 %collective-permute-start.1 = (bf16[64,1152]{1,0:T(8,128)(2,1)S(1)}, bf16[64,1152]{1,0:T(8,128)(2,1)S(1)}, u32[]{:S(2)}, u32[]{:S(2)}) collective-permute-start(bf16[64,1152]{1,0:T(8,128)(2,1)S(1)} %get-tuple-element.71), channel_id=1, source_target_pairs={{0,2},{2,4},{4,6},{6,0},{1,3},{3,5},{5,7},{7,1},{8,10},{10,12},{12... | collective-permute-start | bytes 442376 | tf_op jit(solution)/shard_map/ppermute | solution.py:383
  5.4 2.9 %collective-permute-start.2 = (bf16[64,1152]{1,0:T(8,128)(2,1)S(1)}, bf16[64,1152]{1,0:T(8,128)(2,1)S(1)}, u32[]{:S(2)}, u32[]{:S(2)}) collective-permute-start(bf16[64,1152]{1,0:T(8,128)(2,1)S(1)} %get-tuple-element.72), channel_id=1, source_target_pairs={{0,4},{2,6},{4,0},{6,2},{1,5},{3,7},{5,1},{7,3},{8,12},{10,14},{12... | collective-permute-start | bytes 442376 | tf_op jit(solution)/shard_map/ppermute | solution.py:383
  8.3 1.3 %collective-permute-start.3 = (bf16[64,1152]{1,0:T(8,128)(2,1)S(1)}, bf16[64,1152]{1,0:T(8,128)(2,1)S(1)}, u32[]{:S(2)}, u32[]{:S(2)}) collective-permute-start(bf16[64,1152]{1,0:T(8,128)(2,1)S(1)} %get-tuple-element.73), channel_id=1, source_target_pairs={{0,6},{2,0},{4,2},{6,4},{1,7},{3,1},{5,3},{7,5},{8,14},{10,8},{12,... | collective-permute-start | bytes 442376 | tf_op jit(solution)/shard_map/ppermute | solution.py:383
  9.7 2.3 %copy.6 = bf16[144,8,2,512]{3,1,2,0:T(8,128)(2,1)S(1)} copy(bf16[144,8,2,512]{3,2,1,0:T(2,128)(2,1)} %bitcast.25) | data formatting | bytes 4718592
  12.1 3.6 %collective-permute-done.2.refs_2_ = bf16[64,1152]{1,0:T(8,128)(2,1)S(1)} collective-permute-done((bf16[64,1152]{1,0:T(8,128)(2,1)S(1)}, bf16[64,1152]{1,0:T(8,128)(2,1)S(1)}, u32[]{:S(2)}, u32[]{:S(2)}) %collective-permute-start.2) | collective-permute-done | bytes 147488 | tf_op jit(solution)/shard_map/ppermute | solution.py:383
  16.3 1.0 %fusion = (f32[512,64]{1,0:T(8,128)S(1)}, f32[512,64]{1,0:T(8,128)S(1)}, f32[512,64]{1,0:T(8,128)S(1)}) fusion(f32[64]{0:T(128)S(1)} %multiply_power_fusion, f32[512]{0:T(512)S(1)} %add_convert_fusion), kind=kLoop, calls=%fused_computation.5 | loop fusion | flops 65536 | bytes 395520 | tf_op jit(solution)/shard_map/neg | solution.py:427
  17.5 1.6 %keyval_far.1 = (bf16[2,2,64,256]{3,2,1,0:T(8,128)(2,1)S(1)}, bf16[2,2,64,256]{3,2,1,0:T(8,128)(2,1)S(1)}) custom-call(s32[35]{0:T(128)S(1)} %pad_add_fusion.ids, bf16[64,1152]{1,0:T(8,128)(2,1)S(1)} %get-tuple-element.104.refs_0_, bf16[64,1152]{1,0:T(8,128)(2,1)S(1)} %collective-permute-done.1.refs_1_, bf16[64,1152]{1,0:T(8,128)(2,1)S(1)} %collective-permute-done.2.refs_2_, ...), custom_call_target="tpu_custom_call" | custom-call | flops 301989888 | bytes 1048576 | tf_op jit(solution)/shard_map/keyval_far/pallas_call | solution.py:42
  19.1 1.3 %collective-permute-start.8 = (bf16[256,256]{1,0:T(8,128)(2,1)S(1)}, bf16[256,256]{1,0:T(8,128)(2,1)S(1)}, u32[]{:S(2)}, u32[]{:S(2)}) collective-permute-start(bf16[256,256]{1,0:T(8,128)(2,1)S(1)} %bitcast.24), channel_id=1, source_target_pairs={{0,2},{2,4},{4,6},{6,0},{1,3},{3,5},{5,7},{7,1},{8,10},{10,12},{12... | collective-permute-start | bytes 393224 | tf_op jit(solution)/shard_map/ppermute | solution.py:383
  20.4 2.0 %collective-permute-start.9 = (bf16[256,256]{1,0:T(8,128)(2,1)S(1)}, bf16[256,256]{1,0:T(8,128)(2,1)S(1)}, u32[]{:S(2)}, u32[]{:S(2)}) collective-permute-start(bf16[256,256]{1,0:T(8,128)(2,1)S(1)} %bitcast.23), channel_id=1, source_target_pairs={{0,6},{2,0},{4,2},{6,4},{1,7},{3,1},{5,3},{7,5},{8,14},{10,8},{12,... | collective-permute-start | bytes 393224 | tf_op jit(solution)/shard_map/ppermute | solution.py:383
  22.7 0.9 %copy-done.2 = bf16[64,1152]{1,0:T(8,128)(2,1)S(1)} copy-done((bf16[64,1152]{1,0:T(8,128)(2,1)S(1)}, bf16[64,1152]{1,0:T(8,128)(2,1)}, u32[]{:S(2)}) %copy-start.2) | copy-done | bytes 147480
  23.6 1.8 %keyval_near.1 = (f32[4,2,64,256]{3,2,1,0:T(8,128)S(1)}, f32[4,2,64,256]{3,2,1,0:T(8,128)S(1)}, f32[4,2,64,256]{3,2,1,0:T(8,128)S(1)}) custom-call(s32[35]{0:T(128)S(1)} %pad_add_fusion.ids, bf16[64,1152]{1,0:T(8,128)(2,1)S(1)} %get-tuple-element.104.refs_0_, bf16[64,1152]{1,0:T(8,128)(2,1)S(1)} %collective-permute-done.1.refs_1_, ...), custom_call_target="tpu_custom_call" | custom-call | flops 905969664 | bytes 1048576 | tf_op jit(solution)/shard_map/keyval_near/pallas_call | solution.py:42
  26.7 1.1 %collective-permute-start.10 = (bf16[512,256]{1,0:T(8,128)(2,1)S(1)}, bf16[512,256]{1,0:T(8,128)(2,1)S(1)}, u32[]{:S(2)}, u32[]{:S(2)}) collective-permute-start(bf16[512,256]{1,0:T(8,128)(2,1)S(1)} %get-tuple-element.117), channel_id=1, source_target_pairs={{0,2},{2,4},{4,6},{6,0},{1,3},{3,5},{5,7},{7,1},{8,10},{10,12},{12... | collective-permute-start | bytes 786440 | tf_op jit(solution)/shard_map/ppermute | solution.py:383
  27.8 2.2 %collective-permute-start.11 = (bf16[512,256]{1,0:T(8,128)(2,1)S(1)}, bf16[512,256]{1,0:T(8,128)(2,1)S(1)}, u32[]{:S(2)}, u32[]{:S(2)}) collective-permute-start(bf16[512,256]{1,0:T(8,128)(2,1)S(1)} %get-tuple-element.118), channel_id=1, source_target_pairs={{0,6},{2,0},{4,2},{6,4},{1,7},{3,1},{5,3},{7,5},{8,14},{10,8},{12,... | collective-permute-start | bytes 786440 | tf_op jit(solution)/shard_map/ppermute | solution.py:383
  30.0 2.1 %query_partial.1 = (bf16[4,2,64,256]{3,2,1,0:T(8,128)(2,1)S(1)}, bf16[4,2,64,256]{3,2,1,0:T(8,128)(2,1)S(1)}, bf16[4,2,64,256]{3,2,1,0:T(8,128)(2,1)S(1)}, bf16[4,2,64,256]{3,2,1,0:T(8,128)(2,1)S(1)}) custom-call(s32[35]{0:T(128)S(1)} %pad_add_fusion.ids, bf16[64,1152]{1,0:T(8,128)(2,1)S(1)} %get-tuple-element.104.refs_0_, ...), custom_call_target="tpu_custom_call" | custom-call | flops 1207959552 | bytes 1048576 | tf_op jit(solution)/shard_map/query_partial/pallas_call | solution.py:42
  32.1 3.5 %collective-permute-done.10.refs_1_ = bf16[512,256]{1,0:T(8,128)(2,1)S(1)} collective-permute-done((bf16[512,256]{1,0:T(8,128)(2,1)S(1)}, bf16[512,256]{1,0:T(8,128)(2,1)S(1)}, u32[]{:S(2)}, u32[]{:S(2)}) %collective-permute-start.10) | collective-permute-done | bytes 262176 | tf_op jit(solution)/shard_map/ppermute | solution.py:383
  36.3 3.8 %collective-permute-start.15 = (bf16[512,256]{1,0:T(8,128)(2,1)S(1)}, bf16[512,256]{1,0:T(8,128)(2,1)S(1)}, u32[]{:S(2)}, u32[]{:S(2)}) collective-permute-start(bf16[512,256]{1,0:T(8,128)(2,1)S(1)} %keyval_rotate.1.own), channel_id=1, source_target_pairs={{0,32},{8,40},{16,48},{24,56},{32,64},{40,72},{48,80},{56,88},{64,... | collective-permute-start | bytes 786440 | tf_op jit(solution)/shard_map/ppermute | solution.py:355
  40.1 2.7 %collective-permute-start.12 = (bf16[512,256]{1,0:T(8,128)(2,1)S(1)}, bf16[512,256]{1,0:T(8,128)(2,1)S(1)}, u32[]{:S(2)}, u32[]{:S(2)}) collective-permute-start(bf16[512,256]{1,0:T(8,128)(2,1)S(1)} %bitcast.22), channel_id=1, source_target_pairs={{0,4},{2,6},{4,0},{6,2},{1,5},{3,7},{5,1},{7,3},{8,12},{10,14},{12... | collective-permute-start | bytes 786440 | tf_op jit(solution)/shard_map/ppermute | solution.py:383
  42.8 1.2 %collective-permute-start.13 = (bf16[512,256]{1,0:T(8,128)(2,1)S(1)}, bf16[512,256]{1,0:T(8,128)(2,1)S(1)}, u32[]{:S(2)}, u32[]{:S(2)}) collective-permute-start(bf16[512,256]{1,0:T(8,128)(2,1)S(1)} %bitcast.21), channel_id=1, source_target_pairs={{0,2},{2,4},{4,6},{6,0},{1,3},{3,5},{5,7},{7,1},{8,10},{10,12},{12... | collective-permute-start | bytes 786440 | tf_op jit(solution)/shard_map/ppermute | solution.py:383
  44.0 2.0 %collective-permute-start.14 = (bf16[512,256]{1,0:T(8,128)(2,1)S(1)}, bf16[512,256]{1,0:T(8,128)(2,1)S(1)}, u32[]{:S(2)}, u32[]{:S(2)}) collective-permute-start(bf16[512,256]{1,0:T(8,128)(2,1)S(1)} %bitcast.20), channel_id=1, source_target_pairs={{0,6},{2,0},{4,2},{6,4},{1,7},{3,1},{5,3},{7,5},{8,14},{10,8},{12,... | collective-permute-start | bytes 786440 | tf_op jit(solution)/shard_map/ppermute | solution.py:383
  46.0 2.6 %collective-permute-start.16 = (bf16[512,256]{1,0:T(8,128)(2,1)S(1)}, bf16[512,256]{1,0:T(8,128)(2,1)S(1)}, u32[]{:S(2)}, u32[]{:S(2)}) collective-permute-start(bf16[512,256]{1,0:T(8,128)(2,1)S(1)} %collective-permute-done.15.back1), channel_id=1, source_target_pairs={{0,32},{8,40},{16,48},{24,56},{32,64},{40,72},{48,80},{56,88},{64,... | collective-permute-start | bytes 786440 | tf_op jit(solution)/shard_map/ppermute | solution.py:355
  48.7 2.8 %collective-permute-start.18 = (bf16[512,256]{1,0:T(8,128)(2,1)S(1)}, bf16[512,256]{1,0:T(8,128)(2,1)S(1)}, u32[]{:S(2)}, u32[]{:S(2)}) collective-permute-start(bf16[512,256]{1,0:T(8,128)(2,1)S(1)} %collective-permute-done.15.back1), channel_id=1, source_target_pairs={{0,24},{8,16},{16,8},{24,0},{32,56},{40,48},{48,40},{56,32},{64,88... | collective-permute-start | bytes 786440 | tf_op jit(solution)/shard_map/ppermute | solution.py:355
  51.6 4.0 %collective-permute-start.19 = (bf16[512,256]{1,0:T(8,128)(2,1)S(1)}, bf16[512,256]{1,0:T(8,128)(2,1)S(1)}, u32[]{:S(2)}, u32[]{:S(2)}) collective-permute-start(bf16[512,256]{1,0:T(8,128)(2,1)S(1)} %broadcast_select_fusion), channel_id=1, source_target_pairs={{0,24},{8,16},{16,40},{24,32},{32,56},{40,48},{48,72},{56,64},{64,... | collective-permute-start | bytes 786440 | tf_op jit(solution)/shard_map/ppermute | solution.py:355
  55.6 0.8 query_rotate.1.query
  56.7 0.8 collective-permute-done.18.mirror1
  57.5 2.5 %attend_early.1.before = f32[2,512,256]{2,1,0:T(8,128)S(1)} custom-call(s32[35]{0:T(128)S(1)} %pad_add_fusion.ids, bf16[512,256]{1,0:T(8,128)(2,1)S(1)} %query_rotate.1.query, bf16[512,256]{1,0:T(8,128)(2,1)S(1)} %keyval_rotate.1.own, bf16[512,256]{1,0:T(8,128)(2,1)S(1)} %collective-permute-done.15.back1, ...), custom_call_target="tpu_custom_call" | custom-call | flops 2147483648 | bytes 1048576 | tf_op jit(solution)/shard_map/attend_early/pallas_call | solution.py:42
  60.0 2.1 %collective-permute-done.19.chosen = bf16[512,256]{1,0:T(8,128)(2,1)S(1)} collective-permute-done((bf16[512,256]{1,0:T(8,128)(2,1)S(1)}, bf16[512,256]{1,0:T(8,128)(2,1)S(1)}, u32[]{:S(2)}, u32[]{:S(2)}) %collective-permute-start.19) | collective-permute-done | bytes 262176 | tf_op jit(solution)/shard_map/ppermute | solution.py:355
  62.1 0.8 collective-permute-done.17.pair
  62.9 2.7 %attend_late.1 = bf16[8,144,256]{2,1,0:T(8,128)(2,1)S(1)} custom-call(s32[35]{0:T(128)S(1)} %pad_add_fusion.ids, bf16[512,256]{1,0:T(8,128)(2,1)S(1)} %query_rotate.1.query, bf16[512,256]{1,0:T(8,128)(2,1)S(1)} %collective-permute-done.17.pair, bf16[512,256]{1,0:T(8,128)(2,1)S(1)} %keyval_rotate.1.own, bf16[512,256]{1,0:T(8,128)(2,1)S(1)} %collective-permute-done.15.back1, ...), custom_call_target="tpu_custom_call" | custom-call | flops 2147483648 | bytes 1048576 | tf_op jit(solution)/shard_map/attend_late/pallas_call | solution.py:42
  65.6 14.1 %all_to_all.5.pieces = bf16[8,144,256]{2,1,0:T(8,128)(2,1)S(1)} all-to-all(bf16[8,144,256]{2,1,0:T(8,128)(2,1)S(1)} %attend_late.1), channel_id=1, replica_groups=mesh['z'=8,'xh'=2,'xl'=2,'row'=4,'col'=2] {'xl','row'}, dimensions={0} | all-to-all | bytes 1179648 | tf_op jit(solution)/shard_map/all_to_all | solution.py:498
  79.7 1.5 %finish.1 = bf16[128,1024]{1,0:T(8,128)(2,1)} custom-call(s32[35]{0:T(128)S(1)} %pad_add_fusion.ids, bf16[8,144,256]{2,1,0:T(8,128)(2,1)S(1)} %all_to_all.5.pieces), custom_call_target="tpu_custom_call" | custom-call | bytes 1048576 | tf_op jit(solution)/shard_map/finish/pallas_call | solution.py:42
  (38 shorter events, 5.3 us)
Async XLA Ops:
  0.0 1.1 %copy-start = (bf16[128,2304]{1,0:T(8,128)(2,1)S(1)}, bf16[128,2304]{1,0:T(8,128)(2,1)}, u32[]{:S(2)}) copy-start(bf16[128,2304]{1,0:T(8,128)(2,1)} %tokens.1) | copy-start | bytes 1769476
  1.2 1.7 %collective-permute-start = (bf16[64,2304]{1,0:T(8,128)(2,1)S(1)}, bf16[64,2304]{1,0:T(8,128)(2,1)S(1)}, u32[]{:S(2)}, u32[]{:S(2)}) collective-permute-start(bf16[64,2304]{1,0:T(8,128)(2,1)S(1)} %get-tuple-element.69), channel_id=1, source_target_pairs={{0,1},{1,0},{2,3},{3,2},{4,5},{5,4},{6,7},{7,6},{8,9},{9,8},{10,11... | collective-permute-start | bytes 884744 | tf_op jit(solution)/shard_map/ppermute | solution.py:387
  3.8 8.3 %collective-permute-start.1 = (bf16[64,1152]{1,0:T(8,128)(2,1)S(1)}, bf16[64,1152]{1,0:T(8,128)(2,1)S(1)}, u32[]{:S(2)}, u32[]{:S(2)}) collective-permute-start(bf16[64,1152]{1,0:T(8,128)(2,1)S(1)} %get-tuple-element.71), channel_id=1, source_target_pairs={{0,2},{2,4},{4,6},{6,0},{1,3},{3,5},{5,7},{7,1},{8,10},{10,12},{12... | collective-permute-start | bytes 442376 | tf_op jit(solution)/shard_map/ppermute | solution.py:383
  5.4 10.2 %collective-permute-start.2 = (bf16[64,1152]{1,0:T(8,128)(2,1)S(1)}, bf16[64,1152]{1,0:T(8,128)(2,1)S(1)}, u32[]{:S(2)}, u32[]{:S(2)}) collective-permute-start(bf16[64,1152]{1,0:T(8,128)(2,1)S(1)} %get-tuple-element.72), channel_id=1, source_target_pairs={{0,4},{2,6},{4,0},{6,2},{1,5},{3,7},{5,1},{7,3},{8,12},{10,14},{12... | collective-permute-start | bytes 442376 | tf_op jit(solution)/shard_map/ppermute | solution.py:383
  8.3 7.3 %collective-permute-start.3 = (bf16[64,1152]{1,0:T(8,128)(2,1)S(1)}, bf16[64,1152]{1,0:T(8,128)(2,1)S(1)}, u32[]{:S(2)}, u32[]{:S(2)}) collective-permute-start(bf16[64,1152]{1,0:T(8,128)(2,1)S(1)} %get-tuple-element.73), channel_id=1, source_target_pairs={{0,6},{2,0},{4,2},{6,4},{1,7},{3,1},{5,3},{7,5},{8,14},{10,8},{12,... | collective-permute-start | bytes 442376 | tf_op jit(solution)/shard_map/ppermute | solution.py:383
  12.0 5.3 %collective-permute-start.4 = (bf16[64,1152]{1,0:T(8,128)(2,1)S(1)}, bf16[64,1152]{1,0:T(8,128)(2,1)S(1)}, u32[]{:S(2)}, u32[]{:S(2)}) collective-permute-start(bf16[64,1152]{1,0:T(8,128)(2,1)S(1)} %get-tuple-element.104.refs_0_), channel_id=1, source_target_pairs={{0,1},{1,0},{2,3},{3,2},{4,5},{5,4},{6,7},{7,6},{8,9},{9,8},{10,11... | collective-permute-start | bytes 442376 | tf_op jit(solution)/shard_map/ppermute | solution.py:387
  15.7 1.6 %collective-permute-start.5 = (bf16[64,1152]{1,0:T(8,128)(2,1)S(1)}, bf16[64,1152]{1,0:T(8,128)(2,1)S(1)}, u32[]{:S(2)}, u32[]{:S(2)}) collective-permute-start(bf16[64,1152]{1,0:T(8,128)(2,1)S(1)} %collective-permute-done.1.refs_1_), channel_id=1, source_target_pairs={{0,1},{1,0},{2,3},{3,2},{4,5},{5,4},{6,7},{7,6},{8,9},{9,8},{10,11... | collective-permute-start | bytes 442376 | tf_op jit(solution)/shard_map/ppermute | solution.py:387
  15.7 1.6 %collective-permute-start.6 = (bf16[64,1152]{1,0:T(8,128)(2,1)S(1)}, bf16[64,1152]{1,0:T(8,128)(2,1)S(1)}, u32[]{:S(2)}, u32[]{:S(2)}) collective-permute-start(bf16[64,1152]{1,0:T(8,128)(2,1)S(1)} %collective-permute-done.2.refs_2_), channel_id=1, source_target_pairs={{0,1},{1,0},{2,3},{3,2},{4,5},{5,4},{6,7},{7,6},{8,9},{9,8},{10,11... | collective-permute-start | bytes 442376 | tf_op jit(solution)/shard_map/ppermute | solution.py:387
  16.2 1.4 %collective-permute-start.7 = (bf16[64,1152]{1,0:T(8,128)(2,1)S(1)}, bf16[64,1152]{1,0:T(8,128)(2,1)S(1)}, u32[]{:S(2)}, u32[]{:S(2)}) collective-permute-start(bf16[64,1152]{1,0:T(8,128)(2,1)S(1)} %collective-permute-done.3.refs_3_), channel_id=1, source_target_pairs={{0,1},{1,0},{2,3},{3,2},{4,5},{5,4},{6,7},{7,6},{8,9},{9,8},{10,11... | collective-permute-start | bytes 442376 | tf_op jit(solution)/shard_map/ppermute | solution.py:387
  17.3 5.2 %copy-start.1 = (bf16[64,1152]{1,0:T(8,128)(2,1)}, bf16[64,1152]{1,0:T(8,128)(2,1)S(1)}, u32[]{:S(2)}) copy-start(bf16[64,1152]{1,0:T(8,128)(2,1)S(1)} %collective-permute-done.4.refs_4_) | copy-start | bytes 442372
  19.1 6.9 %collective-permute-start.8 = (bf16[256,256]{1,0:T(8,128)(2,1)S(1)}, bf16[256,256]{1,0:T(8,128)(2,1)S(1)}, u32[]{:S(2)}, u32[]{:S(2)}) collective-permute-start(bf16[256,256]{1,0:T(8,128)(2,1)S(1)} %bitcast.24), channel_id=1, source_target_pairs={{0,2},{2,4},{4,6},{6,0},{1,3},{3,5},{5,7},{7,1},{8,10},{10,12},{12... | collective-permute-start | bytes 393224 | tf_op jit(solution)/shard_map/ppermute | solution.py:383
  20.4 5.6 %collective-permute-start.9 = (bf16[256,256]{1,0:T(8,128)(2,1)S(1)}, bf16[256,256]{1,0:T(8,128)(2,1)S(1)}, u32[]{:S(2)}, u32[]{:S(2)}) collective-permute-start(bf16[256,256]{1,0:T(8,128)(2,1)S(1)} %bitcast.23), channel_id=1, source_target_pairs={{0,6},{2,0},{4,2},{6,4},{1,7},{3,1},{5,3},{7,5},{8,14},{10,8},{12,... | collective-permute-start | bytes 393224 | tf_op jit(solution)/shard_map/ppermute | solution.py:383
  22.7 0.9 %copy-start.2 = (bf16[64,1152]{1,0:T(8,128)(2,1)S(1)}, bf16[64,1152]{1,0:T(8,128)(2,1)}, u32[]{:S(2)}) copy-start(bf16[64,1152]{1,0:T(8,128)(2,1)} %copy-done.1) | copy-start | bytes 442372
  23.6 6.4 %copy-start.3 = (bf16[64,1152]{1,0:T(8,128)(2,1)S(1)}, bf16[64,1152]{1,0:T(8,128)(2,1)}, u32[]{:S(2)}) copy-start(bf16[64,1152]{1,0:T(8,128)(2,1)} %copy-done.1) | copy-start | bytes 442372
  23.6 6.4 %copy-start.4 = (bf16[1152,1024]{1,0:T(8,128)(2,1)S(1)}, bf16[1152,1024]{1,0:T(8,128)(2,1)}, u32[]{:S(2)}) copy-start(bf16[1152,1024]{1,0:T(8,128)(2,1)} %refs_8_.1) | copy-start | bytes 7077892
  26.7 8.9 %collective-permute-start.10 = (bf16[512,256]{1,0:T(8,128)(2,1)S(1)}, bf16[512,256]{1,0:T(8,128)(2,1)S(1)}, u32[]{:S(2)}, u32[]{:S(2)}) collective-permute-start(bf16[512,256]{1,0:T(8,128)(2,1)S(1)} %get-tuple-element.117), channel_id=1, source_target_pairs={{0,2},{2,4},{4,6},{6,0},{1,3},{3,5},{5,7},{7,1},{8,10},{10,12},{12... | collective-permute-start | bytes 786440 | tf_op jit(solution)/shard_map/ppermute | solution.py:383
  27.8 7.8 %collective-permute-start.11 = (bf16[512,256]{1,0:T(8,128)(2,1)S(1)}, bf16[512,256]{1,0:T(8,128)(2,1)S(1)}, u32[]{:S(2)}, u32[]{:S(2)}) collective-permute-start(bf16[512,256]{1,0:T(8,128)(2,1)S(1)} %get-tuple-element.118), channel_id=1, source_target_pairs={{0,6},{2,0},{4,2},{6,4},{1,7},{3,1},{5,3},{7,5},{8,14},{10,8},{12,... | collective-permute-start | bytes 786440 | tf_op jit(solution)/shard_map/ppermute | solution.py:383
  36.3 9.8 %collective-permute-start.15 = (bf16[512,256]{1,0:T(8,128)(2,1)S(1)}, bf16[512,256]{1,0:T(8,128)(2,1)S(1)}, u32[]{:S(2)}, u32[]{:S(2)}) collective-permute-start(bf16[512,256]{1,0:T(8,128)(2,1)S(1)} %keyval_rotate.1.own), channel_id=1, source_target_pairs={{0,32},{8,40},{16,48},{24,56},{32,64},{40,72},{48,80},{56,88},{64,... | collective-permute-start | bytes 786440 | tf_op jit(solution)/shard_map/ppermute | solution.py:355
  40.1 11.4 %collective-permute-start.12 = (bf16[512,256]{1,0:T(8,128)(2,1)S(1)}, bf16[512,256]{1,0:T(8,128)(2,1)S(1)}, u32[]{:S(2)}, u32[]{:S(2)}) collective-permute-start(bf16[512,256]{1,0:T(8,128)(2,1)S(1)} %bitcast.22), channel_id=1, source_target_pairs={{0,4},{2,6},{4,0},{6,2},{1,5},{3,7},{5,1},{7,3},{8,12},{10,14},{12... | collective-permute-start | bytes 786440 | tf_op jit(solution)/shard_map/ppermute | solution.py:383
  42.8 12.8 %collective-permute-start.13 = (bf16[512,256]{1,0:T(8,128)(2,1)S(1)}, bf16[512,256]{1,0:T(8,128)(2,1)S(1)}, u32[]{:S(2)}, u32[]{:S(2)}) collective-permute-start(bf16[512,256]{1,0:T(8,128)(2,1)S(1)} %bitcast.21), channel_id=1, source_target_pairs={{0,2},{2,4},{4,6},{6,0},{1,3},{3,5},{5,7},{7,1},{8,10},{10,12},{12... | collective-permute-start | bytes 786440 | tf_op jit(solution)/shard_map/ppermute | solution.py:383
  44.0 11.6 %collective-permute-start.14 = (bf16[512,256]{1,0:T(8,128)(2,1)S(1)}, bf16[512,256]{1,0:T(8,128)(2,1)S(1)}, u32[]{:S(2)}, u32[]{:S(2)}) collective-permute-start(bf16[512,256]{1,0:T(8,128)(2,1)S(1)} %bitcast.20), channel_id=1, source_target_pairs={{0,6},{2,0},{4,2},{6,4},{1,7},{3,1},{5,3},{7,5},{8,14},{10,8},{12,... | collective-permute-start | bytes 786440 | tf_op jit(solution)/shard_map/ppermute | solution.py:383
  46.0 9.6 %collective-permute-start.16 = (bf16[512,256]{1,0:T(8,128)(2,1)S(1)}, bf16[512,256]{1,0:T(8,128)(2,1)S(1)}, u32[]{:S(2)}, u32[]{:S(2)}) collective-permute-start(bf16[512,256]{1,0:T(8,128)(2,1)S(1)} %collective-permute-done.15.back1), channel_id=1, source_target_pairs={{0,32},{8,40},{16,48},{24,56},{32,64},{40,72},{48,80},{56,88},{64,... | collective-permute-start | bytes 786440 | tf_op jit(solution)/shard_map/ppermute | solution.py:355
  48.7 8.8 %collective-permute-start.18 = (bf16[512,256]{1,0:T(8,128)(2,1)S(1)}, bf16[512,256]{1,0:T(8,128)(2,1)S(1)}, u32[]{:S(2)}, u32[]{:S(2)}) collective-permute-start(bf16[512,256]{1,0:T(8,128)(2,1)S(1)} %collective-permute-done.15.back1), channel_id=1, source_target_pairs={{0,24},{8,16},{16,8},{24,0},{32,56},{40,48},{48,40},{56,32},{64,88... | collective-permute-start | bytes 786440 | tf_op jit(solution)/shard_map/ppermute | solution.py:355
  51.6 10.5 %collective-permute-start.19 = (bf16[512,256]{1,0:T(8,128)(2,1)S(1)}, bf16[512,256]{1,0:T(8,128)(2,1)S(1)}, u32[]{:S(2)}, u32[]{:S(2)}) collective-permute-start(bf16[512,256]{1,0:T(8,128)(2,1)S(1)} %broadcast_select_fusion), channel_id=1, source_target_pairs={{0,24},{8,16},{16,40},{24,32},{32,56},{40,48},{48,72},{56,64},{64,... | collective-permute-start | bytes 786440 | tf_op jit(solution)/shard_map/ppermute | solution.py:355
  56.4 6.5 %collective-permute-start.17 = (bf16[512,256]{1,0:T(8,128)(2,1)S(1)}, bf16[512,256]{1,0:T(8,128)(2,1)S(1)}, u32[]{:S(2)}, u32[]{:S(2)}) collective-permute-start(bf16[512,256]{1,0:T(8,128)(2,1)S(1)} %query_rotate.1.query), channel_id=1, source_target_pairs={{0,8},{8,0},{16,24},{24,16},{32,40},{40,32},{48,56},{56,48},{64,72... | collective-permute-start | bytes 786440 | tf_op jit(solution)/shard_map/ppermute | solution.py:355

commit v5 on v4

--- a/solution.py
+++ b/solution.py
@@ -35,14 +35,13 @@
 f32 = jnp.float32
 VMEM = pl.BlockSpec(memory_space=pltpu.VMEM)
 SMEM = pl.BlockSpec(memory_space=pltpu.SMEM)
-FAR = pl.BlockSpec(memory_space=pltpu.HBM)
-
-
-def local(body, operands, out_shapes, name, scratch=(), flops=0, limit=8 * 2**20, specs=None):
+
+
+def local(body, operands, out_shapes, name, scratch=(), flops=0, limit=8 * 2**20):
     return pl.pallas_call(
         body,
         out_shape=out_shapes,
-        in_specs=specs or [SMEM] + [VMEM] * (len(operands) - 1),
+        in_specs=[SMEM] + [VMEM] * (len(operands) - 1),
         out_specs=jax.tree.map(lambda _: VMEM, out_shapes),
         scratch_shapes=list(scratch),
         compiler_params=pltpu.CompilerParams(vmem_limit_bytes=limit),
@@ -59,21 +58,11 @@
     return ids[3 + shard]
 
 
-def fetch_body(tokens, outgoing, kept, arrived):
-    core = lax.axis_index("col")
-    copies = []
-    for index, (side, to) in enumerate(((1 - core, outgoing), (core, kept))):
-        rows = pl.ds(pl.multiple_of(side * HALF, HALF), HALF)
-        copies.append(pltpu.make_async_copy(tokens.at[rows, :], to, arrived.at[index]))
-        copies[-1].start()
-    for copy in copies:
-        copy.wait()
-
-
 def norm_body(ids, own, received, gain, *refs):
     outs, whole = refs[:ROWS], refs[ROWS]
     _, row, core = scalars(ids)
-    kept, other = own[...].astype(f32), received[...].astype(f32)
+    kept = own[...].astype(f32)
+    other = received[pl.ds(pl.multiple_of(core * HALF, HALF), HALF), :].astype(f32)
     total = jnp.sum(kept * kept, -1, keepdims=True) + jnp.sum(other * other, -1, keepdims=True)
     inverse = lax.rsqrt(total * (1.0 / MODEL) + EPSILON)
     for part in range(2):
@@ -108,18 +97,14 @@
                     out[block, side] = value
                 else:
                     for half in range(2):
-
-                        @pl.when(block >> 1 == half)
-                        def _(half=half, block=block, side=side, value=value):
-                            outs[half][block & 1, side] = value
+                        outs[half][block, side] = value[:, half * HEAD : (half + 1) * HEAD]
 
 
 def join_body(ids, up, down, first, second, up_out, down_out):
-    middle = SHARD // 2
-    up_out[:middle] = (up[:middle] + first[...].astype(f32)).astype(bf16)
-    up_out[middle:] = up[middle:].astype(bf16)
-    down_out[:middle] = down[:middle].astype(bf16)
-    down_out[middle:] = (down[middle:] + second[...].astype(f32)).astype(bf16)
+    up_out[:, :HEAD] = (up[:, :HEAD] + first[...].astype(f32)).astype(bf16)
+    up_out[:, HEAD:] = up[:, HEAD:].astype(bf16)
+    down_out[:, :HEAD] = down[:, :HEAD].astype(bf16)
+    down_out[:, HEAD:] = (down[:, HEAD:] + second[...].astype(f32)).astype(bf16)
 
 
 def rotate_body(rotated, ids, *refs):
@@ -394,16 +379,8 @@
     ids = jnp.concatenate([jnp.stack([shard, row, core]).astype(jnp.int32), active])
     sds = jax.ShapeDtypeStruct
 
-    half_shape = sds((HALF, MODEL // 2), bf16)
-    outgoing, kept = local(
-        fetch_body,
-        (tokens,),
-        (half_shape, half_shape),
-        "fetch",
-        scratch=[pltpu.SemaphoreType.DMA((2,))],
-        specs=[FAR],
-    )
-    received = swapped(outgoing)
+    received = swapped(tokens)
+    kept = lax.dynamic_slice_in_dim(tokens, core * HALF, HALF, 0)
     gain = norm_gain.reshape(1, MODEL)
     piece = sds((HALF, SLAB), bf16)
     normed = local(
@@ -435,11 +412,11 @@
         parts = local(
             functools.partial(partial_body, steps, split_columns),
             (ids, *mine, *theirs, weights),
-            [sds((ROWS // count,) + split[1:], kind)] * (len(steps) * count),
+            [sds(split[:3] + (2 * HEAD // count,), kind)] * (len(steps) * count),
             name,
             flops=flops * len(steps) // ROWS,
         )
-        return [value.reshape(SHARD // count, 2 * HEAD) for value in parts]
+        return [value.reshape(SHARD, 2 * HEAD // count) for value in parts]
 
     def joined(up, down, first, second, name):
         return local(join_body, (ids, up, down, first, second), [held, held], name)

time: 81.6 us -> 80.9 us (level)
    unnamed x11 -> x9, local copies, waits for them, and re-layouts: 4.26 us -> 3.2 us
    dynamic_slice x0 -> x1, local copies, waits for them, and re-layouts: none -> 0.98 us  [on_device(): kept = lax.dynamic_slice_in_dim(tokens, core * HALF, HALF, 0)]
    pallas_call x11 -> x10, Pallas kernels: 15.3 us -> 14.5 us  [local(): pl.pallas_call(body, out_shape=out_shapes, in_specs=[SMEM] + [VMEM] * (le...]
  transfers between devices with their start and end apart: 20 -> 20, of which waited for: 8 -> 7; matrix products, arithmetic and copies ran while one was open for 6% -> 7% of each run, Pallas kernels for 9% -> 9%
where the time goes in v5:
time: 80.9 us; the launch traced here: 80.3 us
  starting transfers between devices  32.8 us (41%)
  Pallas kernels  14.5 us (18%)
  blocking collectives  14.2 us (18%)
  waiting for transfers between devices  11.6 us (14%)
  local copies, waits for them, and re-layouts  4.92 us (6%)
  other arithmetic  1.97 us (2%)
    ppermute x10, starting transfers between devices, onward(): lax.ppermute(value, 'row', [(row, (row + step) % ROWS) for row in range(R...  18.5 us
    pallas_call x10, Pallas kernels, local(): pl.pallas_call(body, out_shape=out_shapes, in_specs=[SMEM] + [VMEM] * (le...  14.5 us
    all_to_all x1, blocking collectives, on_device(): returned = lax.all_to_all(pieces, ('xl', 'row'), 0, 0)  14.2 us
    ppermute x5, starting transfers between devices, along_seq(): return lax.ppermute(value, SEQ, pairs)  13.6 us
    ppermute x10, waiting for transfers between devices, onward(): lax.ppermute(value, 'row', [(row, (row + step) % ROWS) for row in range(R...  7.74 us
    ppermute x5, waiting for transfers between devices, along_seq(): return lax.ppermute(value, SEQ, pairs)  3.65 us
    unnamed x9, local copies, waits for them, and re-layouts  3.2 us
  transfers between devices with their start and end apart: 20, of which 7 were waited for; matrix products, arithmetic and copies ran while one was open for 7% of the time, Pallas kernels for 9%

profile of v5, /device:TPU:64, one launch (start us, length us, event | category | flops | bytes accessed | tf_op | source)
XLA Modules:
  0.0 80.3 jit_solution(558871299871095037)
XLA Ops:
  1.5 1.0 %constant_dynamic-slice_fusion.own = bf16[64,2304]{1,0:T(8,128)(2,1)S(1)} fusion(bf16[128,2304]{1,0:T(8,128)(2,1)} %param.5, s32[]{:T(128)S(6)} %select_n.18), kind=kLoop, calls=%fused_computation.9 | loop fusion | bytes 589828 | tf_op jit(solution)/shard_map/dynamic_slice | solution.py:383
  2.5 0.9 %norm.1 = (bf16[64,1152]{1,0:T(8,128)(2,1)S(1)}, bf16[64,1152]{1,0:T(8,128)(2,1)S(1)}, bf16[64,1152]{1,0:T(8,128)(2,1)S(1)}, bf16[64,1152]{1,0:T(8,128)(2,1)S(1)}) custom-call(s32[35]{0:T(128)S(1)} %pad_add_fusion.ids, bf16[64,2304]{1,0:T(8,128)(2,1)S(1)} %constant_dynamic-slice_fusion.own, bf16[128,2304]{1,0:T(8,128)(2,1)S(1)} %collective-permute-done.received, ...), custom_call_target="tpu_custom_call" | custom-call | bytes 1048576 | tf_op jit(solution)/shard_map/norm/pallas_call | solution.py:41
  3.4 1.7 %collective-permute-start.1 = (bf16[64,1152]{1,0:T(8,128)(2,1)S(1)}, bf16[64,1152]{1,0:T(8,128)(2,1)S(1)}, u32[]{:S(2)}, u32[]{:S(2)}) collective-permute-start(bf16[64,1152]{1,0:T(8,128)(2,1)S(1)} %get-tuple-element.67), channel_id=1, source_target_pairs={{0,2},{2,4},{4,6},{6,0},{1,3},{3,5},{5,7},{7,1},{8,10},{10,12},{12... | collective-permute-start | bytes 442376 | tf_op jit(solution)/shard_map/ppermute | solution.py:368
  5.0 2.9 %collective-permute-start.2 = (bf16[64,1152]{1,0:T(8,128)(2,1)S(1)}, bf16[64,1152]{1,0:T(8,128)(2,1)S(1)}, u32[]{:S(2)}, u32[]{:S(2)}) collective-permute-start(bf16[64,1152]{1,0:T(8,128)(2,1)S(1)} %get-tuple-element.68), channel_id=1, source_target_pairs={{0,4},{2,6},{4,0},{6,2},{1,5},{3,7},{5,1},{7,3},{8,12},{10,14},{12... | collective-permute-start | bytes 442376 | tf_op jit(solution)/shard_map/ppermute | solution.py:368
  7.9 1.3 %collective-permute-start.3 = (bf16[64,1152]{1,0:T(8,128)(2,1)S(1)}, bf16[64,1152]{1,0:T(8,128)(2,1)S(1)}, u32[]{:S(2)}, u32[]{:S(2)}) collective-permute-start(bf16[64,1152]{1,0:T(8,128)(2,1)S(1)} %get-tuple-element.69), channel_id=1, source_target_pairs={{0,6},{2,0},{4,2},{6,4},{1,7},{3,1},{5,3},{7,5},{8,14},{10,8},{12,... | collective-permute-start | bytes 442376 | tf_op jit(solution)/shard_map/ppermute | solution.py:368
  9.3 2.3 %copy.6 = bf16[144,8,2,512]{3,1,2,0:T(8,128)(2,1)S(1)} copy(bf16[144,8,2,512]{3,2,1,0:T(2,128)(2,1)} %bitcast.25) | data formatting | bytes 4718592
  11.7 3.6 %collective-permute-done.2.refs_2_ = bf16[64,1152]{1,0:T(8,128)(2,1)S(1)} collective-permute-done((bf16[64,1152]{1,0:T(8,128)(2,1)S(1)}, bf16[64,1152]{1,0:T(8,128)(2,1)S(1)}, u32[]{:S(2)}, u32[]{:S(2)}) %collective-permute-start.2) | collective-permute-done | bytes 147488 | tf_op jit(solution)/shard_map/ppermute | solution.py:368
  15.9 1.0 %fusion = (f32[512,64]{1,0:T(8,128)S(1)}, f32[512,64]{1,0:T(8,128)S(1)}, f32[512,64]{1,0:T(8,128)S(1)}) fusion(f32[64]{0:T(128)S(1)} %multiply_power_fusion, f32[512]{0:T(512)S(1)} %add_convert_fusion), kind=kLoop, calls=%fused_computation.5 | loop fusion | flops 65536 | bytes 395520 | tf_op jit(solution)/shard_map/neg | solution.py:404
  17.2 1.1 %keyval_far.1 = (bf16[4,2,64,128]{3,2,1,0:T(8,128)(2,1)S(1)}, bf16[4,2,64,128]{3,2,1,0:T(8,128)(2,1)S(1)}) custom-call(s32[35]{0:T(128)S(1)} %pad_add_fusion.ids, bf16[64,1152]{1,0:T(8,128)(2,1)S(1)} %get-tuple-element.100.refs_0_, bf16[64,1152]{1,0:T(8,128)(2,1)S(1)} %collective-permute-done.1.refs_1_, bf16[64,1152]{1,0:T(8,128)(2,1)S(1)} %collective-permute-done.2.refs_2_, ...), custom_call_target="tpu_custom_call" | custom-call | flops 301989888 | bytes 1048576 | tf_op jit(solution)/shard_map/keyval_far/pallas_call | solution.py:41
  18.3 1.3 %collective-permute-start.8 = (bf16[512,128]{1,0:T(8,128)(2,1)S(1)}, bf16[512,128]{1,0:T(8,128)(2,1)S(1)}, u32[]{:S(2)}, u32[]{:S(2)}) collective-permute-start(bf16[512,128]{1,0:T(8,128)(2,1)S(1)} %bitcast.24), channel_id=1, source_target_pairs={{0,2},{2,4},{4,6},{6,0},{1,3},{3,5},{5,7},{7,1},{8,10},{10,12},{12... | collective-permute-start | bytes 393224 | tf_op jit(solution)/shard_map/ppermute | solution.py:368
  19.6 2.0 %collective-permute-start.9 = (bf16[512,128]{1,0:T(8,128)(2,1)S(1)}, bf16[512,128]{1,0:T(8,128)(2,1)S(1)}, u32[]{:S(2)}, u32[]{:S(2)}) collective-permute-start(bf16[512,128]{1,0:T(8,128)(2,1)S(1)} %bitcast.23), channel_id=1, source_target_pairs={{0,6},{2,0},{4,2},{6,4},{1,7},{3,1},{5,3},{7,5},{8,14},{10,8},{12,... | collective-permute-start | bytes 393224 | tf_op jit(solution)/shard_map/ppermute | solution.py:368
  21.8 0.9 %copy-done.1 = bf16[64,1152]{1,0:T(8,128)(2,1)S(1)} copy-done((bf16[64,1152]{1,0:T(8,128)(2,1)S(1)}, bf16[64,1152]{1,0:T(8,128)(2,1)}, u32[]{:S(2)}) %copy-start.1) | copy-done | bytes 147480
  22.8 1.8 %keyval_near.1 = (f32[4,2,64,256]{3,2,1,0:T(8,128)S(1)}, f32[4,2,64,256]{3,2,1,0:T(8,128)S(1)}, f32[4,2,64,256]{3,2,1,0:T(8,128)S(1)}) custom-call(s32[35]{0:T(128)S(1)} %pad_add_fusion.ids, bf16[64,1152]{1,0:T(8,128)(2,1)S(1)} %get-tuple-element.100.refs_0_, bf16[64,1152]{1,0:T(8,128)(2,1)S(1)} %collective-permute-done.1.refs_1_, ...), custom_call_target="tpu_custom_call" | custom-call | flops 905969664 | bytes 1048576 | tf_op jit(solution)/shard_map/keyval_near/pallas_call | solution.py:41
  25.8 1.1 %collective-permute-start.10 = (bf16[512,256]{1,0:T(8,128)(2,1)S(1)}, bf16[512,256]{1,0:T(8,128)(2,1)S(1)}, u32[]{:S(2)}, u32[]{:S(2)}) collective-permute-start(bf16[512,256]{1,0:T(8,128)(2,1)S(1)} %get-tuple-element.113), channel_id=1, source_target_pairs={{0,2},{2,4},{4,6},{6,0},{1,3},{3,5},{5,7},{7,1},{8,10},{10,12},{12... | collective-permute-start | bytes 786440 | tf_op jit(solution)/shard_map/ppermute | solution.py:368
  27.0 2.2 %collective-permute-start.11 = (bf16[512,256]{1,0:T(8,128)(2,1)S(1)}, bf16[512,256]{1,0:T(8,128)(2,1)S(1)}, u32[]{:S(2)}, u32[]{:S(2)}) collective-permute-start(bf16[512,256]{1,0:T(8,128)(2,1)S(1)} %get-tuple-element.114), channel_id=1, source_target_pairs={{0,6},{2,0},{4,2},{6,4},{1,7},{3,1},{5,3},{7,5},{8,14},{10,8},{12,... | collective-permute-start | bytes 786440 | tf_op jit(solution)/shard_map/ppermute | solution.py:368
  29.2 2.1 %query_partial.1 = (bf16[4,2,64,256]{3,2,1,0:T(8,128)(2,1)S(1)}, bf16[4,2,64,256]{3,2,1,0:T(8,128)(2,1)S(1)}, bf16[4,2,64,256]{3,2,1,0:T(8,128)(2,1)S(1)}, bf16[4,2,64,256]{3,2,1,0:T(8,128)(2,1)S(1)}) custom-call(s32[35]{0:T(128)S(1)} %pad_add_fusion.ids, bf16[64,1152]{1,0:T(8,128)(2,1)S(1)} %get-tuple-element.100.refs_0_, ...), custom_call_target="tpu_custom_call" | custom-call | flops 1207959552 | bytes 1048576 | tf_op jit(solution)/shard_map/query_partial/pallas_call | solution.py:41
  31.3 3.4 %collective-permute-done.10.refs_1_ = bf16[512,256]{1,0:T(8,128)(2,1)S(1)} collective-permute-done((bf16[512,256]{1,0:T(8,128)(2,1)S(1)}, bf16[512,256]{1,0:T(8,128)(2,1)S(1)}, u32[]{:S(2)}, u32[]{:S(2)}) %collective-permute-start.10) | collective-permute-done | bytes 262176 | tf_op jit(solution)/shard_map/ppermute | solution.py:368
  35.4 3.8 %collective-permute-start.15 = (bf16[512,256]{1,0:T(8,128)(2,1)S(1)}, bf16[512,256]{1,0:T(8,128)(2,1)S(1)}, u32[]{:S(2)}, u32[]{:S(2)}) collective-permute-start(bf16[512,256]{1,0:T(8,128)(2,1)S(1)} %keyval_rotate.1.own), channel_id=1, source_target_pairs={{0,32},{8,40},{16,48},{24,56},{32,64},{40,72},{48,80},{56,88},{64,... | collective-permute-start | bytes 786440 | tf_op jit(solution)/shard_map/ppermute | solution.py:340
  39.3 2.7 %collective-permute-start.12 = (bf16[512,256]{1,0:T(8,128)(2,1)S(1)}, bf16[512,256]{1,0:T(8,128)(2,1)S(1)}, u32[]{:S(2)}, u32[]{:S(2)}) collective-permute-start(bf16[512,256]{1,0:T(8,128)(2,1)S(1)} %bitcast.22), channel_id=1, source_target_pairs={{0,4},{2,6},{4,0},{6,2},{1,5},{3,7},{5,1},{7,3},{8,12},{10,14},{12... | collective-permute-start | bytes 786440 | tf_op jit(solution)/shard_map/ppermute | solution.py:368
  42.0 1.2 %collective-permute-start.13 = (bf16[512,256]{1,0:T(8,128)(2,1)S(1)}, bf16[512,256]{1,0:T(8,128)(2,1)S(1)}, u32[]{:S(2)}, u32[]{:S(2)}) collective-permute-start(bf16[512,256]{1,0:T(8,128)(2,1)S(1)} %bitcast.21), channel_id=1, source_target_pairs={{0,2},{2,4},{4,6},{6,0},{1,3},{3,5},{5,7},{7,1},{8,10},{10,12},{12... | collective-permute-start | bytes 786440 | tf_op jit(solution)/shard_map/ppermute | solution.py:368
  43.2 2.0 %collective-permute-start.14 = (bf16[512,256]{1,0:T(8,128)(2,1)S(1)}, bf16[512,256]{1,0:T(8,128)(2,1)S(1)}, u32[]{:S(2)}, u32[]{:S(2)}) collective-permute-start(bf16[512,256]{1,0:T(8,128)(2,1)S(1)} %bitcast.20), channel_id=1, source_target_pairs={{0,6},{2,0},{4,2},{6,4},{1,7},{3,1},{5,3},{7,5},{8,14},{10,8},{12,... | collective-permute-start | bytes 786440 | tf_op jit(solution)/shard_map/ppermute | solution.py:368
  45.2 2.6 %collective-permute-start.16 = (bf16[512,256]{1,0:T(8,128)(2,1)S(1)}, bf16[512,256]{1,0:T(8,128)(2,1)S(1)}, u32[]{:S(2)}, u32[]{:S(2)}) collective-permute-start(bf16[512,256]{1,0:T(8,128)(2,1)S(1)} %collective-permute-done.15.back1), channel_id=1, source_target_pairs={{0,32},{8,40},{16,48},{24,56},{32,64},{40,72},{48,80},{56,88},{64,... | collective-permute-start | bytes 786440 | tf_op jit(solution)/shard_map/ppermute | solution.py:340
  47.8 2.8 %collective-permute-start.18 = (bf16[512,256]{1,0:T(8,128)(2,1)S(1)}, bf16[512,256]{1,0:T(8,128)(2,1)S(1)}, u32[]{:S(2)}, u32[]{:S(2)}) collective-permute-start(bf16[512,256]{1,0:T(8,128)(2,1)S(1)} %collective-permute-done.15.back1), channel_id=1, source_target_pairs={{0,24},{8,16},{16,8},{24,0},{32,56},{40,48},{48,40},{56,32},{64,88... | collective-permute-start | bytes 786440 | tf_op jit(solution)/shard_map/ppermute | solution.py:340
  50.7 4.0 %collective-permute-start.19 = (bf16[512,256]{1,0:T(8,128)(2,1)S(1)}, bf16[512,256]{1,0:T(8,128)(2,1)S(1)}, u32[]{:S(2)}, u32[]{:S(2)}) collective-permute-start(bf16[512,256]{1,0:T(8,128)(2,1)S(1)} %broadcast_select_fusion), channel_id=1, source_target_pairs={{0,24},{8,16},{16,40},{24,32},{32,56},{40,48},{48,72},{56,64},{64,... | collective-permute-start | bytes 786440 | tf_op jit(solution)/shard_map/ppermute | solution.py:340
  54.8 0.8 query_rotate.1.query
  55.9 0.8 collective-permute-done.18.mirror1
  56.6 2.5 %attend_early.1.before = f32[2,512,256]{2,1,0:T(8,128)S(1)} custom-call(s32[35]{0:T(128)S(1)} %pad_add_fusion.ids, bf16[512,256]{1,0:T(8,128)(2,1)S(1)} %query_rotate.1.query, bf16[512,256]{1,0:T(8,128)(2,1)S(1)} %keyval_rotate.1.own, bf16[512,256]{1,0:T(8,128)(2,1)S(1)} %collective-permute-done.15.back1, ...), custom_call_target="tpu_custom_call" | custom-call | flops 2147483648 | bytes 1048576 | tf_op jit(solution)/shard_map/attend_early/pallas_call | solution.py:41
  59.1 2.1 %collective-permute-done.19.chosen = bf16[512,256]{1,0:T(8,128)(2,1)S(1)} collective-permute-done((bf16[512,256]{1,0:T(8,128)(2,1)S(1)}, bf16[512,256]{1,0:T(8,128)(2,1)S(1)}, u32[]{:S(2)}, u32[]{:S(2)}) %collective-permute-start.19) | collective-permute-done | bytes 262176 | tf_op jit(solution)/shard_map/ppermute | solution.py:340
  61.3 0.7 collective-permute-done.17.pair
  62.0 2.6 %attend_late.1 = bf16[8,144,256]{2,1,0:T(8,128)(2,1)S(1)} custom-call(s32[35]{0:T(128)S(1)} %pad_add_fusion.ids, bf16[512,256]{1,0:T(8,128)(2,1)S(1)} %query_rotate.1.query, bf16[512,256]{1,0:T(8,128)(2,1)S(1)} %collective-permute-done.17.pair, bf16[512,256]{1,0:T(8,128)(2,1)S(1)} %keyval_rotate.1.own, bf16[512,256]{1,0:T(8,128)(2,1)S(1)} %collective-permute-done.15.back1, ...), custom_call_target="tpu_custom_call" | custom-call | flops 2147483648 | bytes 1048576 | tf_op jit(solution)/shard_map/attend_late/pallas_call | solution.py:41
  64.6 14.2 %all_to_all.5.pieces = bf16[8,144,256]{2,1,0:T(8,128)(2,1)S(1)} all-to-all(bf16[8,144,256]{2,1,0:T(8,128)(2,1)S(1)} %attend_late.1), channel_id=1, replica_groups=mesh['z'=8,'xh'=2,'xl'=2,'row'=4,'col'=2] {'xl','row'}, dimensions={0} | all-to-all | bytes 1179648 | tf_op jit(solution)/shard_map/all_to_all | solution.py:475
  78.8 1.5 %finish.1 = bf16[128,1024]{1,0:T(8,128)(2,1)} custom-call(s32[35]{0:T(128)S(1)} %pad_add_fusion.ids, bf16[8,144,256]{2,1,0:T(8,128)(2,1)S(1)} %all_to_all.5.pieces), custom_call_target="tpu_custom_call" | custom-call | bytes 1048576 | tf_op jit(solution)/shard_map/finish/pallas_call | solution.py:41
  (36 shorter events, 5.0 us)
Async XLA Ops:
  0.0 2.5 %collective-permute-start = (bf16[128,2304]{1,0:T(8,128)(2,1)}, bf16[128,2304]{1,0:T(8,128)(2,1)S(1)}, u32[]{:S(2)}, u32[]{:S(2)}) collective-permute-start(bf16[128,2304]{1,0:T(8,128)(2,1)} %param.5), channel_id=1, source_target_pairs={{0,1},{1,0},{2,3},{3,2},{4,5},{5,4},{6,7},{7,6},{8,9},{9,8},{10,11... | collective-permute-start | bytes 1769480 | tf_op jit(solution)/shard_map/ppermute | solution.py:372
  3.4 8.3 %collective-permute-start.1 = (bf16[64,1152]{1,0:T(8,128)(2,1)S(1)}, bf16[64,1152]{1,0:T(8,128)(2,1)S(1)}, u32[]{:S(2)}, u32[]{:S(2)}) collective-permute-start(bf16[64,1152]{1,0:T(8,128)(2,1)S(1)} %get-tuple-element.67), channel_id=1, source_target_pairs={{0,2},{2,4},{4,6},{6,0},{1,3},{3,5},{5,7},{7,1},{8,10},{10,12},{12... | collective-permute-start | bytes 442376 | tf_op jit(solution)/shard_map/ppermute | solution.py:368
  5.0 10.3 %collective-permute-start.2 = (bf16[64,1152]{1,0:T(8,128)(2,1)S(1)}, bf16[64,1152]{1,0:T(8,128)(2,1)S(1)}, u32[]{:S(2)}, u32[]{:S(2)}) collective-permute-start(bf16[64,1152]{1,0:T(8,128)(2,1)S(1)} %get-tuple-element.68), channel_id=1, source_target_pairs={{0,4},{2,6},{4,0},{6,2},{1,5},{3,7},{5,1},{7,3},{8,12},{10,14},{12... | collective-permute-start | bytes 442376 | tf_op jit(solution)/shard_map/ppermute | solution.py:368
  7.9 7.4 %collective-permute-start.3 = (bf16[64,1152]{1,0:T(8,128)(2,1)S(1)}, bf16[64,1152]{1,0:T(8,128)(2,1)S(1)}, u32[]{:S(2)}, u32[]{:S(2)}) collective-permute-start(bf16[64,1152]{1,0:T(8,128)(2,1)S(1)} %get-tuple-element.69), channel_id=1, source_target_pairs={{0,6},{2,0},{4,2},{6,4},{1,7},{3,1},{5,3},{7,5},{8,14},{10,8},{12,... | collective-permute-start | bytes 442376 | tf_op jit(solution)/shard_map/ppermute | solution.py:368
  11.6 5.4 %collective-permute-start.4 = (bf16[64,1152]{1,0:T(8,128)(2,1)S(1)}, bf16[64,1152]{1,0:T(8,128)(2,1)S(1)}, u32[]{:S(2)}, u32[]{:S(2)}) collective-permute-start(bf16[64,1152]{1,0:T(8,128)(2,1)S(1)} %get-tuple-element.100.refs_0_), channel_id=1, source_target_pairs={{0,1},{1,0},{2,3},{3,2},{4,5},{5,4},{6,7},{7,6},{8,9},{9,8},{10,11... | collective-permute-start | bytes 442376 | tf_op jit(solution)/shard_map/ppermute | solution.py:372
  15.3 1.6 %collective-permute-start.5 = (bf16[64,1152]{1,0:T(8,128)(2,1)S(1)}, bf16[64,1152]{1,0:T(8,128)(2,1)S(1)}, u32[]{:S(2)}, u32[]{:S(2)}) collective-permute-start(bf16[64,1152]{1,0:T(8,128)(2,1)S(1)} %collective-permute-done.1.refs_1_), channel_id=1, source_target_pairs={{0,1},{1,0},{2,3},{3,2},{4,5},{5,4},{6,7},{7,6},{8,9},{9,8},{10,11... | collective-permute-start | bytes 442376 | tf_op jit(solution)/shard_map/ppermute | solution.py:372
  15.3 1.6 %collective-permute-start.6 = (bf16[64,1152]{1,0:T(8,128)(2,1)S(1)}, bf16[64,1152]{1,0:T(8,128)(2,1)S(1)}, u32[]{:S(2)}, u32[]{:S(2)}) collective-permute-start(bf16[64,1152]{1,0:T(8,128)(2,1)S(1)} %collective-permute-done.2.refs_2_), channel_id=1, source_target_pairs={{0,1},{1,0},{2,3},{3,2},{4,5},{5,4},{6,7},{7,6},{8,9},{9,8},{10,11... | collective-permute-start | bytes 442376 | tf_op jit(solution)/shard_map/ppermute | solution.py:372
  15.8 1.4 %collective-permute-start.7 = (bf16[64,1152]{1,0:T(8,128)(2,1)S(1)}, bf16[64,1152]{1,0:T(8,128)(2,1)S(1)}, u32[]{:S(2)}, u32[]{:S(2)}) collective-permute-start(bf16[64,1152]{1,0:T(8,128)(2,1)S(1)} %collective-permute-done.3.refs_3_), channel_id=1, source_target_pairs={{0,1},{1,0},{2,3},{3,2},{4,5},{5,4},{6,7},{7,6},{8,9},{9,8},{10,11... | collective-permute-start | bytes 442376 | tf_op jit(solution)/shard_map/ppermute | solution.py:372
  16.9 4.7 %copy-start = (bf16[64,1152]{1,0:T(8,128)(2,1)}, bf16[64,1152]{1,0:T(8,128)(2,1)S(1)}, u32[]{:S(2)}) copy-start(bf16[64,1152]{1,0:T(8,128)(2,1)S(1)} %collective-permute-done.4.refs_4_) | copy-start | bytes 442372
  18.3 6.9 %collective-permute-start.8 = (bf16[512,128]{1,0:T(8,128)(2,1)S(1)}, bf16[512,128]{1,0:T(8,128)(2,1)S(1)}, u32[]{:S(2)}, u32[]{:S(2)}) collective-permute-start(bf16[512,128]{1,0:T(8,128)(2,1)S(1)} %bitcast.24), channel_id=1, source_target_pairs={{0,2},{2,4},{4,6},{6,0},{1,3},{3,5},{5,7},{7,1},{8,10},{10,12},{12... | collective-permute-start | bytes 393224 | tf_op jit(solution)/shard_map/ppermute | solution.py:368
  19.6 5.6 %collective-permute-start.9 = (bf16[512,128]{1,0:T(8,128)(2,1)S(1)}, bf16[512,128]{1,0:T(8,128)(2,1)S(1)}, u32[]{:S(2)}, u32[]{:S(2)}) collective-permute-start(bf16[512,128]{1,0:T(8,128)(2,1)S(1)} %bitcast.23), channel_id=1, source_target_pairs={{0,6},{2,0},{4,2},{6,4},{1,7},{3,1},{5,3},{7,5},{8,14},{10,8},{12,... | collective-permute-start | bytes 393224 | tf_op jit(solution)/shard_map/ppermute | solution.py:368
  21.8 0.9 %copy-start.1 = (bf16[64,1152]{1,0:T(8,128)(2,1)S(1)}, bf16[64,1152]{1,0:T(8,128)(2,1)}, u32[]{:S(2)}) copy-start(bf16[64,1152]{1,0:T(8,128)(2,1)} %copy-done) | copy-start | bytes 442372
  22.7 6.4 %copy-start.2 = (bf16[64,1152]{1,0:T(8,128)(2,1)S(1)}, bf16[64,1152]{1,0:T(8,128)(2,1)}, u32[]{:S(2)}) copy-start(bf16[64,1152]{1,0:T(8,128)(2,1)} %copy-done) | copy-start | bytes 442372
  22.7 6.4 %copy-start.3 = (bf16[1152,1024]{1,0:T(8,128)(2,1)S(1)}, bf16[1152,1024]{1,0:T(8,128)(2,1)}, u32[]{:S(2)}) copy-start(bf16[1152,1024]{1,0:T(8,128)(2,1)} %refs_8_.1) | copy-start | bytes 7077892
  25.8 8.9 %collective-permute-start.10 = (bf16[512,256]{1,0:T(8,128)(2,1)S(1)}, bf16[512,256]{1,0:T(8,128)(2,1)S(1)}, u32[]{:S(2)}, u32[]{:S(2)}) collective-permute-start(bf16[512,256]{1,0:T(8,128)(2,1)S(1)} %get-tuple-element.113), channel_id=1, source_target_pairs={{0,2},{2,4},{4,6},{6,0},{1,3},{3,5},{5,7},{7,1},{8,10},{10,12},{12... | collective-permute-start | bytes 786440 | tf_op jit(solution)/shard_map/ppermute | solution.py:368
  27.0 7.8 %collective-permute-start.11 = (bf16[512,256]{1,0:T(8,128)(2,1)S(1)}, bf16[512,256]{1,0:T(8,128)(2,1)S(1)}, u32[]{:S(2)}, u32[]{:S(2)}) collective-permute-start(bf16[512,256]{1,0:T(8,128)(2,1)S(1)} %get-tuple-element.114), channel_id=1, source_target_pairs={{0,6},{2,0},{4,2},{6,4},{1,7},{3,1},{5,3},{7,5},{8,14},{10,8},{12,... | collective-permute-start | bytes 786440 | tf_op jit(solution)/shard_map/ppermute | solution.py:368
  35.4 9.8 %collective-permute-start.15 = (bf16[512,256]{1,0:T(8,128)(2,1)S(1)}, bf16[512,256]{1,0:T(8,128)(2,1)S(1)}, u32[]{:S(2)}, u32[]{:S(2)}) collective-permute-start(bf16[512,256]{1,0:T(8,128)(2,1)S(1)} %keyval_rotate.1.own), channel_id=1, source_target_pairs={{0,32},{8,40},{16,48},{24,56},{32,64},{40,72},{48,80},{56,88},{64,... | collective-permute-start | bytes 786440 | tf_op jit(solution)/shard_map/ppermute | solution.py:340
  39.3 11.4 %collective-permute-start.12 = (bf16[512,256]{1,0:T(8,128)(2,1)S(1)}, bf16[512,256]{1,0:T(8,128)(2,1)S(1)}, u32[]{:S(2)}, u32[]{:S(2)}) collective-permute-start(bf16[512,256]{1,0:T(8,128)(2,1)S(1)} %bitcast.22), channel_id=1, source_target_pairs={{0,4},{2,6},{4,0},{6,2},{1,5},{3,7},{5,1},{7,3},{8,12},{10,14},{12... | collective-permute-start | bytes 786440 | tf_op jit(solution)/shard_map/ppermute | solution.py:368
  42.0 12.8 %collective-permute-start.13 = (bf16[512,256]{1,0:T(8,128)(2,1)S(1)}, bf16[512,256]{1,0:T(8,128)(2,1)S(1)}, u32[]{:S(2)}, u32[]{:S(2)}) collective-permute-start(bf16[512,256]{1,0:T(8,128)(2,1)S(1)} %bitcast.21), channel_id=1, source_target_pairs={{0,2},{2,4},{4,6},{6,0},{1,3},{3,5},{5,7},{7,1},{8,10},{10,12},{12... | collective-permute-start | bytes 786440 | tf_op jit(solution)/shard_map/ppermute | solution.py:368
  43.2 11.6 %collective-permute-start.14 = (bf16[512,256]{1,0:T(8,128)(2,1)S(1)}, bf16[512,256]{1,0:T(8,128)(2,1)S(1)}, u32[]{:S(2)}, u32[]{:S(2)}) collective-permute-start(bf16[512,256]{1,0:T(8,128)(2,1)S(1)} %bitcast.20), channel_id=1, source_target_pairs={{0,6},{2,0},{4,2},{6,4},{1,7},{3,1},{5,3},{7,5},{8,14},{10,8},{12,... | collective-permute-start | bytes 786440 | tf_op jit(solution)/shard_map/ppermute | solution.py:368
  45.2 9.6 %collective-permute-start.16 = (bf16[512,256]{1,0:T(8,128)(2,1)S(1)}, bf16[512,256]{1,0:T(8,128)(2,1)S(1)}, u32[]{:S(2)}, u32[]{:S(2)}) collective-permute-start(bf16[512,256]{1,0:T(8,128)(2,1)S(1)} %collective-permute-done.15.back1), channel_id=1, source_target_pairs={{0,32},{8,40},{16,48},{24,56},{32,64},{40,72},{48,80},{56,88},{64,... | collective-permute-start | bytes 786440 | tf_op jit(solution)/shard_map/ppermute | solution.py:340
  47.8 8.8 %collective-permute-start.18 = (bf16[512,256]{1,0:T(8,128)(2,1)S(1)}, bf16[512,256]{1,0:T(8,128)(2,1)S(1)}, u32[]{:S(2)}, u32[]{:S(2)}) collective-permute-start(bf16[512,256]{1,0:T(8,128)(2,1)S(1)} %collective-permute-done.15.back1), channel_id=1, source_target_pairs={{0,24},{8,16},{16,8},{24,0},{32,56},{40,48},{48,40},{56,32},{64,88... | collective-permute-start | bytes 786440 | tf_op jit(solution)/shard_map/ppermute | solution.py:340
  50.7 10.5 %collective-permute-start.19 = (bf16[512,256]{1,0:T(8,128)(2,1)S(1)}, bf16[512,256]{1,0:T(8,128)(2,1)S(1)}, u32[]{:S(2)}, u32[]{:S(2)}) collective-permute-start(bf16[512,256]{1,0:T(8,128)(2,1)S(1)} %broadcast_select_fusion), channel_id=1, source_target_pairs={{0,24},{8,16},{16,40},{24,32},{32,56},{40,48},{48,72},{56,64},{64,... | collective-permute-start | bytes 786440 | tf_op jit(solution)/shard_map/ppermute | solution.py:340
  55.5 6.5 %collective-permute-start.17 = (bf16[512,256]{1,0:T(8,128)(2,1)S(1)}, bf16[512,256]{1,0:T(8,128)(2,1)S(1)}, u32[]{:S(2)}, u32[]{:S(2)}) collective-permute-start(bf16[512,256]{1,0:T(8,128)(2,1)S(1)} %query_rotate.1.query), channel_id=1, source_target_pairs={{0,8},{8,0},{16,24},{24,16},{32,40},{40,32},{48,56},{56,48},{64,72... | collective-permute-start | bytes 786440 | tf_op jit(solution)/shard_map/ppermute | solution.py:340

commit v6 on v5

--- a/solution.py
+++ b/solution.py
@@ -214,10 +214,11 @@
                 lax.fori_loop(low, high, step, 0)
 
 
-def early_body(ids, query, own, back1, mirror1, back2, sums, *masked):
+def early_body(ids, query, own, back1, back2, sums, *masked):
     shard, _, _ = scalars(ids)
     shards = key_shards(shard)
-    held = (own, back1, mirror1, back2)
+    held = (own, back1, back2)
+    shards = (shards[0], shards[1], shards[3])
     blocks = [
         (shards[i], mask_values(ids, shards[i], held[i], masked[i]), held[i], masked[i])
         for i in range(len(held))
@@ -242,7 +243,7 @@
         (chosen, chosen_shard, True),
     )
     for place, (keyval, key_shard, seen) in enumerate(listed):
-        if place == 4:
+        if place == 3:
             common = used
         counted = (key_shard >= first) & seen
         count = jnp.where(counted, live_of(ids, jnp.maximum(key_shard, 0)), 0)
@@ -287,7 +288,7 @@
                 lax.fori_loop(0, (used - low + (width - 1)) // width, step, 0)
 
     count, pair_count = live_of(ids, shard), live_of(ids, partner)
-    attend(query, count, common, 2, sums)
+    attend(query, count, common, 4, sums)
     attend(pair, pair_count, 0, 4, pair_sums)
     same = lax.broadcasted_iota(jnp.int32, (BLOCK, HEAD), 0) == lax.broadcasted_iota(
         jnp.int32, (BLOCK, HEAD), 1
@@ -452,10 +453,10 @@
     masked = pltpu.VMEM((SHARD, 2 * HEAD), bf16)
     before = local(
         early_body,
-        (ids, query, own, back1, mirror1, back2),
+        (ids, query, own, back1, back2),
         sds(sums_shape, f32),
         "attend_early",
-        scratch=[masked] * 4,
+        scratch=[masked] * 3,
         flops=2**31,
     )
     pieces = local(

time: 80.9 us -> 81 us (level)
  waiting for transfers between devices: 11.6 us -> 14.1 us
  blocking collectives: 14.2 us -> 12.7 us
    ppermute x5, waiting for transfers between devices: 3.65 us -> 6.02 us  [along_seq(): return lax.ppermute(value, SEQ, pairs)]
    all_to_all x1, blocking collectives: 14.2 us -> 12.7 us  [on_device(): returned = lax.all_to_all(pieces, ('xl', 'row'), 0, 0)]
  transfers between devices with their start and end apart: 20 -> 20, of which waited for: 7 -> 7; matrix products, arithmetic and copies ran while one was open for 7% -> 7% of each run, Pallas kernels for 9% -> 8%
where the time goes in v6:
time: 81 us; the launch traced here: 80.2 us
  starting transfers between devices  32.1 us (40%)
  Pallas kernels  14.2 us (18%)
  waiting for transfers between devices  14.1 us (17%)
  blocking collectives  12.7 us (16%)
  local copies, waits for them, and re-layouts  4.92 us (6%)
  other arithmetic  1.97 us (2%)
    ppermute x10, starting transfers between devices, onward(): lax.ppermute(value, 'row', [(row, (row + step) % ROWS) for row in range(R...  18.5 us
    pallas_call x10, Pallas kernels, local(): pl.pallas_call(body, out_shape=out_shapes, in_specs=[SMEM] + [VMEM] * (le...  14.2 us
    ppermute x5, starting transfers between devices, along_seq(): return lax.ppermute(value, SEQ, pairs)  13 us
    all_to_all x1, blocking collectives, on_device(): returned = lax.all_to_all(pieces, ('xl', 'row'), 0, 0)  12.7 us
    ppermute x10, waiting for transfers between devices, onward(): lax.ppermute(value, 'row', [(row, (row + step) % ROWS) for row in range(R...  7.78 us
    ppermute x5, waiting for transfers between devices, along_seq(): return lax.ppermute(value, SEQ, pairs)  6.02 us
    unnamed x9, local copies, waits for them, and re-layouts  3.2 us
  transfers between devices with their start and end apart: 20, of which 7 were waited for; matrix products, arithmetic and copies ran while one was open for 7% of the time, Pallas kernels for 8%

profile of v6, /device:TPU:64, one launch (start us, length us, event | category | flops | bytes accessed | tf_op | source)
XLA Modules:
  0.0 80.2 jit_solution(5839120449866533719)
XLA Ops:
  0.0 0.7 reshape.43.gain
  1.5 1.0 %constant_dynamic-slice_fusion.own = bf16[64,2304]{1,0:T(8,128)(2,1)S(1)} fusion(bf16[128,2304]{1,0:T(8,128)(2,1)} %param.5, s32[]{:T(128)S(6)} %select_n.18), kind=kLoop, calls=%fused_computation.9 | loop fusion | bytes 589828 | tf_op jit(solution)/shard_map/dynamic_slice | solution.py:384
  2.5 0.9 %norm.1 = (bf16[64,1152]{1,0:T(8,128)(2,1)S(1)}, bf16[64,1152]{1,0:T(8,128)(2,1)S(1)}, bf16[64,1152]{1,0:T(8,128)(2,1)S(1)}, bf16[64,1152]{1,0:T(8,128)(2,1)S(1)}) custom-call(s32[35]{0:T(128)S(1)} %pad_add_fusion.ids, bf16[64,2304]{1,0:T(8,128)(2,1)S(1)} %constant_dynamic-slice_fusion.own, bf16[128,2304]{1,0:T(8,128)(2,1)S(1)} %collective-permute-done.received, ...), custom_call_target="tpu_custom_call" | custom-call | bytes 1048576 | tf_op jit(solution)/shard_map/norm/pallas_call | solution.py:41
  3.4 1.7 %collective-permute-start.1 = (bf16[64,1152]{1,0:T(8,128)(2,1)S(1)}, bf16[64,1152]{1,0:T(8,128)(2,1)S(1)}, u32[]{:S(2)}, u32[]{:S(2)}) collective-permute-start(bf16[64,1152]{1,0:T(8,128)(2,1)S(1)} %get-tuple-element.67), channel_id=1, source_target_pairs={{0,2},{2,4},{4,6},{6,0},{1,3},{3,5},{5,7},{7,1},{8,10},{10,12},{12... | collective-permute-start | bytes 442376 | tf_op jit(solution)/shard_map/ppermute | solution.py:369
  5.0 2.9 %collective-permute-start.2 = (bf16[64,1152]{1,0:T(8,128)(2,1)S(1)}, bf16[64,1152]{1,0:T(8,128)(2,1)S(1)}, u32[]{:S(2)}, u32[]{:S(2)}) collective-permute-start(bf16[64,1152]{1,0:T(8,128)(2,1)S(1)} %get-tuple-element.68), channel_id=1, source_target_pairs={{0,4},{2,6},{4,0},{6,2},{1,5},{3,7},{5,1},{7,3},{8,12},{10,14},{12... | collective-permute-start | bytes 442376 | tf_op jit(solution)/shard_map/ppermute | solution.py:369
  7.9 1.3 %collective-permute-start.3 = (bf16[64,1152]{1,0:T(8,128)(2,1)S(1)}, bf16[64,1152]{1,0:T(8,128)(2,1)S(1)}, u32[]{:S(2)}, u32[]{:S(2)}) collective-permute-start(bf16[64,1152]{1,0:T(8,128)(2,1)S(1)} %get-tuple-element.69), channel_id=1, source_target_pairs={{0,6},{2,0},{4,2},{6,4},{1,7},{3,1},{5,3},{7,5},{8,14},{10,8},{12,... | collective-permute-start | bytes 442376 | tf_op jit(solution)/shard_map/ppermute | solution.py:369
  9.3 2.3 %copy.6 = bf16[144,8,2,512]{3,1,2,0:T(8,128)(2,1)S(1)} copy(bf16[144,8,2,512]{3,2,1,0:T(2,128)(2,1)} %bitcast.25) | data formatting | bytes 4718592
  11.7 3.6 %collective-permute-done.2.refs_2_ = bf16[64,1152]{1,0:T(8,128)(2,1)S(1)} collective-permute-done((bf16[64,1152]{1,0:T(8,128)(2,1)S(1)}, bf16[64,1152]{1,0:T(8,128)(2,1)S(1)}, u32[]{:S(2)}, u32[]{:S(2)}) %collective-permute-start.2) | collective-permute-done | bytes 147488 | tf_op jit(solution)/shard_map/ppermute | solution.py:369
  15.9 1.0 %fusion = (f32[512,64]{1,0:T(8,128)S(1)}, f32[512,64]{1,0:T(8,128)S(1)}, f32[512,64]{1,0:T(8,128)S(1)}) fusion(f32[64]{0:T(128)S(1)} %multiply_power_fusion, f32[512]{0:T(512)S(1)} %add_convert_fusion), kind=kLoop, calls=%fused_computation.5 | loop fusion | flops 65536 | bytes 395520 | tf_op jit(solution)/shard_map/neg | solution.py:405
  17.2 1.1 %keyval_far.1 = (bf16[4,2,64,128]{3,2,1,0:T(8,128)(2,1)S(1)}, bf16[4,2,64,128]{3,2,1,0:T(8,128)(2,1)S(1)}) custom-call(s32[35]{0:T(128)S(1)} %pad_add_fusion.ids, bf16[64,1152]{1,0:T(8,128)(2,1)S(1)} %get-tuple-element.100.refs_0_, bf16[64,1152]{1,0:T(8,128)(2,1)S(1)} %collective-permute-done.1.refs_1_, bf16[64,1152]{1,0:T(8,128)(2,1)S(1)} %collective-permute-done.2.refs_2_, ...), custom_call_target="tpu_custom_call" | custom-call | flops 301989888 | bytes 1048576 | tf_op jit(solution)/shard_map/keyval_far/pallas_call | solution.py:41
  18.3 1.3 %collective-permute-start.8 = (bf16[512,128]{1,0:T(8,128)(2,1)S(1)}, bf16[512,128]{1,0:T(8,128)(2,1)S(1)}, u32[]{:S(2)}, u32[]{:S(2)}) collective-permute-start(bf16[512,128]{1,0:T(8,128)(2,1)S(1)} %bitcast.24), channel_id=1, source_target_pairs={{0,2},{2,4},{4,6},{6,0},{1,3},{3,5},{5,7},{7,1},{8,10},{10,12},{12... | collective-permute-start | bytes 393224 | tf_op jit(solution)/shard_map/ppermute | solution.py:369
  19.6 2.0 %collective-permute-start.9 = (bf16[512,128]{1,0:T(8,128)(2,1)S(1)}, bf16[512,128]{1,0:T(8,128)(2,1)S(1)}, u32[]{:S(2)}, u32[]{:S(2)}) collective-permute-start(bf16[512,128]{1,0:T(8,128)(2,1)S(1)} %bitcast.23), channel_id=1, source_target_pairs={{0,6},{2,0},{4,2},{6,4},{1,7},{3,1},{5,3},{7,5},{8,14},{10,8},{12,... | collective-permute-start | bytes 393224 | tf_op jit(solution)/shard_map/ppermute | solution.py:369
  21.8 0.9 %copy-done.1 = bf16[64,1152]{1,0:T(8,128)(2,1)S(1)} copy-done((bf16[64,1152]{1,0:T(8,128)(2,1)S(1)}, bf16[64,1152]{1,0:T(8,128)(2,1)}, u32[]{:S(2)}) %copy-start.1) | copy-done | bytes 147480
  22.8 1.8 %keyval_near.1 = (f32[4,2,64,256]{3,2,1,0:T(8,128)S(1)}, f32[4,2,64,256]{3,2,1,0:T(8,128)S(1)}, f32[4,2,64,256]{3,2,1,0:T(8,128)S(1)}) custom-call(s32[35]{0:T(128)S(1)} %pad_add_fusion.ids, bf16[64,1152]{1,0:T(8,128)(2,1)S(1)} %get-tuple-element.100.refs_0_, bf16[64,1152]{1,0:T(8,128)(2,1)S(1)} %collective-permute-done.1.refs_1_, ...), custom_call_target="tpu_custom_call" | custom-call | flops 905969664 | bytes 1048576 | tf_op jit(solution)/shard_map/keyval_near/pallas_call | solution.py:41
  25.8 1.1 %collective-permute-start.10 = (bf16[512,256]{1,0:T(8,128)(2,1)S(1)}, bf16[512,256]{1,0:T(8,128)(2,1)S(1)}, u32[]{:S(2)}, u32[]{:S(2)}) collective-permute-start(bf16[512,256]{1,0:T(8,128)(2,1)S(1)} %get-tuple-element.113), channel_id=1, source_target_pairs={{0,2},{2,4},{4,6},{6,0},{1,3},{3,5},{5,7},{7,1},{8,10},{10,12},{12... | collective-permute-start | bytes 786440 | tf_op jit(solution)/shard_map/ppermute | solution.py:369
  27.0 2.2 %collective-permute-start.11 = (bf16[512,256]{1,0:T(8,128)(2,1)S(1)}, bf16[512,256]{1,0:T(8,128)(2,1)S(1)}, u32[]{:S(2)}, u32[]{:S(2)}) collective-permute-start(bf16[512,256]{1,0:T(8,128)(2,1)S(1)} %get-tuple-element.114), channel_id=1, source_target_pairs={{0,6},{2,0},{4,2},{6,4},{1,7},{3,1},{5,3},{7,5},{8,14},{10,8},{12,... | collective-permute-start | bytes 786440 | tf_op jit(solution)/shard_map/ppermute | solution.py:369
  29.2 2.1 %query_partial.1 = (bf16[4,2,64,256]{3,2,1,0:T(8,128)(2,1)S(1)}, bf16[4,2,64,256]{3,2,1,0:T(8,128)(2,1)S(1)}, bf16[4,2,64,256]{3,2,1,0:T(8,128)(2,1)S(1)}, bf16[4,2,64,256]{3,2,1,0:T(8,128)(2,1)S(1)}) custom-call(s32[35]{0:T(128)S(1)} %pad_add_fusion.ids, bf16[64,1152]{1,0:T(8,128)(2,1)S(1)} %get-tuple-element.100.refs_0_, ...), custom_call_target="tpu_custom_call" | custom-call | flops 1207959552 | bytes 1048576 | tf_op jit(solution)/shard_map/query_partial/pallas_call | solution.py:41
  31.3 3.4 %collective-permute-done.10.refs_1_ = bf16[512,256]{1,0:T(8,128)(2,1)S(1)} collective-permute-done((bf16[512,256]{1,0:T(8,128)(2,1)S(1)}, bf16[512,256]{1,0:T(8,128)(2,1)S(1)}, u32[]{:S(2)}, u32[]{:S(2)}) %collective-permute-start.10) | collective-permute-done | bytes 262176 | tf_op jit(solution)/shard_map/ppermute | solution.py:369
  35.4 3.8 %collective-permute-start.15 = (bf16[512,256]{1,0:T(8,128)(2,1)S(1)}, bf16[512,256]{1,0:T(8,128)(2,1)S(1)}, u32[]{:S(2)}, u32[]{:S(2)}) collective-permute-start(bf16[512,256]{1,0:T(8,128)(2,1)S(1)} %keyval_rotate.1.own), channel_id=1, source_target_pairs={{0,32},{8,40},{16,48},{24,56},{32,64},{40,72},{48,80},{56,88},{64,... | collective-permute-start | bytes 786440 | tf_op jit(solution)/shard_map/ppermute | solution.py:341
  39.3 2.7 %collective-permute-start.12 = (bf16[512,256]{1,0:T(8,128)(2,1)S(1)}, bf16[512,256]{1,0:T(8,128)(2,1)S(1)}, u32[]{:S(2)}, u32[]{:S(2)}) collective-permute-start(bf16[512,256]{1,0:T(8,128)(2,1)S(1)} %bitcast.22), channel_id=1, source_target_pairs={{0,4},{2,6},{4,0},{6,2},{1,5},{3,7},{5,1},{7,3},{8,12},{10,14},{12... | collective-permute-start | bytes 786440 | tf_op jit(solution)/shard_map/ppermute | solution.py:369
  42.0 1.2 %collective-permute-start.13 = (bf16[512,256]{1,0:T(8,128)(2,1)S(1)}, bf16[512,256]{1,0:T(8,128)(2,1)S(1)}, u32[]{:S(2)}, u32[]{:S(2)}) collective-permute-start(bf16[512,256]{1,0:T(8,128)(2,1)S(1)} %bitcast.21), channel_id=1, source_target_pairs={{0,2},{2,4},{4,6},{6,0},{1,3},{3,5},{5,7},{7,1},{8,10},{10,12},{12... | collective-permute-start | bytes 786440 | tf_op jit(solution)/shard_map/ppermute | solution.py:369
  43.2 2.0 %collective-permute-start.14 = (bf16[512,256]{1,0:T(8,128)(2,1)S(1)}, bf16[512,256]{1,0:T(8,128)(2,1)S(1)}, u32[]{:S(2)}, u32[]{:S(2)}) collective-permute-start(bf16[512,256]{1,0:T(8,128)(2,1)S(1)} %bitcast.20), channel_id=1, source_target_pairs={{0,6},{2,0},{4,2},{6,4},{1,7},{3,1},{5,3},{7,5},{8,14},{10,8},{12,... | collective-permute-start | bytes 786440 | tf_op jit(solution)/shard_map/ppermute | solution.py:369
  45.2 2.6 %collective-permute-start.16 = (bf16[512,256]{1,0:T(8,128)(2,1)S(1)}, bf16[512,256]{1,0:T(8,128)(2,1)S(1)}, u32[]{:S(2)}, u32[]{:S(2)}) collective-permute-start(bf16[512,256]{1,0:T(8,128)(2,1)S(1)} %collective-permute-done.15.back1), channel_id=1, source_target_pairs={{0,32},{8,40},{16,48},{24,56},{32,64},{40,72},{48,80},{56,88},{64,... | collective-permute-start | bytes 786440 | tf_op jit(solution)/shard_map/ppermute | solution.py:341
  47.9 4.7 %collective-permute-start.19 = (bf16[512,256]{1,0:T(8,128)(2,1)S(1)}, bf16[512,256]{1,0:T(8,128)(2,1)S(1)}, u32[]{:S(2)}, u32[]{:S(2)}) collective-permute-start(bf16[512,256]{1,0:T(8,128)(2,1)S(1)} %broadcast_select_fusion), channel_id=1, source_target_pairs={{0,24},{8,16},{16,40},{24,32},{32,56},{40,48},{48,72},{56,64},{64,... | collective-permute-start | bytes 786440 | tf_op jit(solution)/shard_map/ppermute | solution.py:341
  53.4 0.8 query_rotate.1.query
  54.2 1.6 %collective-permute-start.17 = (bf16[512,256]{1,0:T(8,128)(2,1)S(1)}, bf16[512,256]{1,0:T(8,128)(2,1)S(1)}, u32[]{:S(2)}, u32[]{:S(2)}) collective-permute-start(bf16[512,256]{1,0:T(8,128)(2,1)S(1)} %query_rotate.1.query), channel_id=1, source_target_pairs={{0,8},{8,0},{16,24},{24,16},{32,40},{40,32},{48,56},{56,48},{64,72... | collective-permute-start | bytes 786440 | tf_op jit(solution)/shard_map/ppermute | solution.py:341
  55.8 2.0 %attend_early.1.before = f32[2,512,256]{2,1,0:T(8,128)S(1)} custom-call(s32[35]{0:T(128)S(1)} %pad_add_fusion.ids, bf16[512,256]{1,0:T(8,128)(2,1)S(1)} %query_rotate.1.query, bf16[512,256]{1,0:T(8,128)(2,1)S(1)} %keyval_rotate.1.own, bf16[512,256]{1,0:T(8,128)(2,1)S(1)} %collective-permute-done.15.back1, bf16[512,256]{1,0:T(8,128)(2,1)S(1)} %collective-permute-done.16.back2), custom_call_target="tpu_custom_call" | custom-call | flops 2147483648 | bytes 1048576 | tf_op jit(solution)/shard_map/attend_early/pallas_call | solution.py:41
  57.8 2.4 %collective-permute-done.19.chosen = bf16[512,256]{1,0:T(8,128)(2,1)S(1)} collective-permute-done((bf16[512,256]{1,0:T(8,128)(2,1)S(1)}, bf16[512,256]{1,0:T(8,128)(2,1)S(1)}, u32[]{:S(2)}, u32[]{:S(2)}) %collective-permute-start.19) | collective-permute-done | bytes 262176 | tf_op jit(solution)/shard_map/ppermute | solution.py:341
  60.3 3.0 %collective-permute-done.18.mirror1 = bf16[512,256]{1,0:T(8,128)(2,1)S(1)} collective-permute-done((bf16[512,256]{1,0:T(8,128)(2,1)S(1)}, bf16[512,256]{1,0:T(8,128)(2,1)S(1)}, u32[]{:S(2)}, u32[]{:S(2)}) %collective-permute-start.18) | collective-permute-done | bytes 262176 | tf_op jit(solution)/shard_map/ppermute | solution.py:341
  63.3 2.7 %attend_late.1 = bf16[8,144,256]{2,1,0:T(8,128)(2,1)S(1)} custom-call(s32[35]{0:T(128)S(1)} %pad_add_fusion.ids, bf16[512,256]{1,0:T(8,128)(2,1)S(1)} %query_rotate.1.query, bf16[512,256]{1,0:T(8,128)(2,1)S(1)} %collective-permute-done.17.pair, bf16[512,256]{1,0:T(8,128)(2,1)S(1)} %keyval_rotate.1.own, bf16[512,256]{1,0:T(8,128)(2,1)S(1)} %collective-permute-done.15.back1, ...), custom_call_target="tpu_custom_call" | custom-call | flops 2147483648 | bytes 1048576 | tf_op jit(solution)/shard_map/attend_late/pallas_call | solution.py:41
  66.0 12.7 %all_to_all.5.pieces = bf16[8,144,256]{2,1,0:T(8,128)(2,1)S(1)} all-to-all(bf16[8,144,256]{2,1,0:T(8,128)(2,1)S(1)} %attend_late.1), channel_id=1, replica_groups=mesh['z'=8,'xh'=2,'xl'=2,'row'=4,'col'=2] {'xl','row'}, dimensions={0} | all-to-all | bytes 1179648 | tf_op jit(solution)/shard_map/all_to_all | solution.py:476
  78.7 1.5 %finish.1 = bf16[128,1024]{1,0:T(8,128)(2,1)} custom-call(s32[35]{0:T(128)S(1)} %pad_add_fusion.ids, bf16[8,144,256]{2,1,0:T(8,128)(2,1)S(1)} %all_to_all.5.pieces), custom_call_target="tpu_custom_call" | custom-call | bytes 1048576 | tf_op jit(solution)/shard_map/finish/pallas_call | solution.py:41
  (36 shorter events, 4.8 us)
Async XLA Ops:
  0.0 2.5 %collective-permute-start = (bf16[128,2304]{1,0:T(8,128)(2,1)}, bf16[128,2304]{1,0:T(8,128)(2,1)S(1)}, u32[]{:S(2)}, u32[]{:S(2)}) collective-permute-start(bf16[128,2304]{1,0:T(8,128)(2,1)} %param.5), channel_id=1, source_target_pairs={{0,1},{1,0},{2,3},{3,2},{4,5},{5,4},{6,7},{7,6},{8,9},{9,8},{10,11... | collective-permute-start | bytes 1769480 | tf_op jit(solution)/shard_map/ppermute | solution.py:373
  3.4 8.3 %collective-permute-start.1 = (bf16[64,1152]{1,0:T(8,128)(2,1)S(1)}, bf16[64,1152]{1,0:T(8,128)(2,1)S(1)}, u32[]{:S(2)}, u32[]{:S(2)}) collective-permute-start(bf16[64,1152]{1,0:T(8,128)(2,1)S(1)} %get-tuple-element.67), channel_id=1, source_target_pairs={{0,2},{2,4},{4,6},{6,0},{1,3},{3,5},{5,7},{7,1},{8,10},{10,12},{12... | collective-permute-start | bytes 442376 | tf_op jit(solution)/shard_map/ppermute | solution.py:369
  5.0 10.3 %collective-permute-start.2 = (bf16[64,1152]{1,0:T(8,128)(2,1)S(1)}, bf16[64,1152]{1,0:T(8,128)(2,1)S(1)}, u32[]{:S(2)}, u32[]{:S(2)}) collective-permute-start(bf16[64,1152]{1,0:T(8,128)(2,1)S(1)} %get-tuple-element.68), channel_id=1, source_target_pairs={{0,4},{2,6},{4,0},{6,2},{1,5},{3,7},{5,1},{7,3},{8,12},{10,14},{12... | collective-permute-start | bytes 442376 | tf_op jit(solution)/shard_map/ppermute | solution.py:369
  7.9 7.4 %collective-permute-start.3 = (bf16[64,1152]{1,0:T(8,128)(2,1)S(1)}, bf16[64,1152]{1,0:T(8,128)(2,1)S(1)}, u32[]{:S(2)}, u32[]{:S(2)}) collective-permute-start(bf16[64,1152]{1,0:T(8,128)(2,1)S(1)} %get-tuple-element.69), channel_id=1, source_target_pairs={{0,6},{2,0},{4,2},{6,4},{1,7},{3,1},{5,3},{7,5},{8,14},{10,8},{12,... | collective-permute-start | bytes 442376 | tf_op jit(solution)/shard_map/ppermute | solution.py:369
  11.6 5.4 %collective-permute-start.4 = (bf16[64,1152]{1,0:T(8,128)(2,1)S(1)}, bf16[64,1152]{1,0:T(8,128)(2,1)S(1)}, u32[]{:S(2)}, u32[]{:S(2)}) collective-permute-start(bf16[64,1152]{1,0:T(8,128)(2,1)S(1)} %get-tuple-element.100.refs_0_), channel_id=1, source_target_pairs={{0,1},{1,0},{2,3},{3,2},{4,5},{5,4},{6,7},{7,6},{8,9},{9,8},{10,11... | collective-permute-start | bytes 442376 | tf_op jit(solution)/shard_map/ppermute | solution.py:373
  15.3 1.6 %collective-permute-start.5 = (bf16[64,1152]{1,0:T(8,128)(2,1)S(1)}, bf16[64,1152]{1,0:T(8,128)(2,1)S(1)}, u32[]{:S(2)}, u32[]{:S(2)}) collective-permute-start(bf16[64,1152]{1,0:T(8,128)(2,1)S(1)} %collective-permute-done.1.refs_1_), channel_id=1, source_target_pairs={{0,1},{1,0},{2,3},{3,2},{4,5},{5,4},{6,7},{7,6},{8,9},{9,8},{10,11... | collective-permute-start | bytes 442376 | tf_op jit(solution)/shard_map/ppermute | solution.py:373
  15.3 1.6 %collective-permute-start.6 = (bf16[64,1152]{1,0:T(8,128)(2,1)S(1)}, bf16[64,1152]{1,0:T(8,128)(2,1)S(1)}, u32[]{:S(2)}, u32[]{:S(2)}) collective-permute-start(bf16[64,1152]{1,0:T(8,128)(2,1)S(1)} %collective-permute-done.2.refs_2_), channel_id=1, source_target_pairs={{0,1},{1,0},{2,3},{3,2},{4,5},{5,4},{6,7},{7,6},{8,9},{9,8},{10,11... | collective-permute-start | bytes 442376 | tf_op jit(solution)/shard_map/ppermute | solution.py:373
  15.8 1.4 %collective-permute-start.7 = (bf16[64,1152]{1,0:T(8,128)(2,1)S(1)}, bf16[64,1152]{1,0:T(8,128)(2,1)S(1)}, u32[]{:S(2)}, u32[]{:S(2)}) collective-permute-start(bf16[64,1152]{1,0:T(8,128)(2,1)S(1)} %collective-permute-done.3.refs_3_), channel_id=1, source_target_pairs={{0,1},{1,0},{2,3},{3,2},{4,5},{5,4},{6,7},{7,6},{8,9},{9,8},{10,11... | collective-permute-start | bytes 442376 | tf_op jit(solution)/shard_map/ppermute | solution.py:373
  16.9 4.7 %copy-start = (bf16[64,1152]{1,0:T(8,128)(2,1)}, bf16[64,1152]{1,0:T(8,128)(2,1)S(1)}, u32[]{:S(2)}) copy-start(bf16[64,1152]{1,0:T(8,128)(2,1)S(1)} %collective-permute-done.4.refs_4_) | copy-start | bytes 442372
  18.3 6.9 %collective-permute-start.8 = (bf16[512,128]{1,0:T(8,128)(2,1)S(1)}, bf16[512,128]{1,0:T(8,128)(2,1)S(1)}, u32[]{:S(2)}, u32[]{:S(2)}) collective-permute-start(bf16[512,128]{1,0:T(8,128)(2,1)S(1)} %bitcast.24), channel_id=1, source_target_pairs={{0,2},{2,4},{4,6},{6,0},{1,3},{3,5},{5,7},{7,1},{8,10},{10,12},{12... | collective-permute-start | bytes 393224 | tf_op jit(solution)/shard_map/ppermute | solution.py:369
  19.6 5.6 %collective-permute-start.9 = (bf16[512,128]{1,0:T(8,128)(2,1)S(1)}, bf16[512,128]{1,0:T(8,128)(2,1)S(1)}, u32[]{:S(2)}, u32[]{:S(2)}) collective-permute-start(bf16[512,128]{1,0:T(8,128)(2,1)S(1)} %bitcast.23), channel_id=1, source_target_pairs={{0,6},{2,0},{4,2},{6,4},{1,7},{3,1},{5,3},{7,5},{8,14},{10,8},{12,... | collective-permute-start | bytes 393224 | tf_op jit(solution)/shard_map/ppermute | solution.py:369
  21.8 0.9 %copy-start.1 = (bf16[64,1152]{1,0:T(8,128)(2,1)S(1)}, bf16[64,1152]{1,0:T(8,128)(2,1)}, u32[]{:S(2)}) copy-start(bf16[64,1152]{1,0:T(8,128)(2,1)} %copy-done) | copy-start | bytes 442372
  22.7 6.4 %copy-start.2 = (bf16[64,1152]{1,0:T(8,128)(2,1)S(1)}, bf16[64,1152]{1,0:T(8,128)(2,1)}, u32[]{:S(2)}) copy-start(bf16[64,1152]{1,0:T(8,128)(2,1)} %copy-done) | copy-start | bytes 442372
  22.7 6.4 %copy-start.3 = (bf16[1152,1024]{1,0:T(8,128)(2,1)S(1)}, bf16[1152,1024]{1,0:T(8,128)(2,1)}, u32[]{:S(2)}) copy-start(bf16[1152,1024]{1,0:T(8,128)(2,1)} %refs_8_.1) | copy-start | bytes 7077892
  25.8 8.9 %collective-permute-start.10 = (bf16[512,256]{1,0:T(8,128)(2,1)S(1)}, bf16[512,256]{1,0:T(8,128)(2,1)S(1)}, u32[]{:S(2)}, u32[]{:S(2)}) collective-permute-start(bf16[512,256]{1,0:T(8,128)(2,1)S(1)} %get-tuple-element.113), channel_id=1, source_target_pairs={{0,2},{2,4},{4,6},{6,0},{1,3},{3,5},{5,7},{7,1},{8,10},{10,12},{12... | collective-permute-start | bytes 786440 | tf_op jit(solution)/shard_map/ppermute | solution.py:369
  27.0 7.8 %collective-permute-start.11 = (bf16[512,256]{1,0:T(8,128)(2,1)S(1)}, bf16[512,256]{1,0:T(8,128)(2,1)S(1)}, u32[]{:S(2)}, u32[]{:S(2)}) collective-permute-start(bf16[512,256]{1,0:T(8,128)(2,1)S(1)} %get-tuple-element.114), channel_id=1, source_target_pairs={{0,6},{2,0},{4,2},{6,4},{1,7},{3,1},{5,3},{7,5},{8,14},{10,8},{12,... | collective-permute-start | bytes 786440 | tf_op jit(solution)/shard_map/ppermute | solution.py:369
  35.4 9.8 %collective-permute-start.15 = (bf16[512,256]{1,0:T(8,128)(2,1)S(1)}, bf16[512,256]{1,0:T(8,128)(2,1)S(1)}, u32[]{:S(2)}, u32[]{:S(2)}) collective-permute-start(bf16[512,256]{1,0:T(8,128)(2,1)S(1)} %keyval_rotate.1.own), channel_id=1, source_target_pairs={{0,32},{8,40},{16,48},{24,56},{32,64},{40,72},{48,80},{56,88},{64,... | collective-permute-start | bytes 786440 | tf_op jit(solution)/shard_map/ppermute | solution.py:341
  39.3 13.3 %collective-permute-start.12 = (bf16[512,256]{1,0:T(8,128)(2,1)S(1)}, bf16[512,256]{1,0:T(8,128)(2,1)S(1)}, u32[]{:S(2)}, u32[]{:S(2)}) collective-permute-start(bf16[512,256]{1,0:T(8,128)(2,1)S(1)} %bitcast.22), channel_id=1, source_target_pairs={{0,4},{2,6},{4,0},{6,2},{1,5},{3,7},{5,1},{7,3},{8,12},{10,14},{12... | collective-permute-start | bytes 786440 | tf_op jit(solution)/shard_map/ppermute | solution.py:369
  42.0 10.9 %collective-permute-start.13 = (bf16[512,256]{1,0:T(8,128)(2,1)S(1)}, bf16[512,256]{1,0:T(8,128)(2,1)S(1)}, u32[]{:S(2)}, u32[]{:S(2)}) collective-permute-start(bf16[512,256]{1,0:T(8,128)(2,1)S(1)} %bitcast.21), channel_id=1, source_target_pairs={{0,2},{2,4},{4,6},{6,0},{1,3},{3,5},{5,7},{7,1},{8,10},{10,12},{12... | collective-permute-start | bytes 786440 | tf_op jit(solution)/shard_map/ppermute | solution.py:369
  43.2 9.7 %collective-permute-start.14 = (bf16[512,256]{1,0:T(8,128)(2,1)S(1)}, bf16[512,256]{1,0:T(8,128)(2,1)S(1)}, u32[]{:S(2)}, u32[]{:S(2)}) collective-permute-start(bf16[512,256]{1,0:T(8,128)(2,1)S(1)} %bitcast.20), channel_id=1, source_target_pairs={{0,6},{2,0},{4,2},{6,4},{1,7},{3,1},{5,3},{7,5},{8,14},{10,8},{12,... | collective-permute-start | bytes 786440 | tf_op jit(solution)/shard_map/ppermute | solution.py:369
  45.2 8.3 %collective-permute-start.16 = (bf16[512,256]{1,0:T(8,128)(2,1)S(1)}, bf16[512,256]{1,0:T(8,128)(2,1)S(1)}, u32[]{:S(2)}, u32[]{:S(2)}) collective-permute-start(bf16[512,256]{1,0:T(8,128)(2,1)S(1)} %collective-permute-done.15.back1), channel_id=1, source_target_pairs={{0,32},{8,40},{16,48},{24,56},{32,64},{40,72},{48,80},{56,88},{64,... | collective-permute-start | bytes 786440 | tf_op jit(solution)/shard_map/ppermute | solution.py:341
  47.9 12.4 %collective-permute-start.19 = (bf16[512,256]{1,0:T(8,128)(2,1)S(1)}, bf16[512,256]{1,0:T(8,128)(2,1)S(1)}, u32[]{:S(2)}, u32[]{:S(2)}) collective-permute-start(bf16[512,256]{1,0:T(8,128)(2,1)S(1)} %broadcast_select_fusion), channel_id=1, source_target_pairs={{0,24},{8,16},{16,40},{24,32},{32,56},{40,48},{48,72},{56,64},{64,... | collective-permute-start | bytes 786440 | tf_op jit(solution)/shard_map/ppermute | solution.py:341
  52.6 10.7 %collective-permute-start.18 = (bf16[512,256]{1,0:T(8,128)(2,1)S(1)}, bf16[512,256]{1,0:T(8,128)(2,1)S(1)}, u32[]{:S(2)}, u32[]{:S(2)}) collective-permute-start(bf16[512,256]{1,0:T(8,128)(2,1)S(1)} %collective-permute-done.15.back1), channel_id=1, source_target_pairs={{0,24},{8,16},{16,8},{24,0},{32,56},{40,48},{48,40},{56,32},{64,88... | collective-permute-start | bytes 786440 | tf_op jit(solution)/shard_map/ppermute | solution.py:341
  54.2 9.0 %collective-permute-start.17 = (bf16[512,256]{1,0:T(8,128)(2,1)S(1)}, bf16[512,256]{1,0:T(8,128)(2,1)S(1)}, u32[]{:S(2)}, u32[]{:S(2)}) collective-permute-start(bf16[512,256]{1,0:T(8,128)(2,1)S(1)} %query_rotate.1.query), channel_id=1, source_target_pairs={{0,8},{8,0},{16,24},{24,16},{32,40},{40,32},{48,56},{56,48},{64,72... | collective-permute-start | bytes 786440 | tf_op jit(solution)/shard_map/ppermute | solution.py:341

commit v7 on v6

--- a/solution.py
+++ b/solution.py
@@ -341,9 +341,11 @@
     return lax.ppermute(value, SEQ, pairs)
 
 
-def hop(value):
+def hop(value, places=(0, 1, 2, 3)):
     planes = SEQ_SHARDS // PLANE
-    return along_seq(value, lambda z, x: (z + 1, x) if z % planes != planes - 1 else None)
+    return along_seq(
+        value, lambda z, x: (z + 1, x) if x in places and z % planes != planes - 1 else None
+    )
 
 
 def mirrored(value):
@@ -440,8 +442,12 @@
 
     back1 = hop(own)
     back2 = hop(back1)
-    mirror1 = mirrored(back1)
-    chosen = turned(jnp.where(lax.axis_index("xh") == 0, own, back1))
+    across = turned(back1)
+    opposite = mirrored(own)
+    lower = lax.axis_index("xh") == 0
+    raised = hop(opposite, (0, 1))
+    mirror1 = jnp.where(lower, raised, across)
+    chosen = jnp.where(lower, across, opposite)
 
     query_sums, back2 = lax.optimization_barrier((query_sums, back2))
     query = local(

time: 81 us -> 82.2 us (1.015)
  other arithmetic: 1.97 us -> 2.94 us
    ppermute x10, waiting for transfers between devices: 7.78 us -> 8.89 us  [onward(): lax.ppermute(value, 'row', [(row, (row + step) % ROWS) for row in range(R...]
    select_n x1, other arithmetic: 0.03 us -> 1 us  [on_device(): chosen = jnp.where(lower, across, opposite)]
    ppermute x5 -> x6, waiting for transfers between devices: 6.02 us -> 5.09 us  [along_seq(): return lax.ppermute(value, SEQ, pairs)]
    ppermute x5 -> x6, starting transfers between devices: 13 us -> 13.2 us  [along_seq(): return lax.ppermute(value, SEQ, pairs)]
  transfers between devices with their start and end apart: 20 -> 21, of which waited for: 7 -> 9; matrix products, arithmetic and copies ran while one was open for 7% -> 9% of each run, Pallas kernels for 8% -> 8%
where the time goes in v7:
time: 82.2 us; the launch traced here: 81.1 us
  starting transfers between devices  32.2 us (39%)
  waiting for transfers between devices  14.2 us (17%)
  Pallas kernels  14.2 us (17%)
  blocking collectives  12.3 us (15%)
  local copies, waits for them, and re-layouts  4.92 us (6%)
  other arithmetic  2.94 us (4%)
    ppermute x10, starting transfers between devices, onward(): lax.ppermute(value, 'row', [(row, (row + step) % ROWS) for row in range(R...  18.4 us
    pallas_call x10, Pallas kernels, local(): pl.pallas_call(body, out_shape=out_shapes, in_specs=[SMEM] + [VMEM] * (le...  14.2 us
    ppermute x6, starting transfers between devices, along_seq(): return lax.ppermute(value, SEQ, pairs)  13.2 us
    all_to_all x1, blocking collectives, on_device(): returned = lax.all_to_all(pieces, ('xl', 'row'), 0, 0)  12.3 us
    ppermute x10, waiting for transfers between devices, onward(): lax.ppermute(value, 'row', [(row, (row + step) % ROWS) for row in range(R...  8.89 us
    ppermute x6, waiting for transfers between devices, along_seq(): return lax.ppermute(value, SEQ, pairs)  5.09 us
    unnamed x9, local copies, waits for them, and re-layouts  3.2 us
  transfers between devices with their start and end apart: 21, of which 9 were waited for; matrix products, arithmetic and copies ran while one was open for 9% of the time, Pallas kernels for 8%

profile of v7, /device:TPU:64, one launch (start us, length us, event | category | flops | bytes accessed | tf_op | source)
XLA Modules:
  0.0 81.1 jit_solution(9612046864000172917)
XLA Ops:
  1.5 1.0 %constant_dynamic-slice_fusion.own = bf16[64,2304]{1,0:T(8,128)(2,1)S(1)} fusion(bf16[128,2304]{1,0:T(8,128)(2,1)} %param.5, s32[]{:T(128)S(6)} %select_n.22), kind=kLoop, calls=%fused_computation.10 | loop fusion | bytes 589828 | tf_op jit(solution)/shard_map/dynamic_slice | solution.py:386
  2.5 0.9 %norm.1 = (bf16[64,1152]{1,0:T(8,128)(2,1)S(1)}, bf16[64,1152]{1,0:T(8,128)(2,1)S(1)}, bf16[64,1152]{1,0:T(8,128)(2,1)S(1)}, bf16[64,1152]{1,0:T(8,128)(2,1)S(1)}) custom-call(s32[35]{0:T(128)S(1)} %pad_add_fusion.ids, bf16[64,2304]{1,0:T(8,128)(2,1)S(1)} %constant_dynamic-slice_fusion.own, bf16[128,2304]{1,0:T(8,128)(2,1)S(1)} %collective-permute-done.received, ...), custom_call_target="tpu_custom_call" | custom-call | bytes 1048576 | tf_op jit(solution)/shard_map/norm/pallas_call | solution.py:41
  3.4 1.7 %collective-permute-start.1 = (bf16[64,1152]{1,0:T(8,128)(2,1)S(1)}, bf16[64,1152]{1,0:T(8,128)(2,1)S(1)}, u32[]{:S(2)}, u32[]{:S(2)}) collective-permute-start(bf16[64,1152]{1,0:T(8,128)(2,1)S(1)} %get-tuple-element.67), channel_id=1, source_target_pairs={{0,2},{2,4},{4,6},{6,0},{1,3},{3,5},{5,7},{7,1},{8,10},{10,12},{12... | collective-permute-start | bytes 442376 | tf_op jit(solution)/shard_map/ppermute | solution.py:371
  5.0 2.9 %collective-permute-start.2 = (bf16[64,1152]{1,0:T(8,128)(2,1)S(1)}, bf16[64,1152]{1,0:T(8,128)(2,1)S(1)}, u32[]{:S(2)}, u32[]{:S(2)}) collective-permute-start(bf16[64,1152]{1,0:T(8,128)(2,1)S(1)} %get-tuple-element.68), channel_id=1, source_target_pairs={{0,4},{2,6},{4,0},{6,2},{1,5},{3,7},{5,1},{7,3},{8,12},{10,14},{12... | collective-permute-start | bytes 442376 | tf_op jit(solution)/shard_map/ppermute | solution.py:371
  7.9 1.3 %collective-permute-start.3 = (bf16[64,1152]{1,0:T(8,128)(2,1)S(1)}, bf16[64,1152]{1,0:T(8,128)(2,1)S(1)}, u32[]{:S(2)}, u32[]{:S(2)}) collective-permute-start(bf16[64,1152]{1,0:T(8,128)(2,1)S(1)} %get-tuple-element.69), channel_id=1, source_target_pairs={{0,6},{2,0},{4,2},{6,4},{1,7},{3,1},{5,3},{7,5},{8,14},{10,8},{12,... | collective-permute-start | bytes 442376 | tf_op jit(solution)/shard_map/ppermute | solution.py:371
  9.3 2.3 %copy.6 = bf16[144,8,2,512]{3,1,2,0:T(8,128)(2,1)S(1)} copy(bf16[144,8,2,512]{3,2,1,0:T(2,128)(2,1)} %bitcast.25) | data formatting | bytes 4718592
  11.7 3.6 %collective-permute-done.2.refs_2_ = bf16[64,1152]{1,0:T(8,128)(2,1)S(1)} collective-permute-done((bf16[64,1152]{1,0:T(8,128)(2,1)S(1)}, bf16[64,1152]{1,0:T(8,128)(2,1)S(1)}, u32[]{:S(2)}, u32[]{:S(2)}) %collective-permute-start.2) | collective-permute-done | bytes 147488 | tf_op jit(solution)/shard_map/ppermute | solution.py:371
  15.9 1.0 %fusion = (f32[512,64]{1,0:T(8,128)S(1)}, f32[512,64]{1,0:T(8,128)S(1)}, f32[512,64]{1,0:T(8,128)S(1)}) fusion(f32[64]{0:T(128)S(1)} %multiply_power_fusion, f32[512]{0:T(512)S(1)} %add_convert_fusion), kind=kLoop, calls=%fused_computation.6 | loop fusion | flops 65536 | bytes 395520 | tf_op jit(solution)/shard_map/neg | solution.py:407
  17.2 1.1 %keyval_far.1 = (bf16[4,2,64,128]{3,2,1,0:T(8,128)(2,1)S(1)}, bf16[4,2,64,128]{3,2,1,0:T(8,128)(2,1)S(1)}) custom-call(s32[35]{0:T(128)S(1)} %pad_add_fusion.ids, bf16[64,1152]{1,0:T(8,128)(2,1)S(1)} %get-tuple-element.100.refs_0_, bf16[64,1152]{1,0:T(8,128)(2,1)S(1)} %collective-permute-done.1.refs_1_, bf16[64,1152]{1,0:T(8,128)(2,1)S(1)} %collective-permute-done.2.refs_2_, ...), custom_call_target="tpu_custom_call" | custom-call | flops 301989888 | bytes 1048576 | tf_op jit(solution)/shard_map/keyval_far/pallas_call | solution.py:41
  18.3 1.3 %collective-permute-start.8 = (bf16[512,128]{1,0:T(8,128)(2,1)S(1)}, bf16[512,128]{1,0:T(8,128)(2,1)S(1)}, u32[]{:S(2)}, u32[]{:S(2)}) collective-permute-start(bf16[512,128]{1,0:T(8,128)(2,1)S(1)} %bitcast.24), channel_id=1, source_target_pairs={{0,2},{2,4},{4,6},{6,0},{1,3},{3,5},{5,7},{7,1},{8,10},{10,12},{12... | collective-permute-start | bytes 393224 | tf_op jit(solution)/shard_map/ppermute | solution.py:371
  19.6 2.0 %collective-permute-start.9 = (bf16[512,128]{1,0:T(8,128)(2,1)S(1)}, bf16[512,128]{1,0:T(8,128)(2,1)S(1)}, u32[]{:S(2)}, u32[]{:S(2)}) collective-permute-start(bf16[512,128]{1,0:T(8,128)(2,1)S(1)} %bitcast.23), channel_id=1, source_target_pairs={{0,6},{2,0},{4,2},{6,4},{1,7},{3,1},{5,3},{7,5},{8,14},{10,8},{12,... | collective-permute-start | bytes 393224 | tf_op jit(solution)/shard_map/ppermute | solution.py:371
  21.8 0.9 %copy-done.1 = bf16[64,1152]{1,0:T(8,128)(2,1)S(1)} copy-done((bf16[64,1152]{1,0:T(8,128)(2,1)S(1)}, bf16[64,1152]{1,0:T(8,128)(2,1)}, u32[]{:S(2)}) %copy-start.1) | copy-done | bytes 147480
  22.8 1.8 %keyval_near.1 = (f32[4,2,64,256]{3,2,1,0:T(8,128)S(1)}, f32[4,2,64,256]{3,2,1,0:T(8,128)S(1)}, f32[4,2,64,256]{3,2,1,0:T(8,128)S(1)}) custom-call(s32[35]{0:T(128)S(1)} %pad_add_fusion.ids, bf16[64,1152]{1,0:T(8,128)(2,1)S(1)} %get-tuple-element.100.refs_0_, bf16[64,1152]{1,0:T(8,128)(2,1)S(1)} %collective-permute-done.1.refs_1_, ...), custom_call_target="tpu_custom_call" | custom-call | flops 905969664 | bytes 1048576 | tf_op jit(solution)/shard_map/keyval_near/pallas_call | solution.py:41
  25.8 1.1 %collective-permute-start.10 = (bf16[512,256]{1,0:T(8,128)(2,1)S(1)}, bf16[512,256]{1,0:T(8,128)(2,1)S(1)}, u32[]{:S(2)}, u32[]{:S(2)}) collective-permute-start(bf16[512,256]{1,0:T(8,128)(2,1)S(1)} %get-tuple-element.113), channel_id=1, source_target_pairs={{0,2},{2,4},{4,6},{6,0},{1,3},{3,5},{5,7},{7,1},{8,10},{10,12},{12... | collective-permute-start | bytes 786440 | tf_op jit(solution)/shard_map/ppermute | solution.py:371
  27.0 2.2 %collective-permute-start.11 = (bf16[512,256]{1,0:T(8,128)(2,1)S(1)}, bf16[512,256]{1,0:T(8,128)(2,1)S(1)}, u32[]{:S(2)}, u32[]{:S(2)}) collective-permute-start(bf16[512,256]{1,0:T(8,128)(2,1)S(1)} %get-tuple-element.114), channel_id=1, source_target_pairs={{0,6},{2,0},{4,2},{6,4},{1,7},{3,1},{5,3},{7,5},{8,14},{10,8},{12,... | collective-permute-start | bytes 786440 | tf_op jit(solution)/shard_map/ppermute | solution.py:371
  29.2 2.1 %query_partial.1 = (bf16[4,2,64,256]{3,2,1,0:T(8,128)(2,1)S(1)}, bf16[4,2,64,256]{3,2,1,0:T(8,128)(2,1)S(1)}, bf16[4,2,64,256]{3,2,1,0:T(8,128)(2,1)S(1)}, bf16[4,2,64,256]{3,2,1,0:T(8,128)(2,1)S(1)}) custom-call(s32[35]{0:T(128)S(1)} %pad_add_fusion.ids, bf16[64,1152]{1,0:T(8,128)(2,1)S(1)} %get-tuple-element.100.refs_0_, ...), custom_call_target="tpu_custom_call" | custom-call | flops 1207959552 | bytes 1048576 | tf_op jit(solution)/shard_map/query_partial/pallas_call | solution.py:41
  31.3 3.4 %collective-permute-done.10.refs_1_ = bf16[512,256]{1,0:T(8,128)(2,1)S(1)} collective-permute-done((bf16[512,256]{1,0:T(8,128)(2,1)S(1)}, bf16[512,256]{1,0:T(8,128)(2,1)S(1)}, u32[]{:S(2)}, u32[]{:S(2)}) %collective-permute-start.10) | collective-permute-done | bytes 262176 | tf_op jit(solution)/shard_map/ppermute | solution.py:371
  35.4 3.8 %collective-permute-start.15 = (bf16[512,256]{1,0:T(8,128)(2,1)S(1)}, bf16[512,256]{1,0:T(8,128)(2,1)S(1)}, u32[]{:S(2)}, u32[]{:S(2)}) collective-permute-start(bf16[512,256]{1,0:T(8,128)(2,1)S(1)} %keyval_rotate.1.own), channel_id=1, source_target_pairs={{0,32},{8,40},{16,48},{24,56},{32,64},{40,72},{48,80},{56,88},{64,... | collective-permute-start | bytes 786440 | tf_op jit(solution)/shard_map/ppermute | solution.py:341
  39.3 2.8 %collective-permute-start.18 = (bf16[512,256]{1,0:T(8,128)(2,1)S(1)}, bf16[512,256]{1,0:T(8,128)(2,1)S(1)}, u32[]{:S(2)}, u32[]{:S(2)}) collective-permute-start(bf16[512,256]{1,0:T(8,128)(2,1)S(1)} %keyval_rotate.1.own), channel_id=1, source_target_pairs={{0,24},{8,16},{16,8},{24,0},{32,56},{40,48},{48,40},{56,32},{64,88... | collective-permute-start | bytes 786440 | tf_op jit(solution)/shard_map/ppermute | solution.py:341
  42.1 2.6 %collective-permute-start.12 = (bf16[512,256]{1,0:T(8,128)(2,1)S(1)}, bf16[512,256]{1,0:T(8,128)(2,1)S(1)}, u32[]{:S(2)}, u32[]{:S(2)}) collective-permute-start(bf16[512,256]{1,0:T(8,128)(2,1)S(1)} %bitcast.22), channel_id=1, source_target_pairs={{0,4},{2,6},{4,0},{6,2},{1,5},{3,7},{5,1},{7,3},{8,12},{10,14},{12... | collective-permute-start | bytes 786440 | tf_op jit(solution)/shard_map/ppermute | solution.py:371
  44.7 1.2 %collective-permute-start.13 = (bf16[512,256]{1,0:T(8,128)(2,1)S(1)}, bf16[512,256]{1,0:T(8,128)(2,1)S(1)}, u32[]{:S(2)}, u32[]{:S(2)}) collective-permute-start(bf16[512,256]{1,0:T(8,128)(2,1)S(1)} %bitcast.21), channel_id=1, source_target_pairs={{0,2},{2,4},{4,6},{6,0},{1,3},{3,5},{5,7},{7,1},{8,10},{10,12},{12... | collective-permute-start | bytes 786440 | tf_op jit(solution)/shard_map/ppermute | solution.py:371
  45.9 2.0 %collective-permute-start.14 = (bf16[512,256]{1,0:T(8,128)(2,1)S(1)}, bf16[512,256]{1,0:T(8,128)(2,1)S(1)}, u32[]{:S(2)}, u32[]{:S(2)}) collective-permute-start(bf16[512,256]{1,0:T(8,128)(2,1)S(1)} %bitcast.20), channel_id=1, source_target_pairs={{0,6},{2,0},{4,2},{6,4},{1,7},{3,1},{5,3},{7,5},{8,14},{10,8},{12,... | collective-permute-start | bytes 786440 | tf_op jit(solution)/shard_map/ppermute | solution.py:371
  48.0 1.9 %collective-permute-start.16 = (bf16[512,256]{1,0:T(8,128)(2,1)S(1)}, bf16[512,256]{1,0:T(8,128)(2,1)S(1)}, u32[]{:S(2)}, u32[]{:S(2)}) collective-permute-start(bf16[512,256]{1,0:T(8,128)(2,1)S(1)} %collective-permute-done.15.back1), channel_id=1, source_target_pairs={{0,32},{8,40},{16,48},{24,56},{32,64},{40,72},{48,80},{56,88},{64,... | collective-permute-start | bytes 786440 | tf_op jit(solution)/shard_map/ppermute | solution.py:341
  49.9 1.9 %collective-permute-start.19 = (bf16[512,256]{1,0:T(8,128)(2,1)S(1)}, bf16[512,256]{1,0:T(8,128)(2,1)}, u32[]{:S(2)}, u32[]{:S(2)}) collective-permute-start(bf16[512,256]{1,0:T(8,128)(2,1)S(1)} %collective-permute-done.18), channel_id=1, source_target_pairs={{0,32},{8,40},{32,64},{40,72},{64,96},{72,104},{128,160},{136,168}... | collective-permute-start | bytes 786440 | tf_op jit(solution)/shard_map/ppermute | solution.py:341
  52.6 2.4 %collective-permute-start.20 = (bf16[512,256]{1,0:T(8,128)(2,1)S(1)}, bf16[512,256]{1,0:T(8,128)(2,1)S(1)}, u32[]{:S(2)}, u32[]{:S(2)}) collective-permute-start(bf16[512,256]{1,0:T(8,128)(2,1)S(1)} %collective-permute-done.15.back1), channel_id=1, source_target_pairs={{0,24},{8,16},{16,40},{24,32},{32,56},{40,48},{48,72},{56,64},{64,... | collective-permute-start | bytes 786440 | tf_op jit(solution)/shard_map/ppermute | solution.py:341
  55.4 2.0 %collective-permute-done.16.back2 = bf16[512,256]{1,0:T(8,128)(2,1)S(1)} collective-permute-done((bf16[512,256]{1,0:T(8,128)(2,1)S(1)}, bf16[512,256]{1,0:T(8,128)(2,1)S(1)}, u32[]{:S(2)}, u32[]{:S(2)}) %collective-permute-start.16) | collective-permute-done | bytes 262176 | tf_op jit(solution)/shard_map/ppermute | solution.py:341
  58.4 2.0 %attend_early.1.before = f32[2,512,256]{2,1,0:T(8,128)S(1)} custom-call(s32[35]{0:T(128)S(1)} %pad_add_fusion.ids, bf16[512,256]{1,0:T(8,128)(2,1)S(1)} %query_rotate.1.query, bf16[512,256]{1,0:T(8,128)(2,1)S(1)} %keyval_rotate.1.own, bf16[512,256]{1,0:T(8,128)(2,1)S(1)} %collective-permute-done.15.back1, bf16[512,256]{1,0:T(8,128)(2,1)S(1)} %collective-permute-done.16.back2), custom_call_target="tpu_custom_call" | custom-call | flops 2147483648 | bytes 1048576 | tf_op jit(solution)/shard_map/attend_early/pallas_call | solution.py:41
  60.4 2.5 %collective-permute-done.20 = bf16[512,256]{1,0:T(8,128)(2,1)S(1)} collective-permute-done((bf16[512,256]{1,0:T(8,128)(2,1)S(1)}, bf16[512,256]{1,0:T(8,128)(2,1)S(1)}, u32[]{:S(2)}, u32[]{:S(2)}) %collective-permute-start.20) | collective-permute-done | bytes 262176 | tf_op jit(solution)/shard_map/ppermute | solution.py:341
  62.9 1.0 %broadcast_select_fusion = (bf16[512,256]{1,0:T(8,128)(2,1)S(1)}, bf16[512,256]{1,0:T(8,128)(2,1)S(1)}) fusion(bf16[512,256]{1,0:T(8,128)(2,1)S(1)} %collective-permute-done.20, bf16[512,256]{1,0:T(8,128)(2,1)S(1)} %collective-permute-done.18, pred[]{:T(512)S(6)} %eq.5, bf16[512,256]{1,0:T(8,128)(2,1)} %collective-permute-done.19), kind=kLoop, calls=%fused_computation.4 | loop fusion | flops 262144 | bytes 1310721 | tf_op jit(solution)/shard_map/jit(_where)/select_n | solution.py:450
  64.6 2.7 %attend_late.1 = bf16[8,144,256]{2,1,0:T(8,128)(2,1)S(1)} custom-call(s32[35]{0:T(128)S(1)} %pad_add_fusion.ids, bf16[512,256]{1,0:T(8,128)(2,1)S(1)} %query_rotate.1.query, bf16[512,256]{1,0:T(8,128)(2,1)S(1)} %collective-permute-done.17.pair, bf16[512,256]{1,0:T(8,128)(2,1)S(1)} %keyval_rotate.1.own, bf16[512,256]{1,0:T(8,128)(2,1)S(1)} %collective-permute-done.15.back1, ...), custom_call_target="tpu_custom_call" | custom-call | flops 2147483648 | bytes 1048576 | tf_op jit(solution)/shard_map/attend_late/pallas_call | solution.py:41
  67.3 12.3 %all_to_all.5.pieces = bf16[8,144,256]{2,1,0:T(8,128)(2,1)S(1)} all-to-all(bf16[8,144,256]{2,1,0:T(8,128)(2,1)S(1)} %attend_late.1), channel_id=1, replica_groups=mesh['z'=8,'xh'=2,'xl'=2,'row'=4,'col'=2] {'xl','row'}, dimensions={0} | all-to-all | bytes 1179648 | tf_op jit(solution)/shard_map/all_to_all | solution.py:482
  79.6 1.5 %finish.1 = bf16[128,1024]{1,0:T(8,128)(2,1)} custom-call(s32[35]{0:T(128)S(1)} %pad_add_fusion.ids, bf16[8,144,256]{2,1,0:T(8,128)(2,1)S(1)} %all_to_all.5.pieces), custom_call_target="tpu_custom_call" | custom-call | bytes 1048576 | tf_op jit(solution)/shard_map/finish/pallas_call | solution.py:41
  (38 shorter events, 7.5 us)
Async XLA Ops:
  0.0 2.5 %collective-permute-start = (bf16[128,2304]{1,0:T(8,128)(2,1)}, bf16[128,2304]{1,0:T(8,128)(2,1)S(1)}, u32[]{:S(2)}, u32[]{:S(2)}) collective-permute-start(bf16[128,2304]{1,0:T(8,128)(2,1)} %param.5), channel_id=1, source_target_pairs={{0,1},{1,0},{2,3},{3,2},{4,5},{5,4},{6,7},{7,6},{8,9},{9,8},{10,11... | collective-permute-start | bytes 1769480 | tf_op jit(solution)/shard_map/ppermute | solution.py:375
  3.4 8.3 %collective-permute-start.1 = (bf16[64,1152]{1,0:T(8,128)(2,1)S(1)}, bf16[64,1152]{1,0:T(8,128)(2,1)S(1)}, u32[]{:S(2)}, u32[]{:S(2)}) collective-permute-start(bf16[64,1152]{1,0:T(8,128)(2,1)S(1)} %get-tuple-element.67), channel_id=1, source_target_pairs={{0,2},{2,4},{4,6},{6,0},{1,3},{3,5},{5,7},{7,1},{8,10},{10,12},{12... | collective-permute-start | bytes 442376 | tf_op jit(solution)/shard_map/ppermute | solution.py:371
  5.0 10.3 %collective-permute-start.2 = (bf16[64,1152]{1,0:T(8,128)(2,1)S(1)}, bf16[64,1152]{1,0:T(8,128)(2,1)S(1)}, u32[]{:S(2)}, u32[]{:S(2)}) collective-permute-start(bf16[64,1152]{1,0:T(8,128)(2,1)S(1)} %get-tuple-element.68), channel_id=1, source_target_pairs={{0,4},{2,6},{4,0},{6,2},{1,5},{3,7},{5,1},{7,3},{8,12},{10,14},{12... | collective-permute-start | bytes 442376 | tf_op jit(solution)/shard_map/ppermute | solution.py:371
  7.9 7.4 %collective-permute-start.3 = (bf16[64,1152]{1,0:T(8,128)(2,1)S(1)}, bf16[64,1152]{1,0:T(8,128)(2,1)S(1)}, u32[]{:S(2)}, u32[]{:S(2)}) collective-permute-start(bf16[64,1152]{1,0:T(8,128)(2,1)S(1)} %get-tuple-element.69), channel_id=1, source_target_pairs={{0,6},{2,0},{4,2},{6,4},{1,7},{3,1},{5,3},{7,5},{8,14},{10,8},{12,... | collective-permute-start | bytes 442376 | tf_op jit(solution)/shard_map/ppermute | solution.py:371
  11.6 5.4 %collective-permute-start.4 = (bf16[64,1152]{1,0:T(8,128)(2,1)S(1)}, bf16[64,1152]{1,0:T(8,128)(2,1)S(1)}, u32[]{:S(2)}, u32[]{:S(2)}) collective-permute-start(bf16[64,1152]{1,0:T(8,128)(2,1)S(1)} %get-tuple-element.100.refs_0_), channel_id=1, source_target_pairs={{0,1},{1,0},{2,3},{3,2},{4,5},{5,4},{6,7},{7,6},{8,9},{9,8},{10,11... | collective-permute-start | bytes 442376 | tf_op jit(solution)/shard_map/ppermute | solution.py:375
  15.3 1.6 %collective-permute-start.5 = (bf16[64,1152]{1,0:T(8,128)(2,1)S(1)}, bf16[64,1152]{1,0:T(8,128)(2,1)S(1)}, u32[]{:S(2)}, u32[]{:S(2)}) collective-permute-start(bf16[64,1152]{1,0:T(8,128)(2,1)S(1)} %collective-permute-done.1.refs_1_), channel_id=1, source_target_pairs={{0,1},{1,0},{2,3},{3,2},{4,5},{5,4},{6,7},{7,6},{8,9},{9,8},{10,11... | collective-permute-start | bytes 442376 | tf_op jit(solution)/shard_map/ppermute | solution.py:375
  15.3 1.6 %collective-permute-start.6 = (bf16[64,1152]{1,0:T(8,128)(2,1)S(1)}, bf16[64,1152]{1,0:T(8,128)(2,1)S(1)}, u32[]{:S(2)}, u32[]{:S(2)}) collective-permute-start(bf16[64,1152]{1,0:T(8,128)(2,1)S(1)} %collective-permute-done.2.refs_2_), channel_id=1, source_target_pairs={{0,1},{1,0},{2,3},{3,2},{4,5},{5,4},{6,7},{7,6},{8,9},{9,8},{10,11... | collective-permute-start | bytes 442376 | tf_op jit(solution)/shard_map/ppermute | solution.py:375
  15.8 1.4 %collective-permute-start.7 = (bf16[64,1152]{1,0:T(8,128)(2,1)S(1)}, bf16[64,1152]{1,0:T(8,128)(2,1)S(1)}, u32[]{:S(2)}, u32[]{:S(2)}) collective-permute-start(bf16[64,1152]{1,0:T(8,128)(2,1)S(1)} %collective-permute-done.3.refs_3_), channel_id=1, source_target_pairs={{0,1},{1,0},{2,3},{3,2},{4,5},{5,4},{6,7},{7,6},{8,9},{9,8},{10,11... | collective-permute-start | bytes 442376 | tf_op jit(solution)/shard_map/ppermute | solution.py:375
  16.9 4.7 %copy-start = (bf16[64,1152]{1,0:T(8,128)(2,1)}, bf16[64,1152]{1,0:T(8,128)(2,1)S(1)}, u32[]{:S(2)}) copy-start(bf16[64,1152]{1,0:T(8,128)(2,1)S(1)} %collective-permute-done.4.refs_4_) | copy-start | bytes 442372
  18.3 6.9 %collective-permute-start.8 = (bf16[512,128]{1,0:T(8,128)(2,1)S(1)}, bf16[512,128]{1,0:T(8,128)(2,1)S(1)}, u32[]{:S(2)}, u32[]{:S(2)}) collective-permute-start(bf16[512,128]{1,0:T(8,128)(2,1)S(1)} %bitcast.24), channel_id=1, source_target_pairs={{0,2},{2,4},{4,6},{6,0},{1,3},{3,5},{5,7},{7,1},{8,10},{10,12},{12... | collective-permute-start | bytes 393224 | tf_op jit(solution)/shard_map/ppermute | solution.py:371
  19.6 5.6 %collective-permute-start.9 = (bf16[512,128]{1,0:T(8,128)(2,1)S(1)}, bf16[512,128]{1,0:T(8,128)(2,1)S(1)}, u32[]{:S(2)}, u32[]{:S(2)}) collective-permute-start(bf16[512,128]{1,0:T(8,128)(2,1)S(1)} %bitcast.23), channel_id=1, source_target_pairs={{0,6},{2,0},{4,2},{6,4},{1,7},{3,1},{5,3},{7,5},{8,14},{10,8},{12,... | collective-permute-start | bytes 393224 | tf_op jit(solution)/shard_map/ppermute | solution.py:371
  21.8 0.9 %copy-start.1 = (bf16[64,1152]{1,0:T(8,128)(2,1)S(1)}, bf16[64,1152]{1,0:T(8,128)(2,1)}, u32[]{:S(2)}) copy-start(bf16[64,1152]{1,0:T(8,128)(2,1)} %copy-done) | copy-start | bytes 442372
  22.7 6.4 %copy-start.2 = (bf16[64,1152]{1,0:T(8,128)(2,1)S(1)}, bf16[64,1152]{1,0:T(8,128)(2,1)}, u32[]{:S(2)}) copy-start(bf16[64,1152]{1,0:T(8,128)(2,1)} %copy-done) | copy-start | bytes 442372
  22.7 6.4 %copy-start.3 = (bf16[1152,1024]{1,0:T(8,128)(2,1)S(1)}, bf16[1152,1024]{1,0:T(8,128)(2,1)}, u32[]{:S(2)}) copy-start(bf16[1152,1024]{1,0:T(8,128)(2,1)} %refs_8_.1) | copy-start | bytes 7077892
  25.8 8.9 %collective-permute-start.10 = (bf16[512,256]{1,0:T(8,128)(2,1)S(1)}, bf16[512,256]{1,0:T(8,128)(2,1)S(1)}, u32[]{:S(2)}, u32[]{:S(2)}) collective-permute-start(bf16[512,256]{1,0:T(8,128)(2,1)S(1)} %get-tuple-element.113), channel_id=1, source_target_pairs={{0,2},{2,4},{4,6},{6,0},{1,3},{3,5},{5,7},{7,1},{8,10},{10,12},{12... | collective-permute-start | bytes 786440 | tf_op jit(solution)/shard_map/ppermute | solution.py:371
  27.0 7.8 %collective-permute-start.11 = (bf16[512,256]{1,0:T(8,128)(2,1)S(1)}, bf16[512,256]{1,0:T(8,128)(2,1)S(1)}, u32[]{:S(2)}, u32[]{:S(2)}) collective-permute-start(bf16[512,256]{1,0:T(8,128)(2,1)S(1)} %get-tuple-element.114), channel_id=1, source_target_pairs={{0,6},{2,0},{4,2},{6,4},{1,7},{3,1},{5,3},{7,5},{8,14},{10,8},{12,... | collective-permute-start | bytes 786440 | tf_op jit(solution)/shard_map/ppermute | solution.py:371
  35.4 12.5 %collective-permute-start.15 = (bf16[512,256]{1,0:T(8,128)(2,1)S(1)}, bf16[512,256]{1,0:T(8,128)(2,1)S(1)}, u32[]{:S(2)}, u32[]{:S(2)}) collective-permute-start(bf16[512,256]{1,0:T(8,128)(2,1)S(1)} %keyval_rotate.1.own), channel_id=1, source_target_pairs={{0,32},{8,40},{16,48},{24,56},{32,64},{40,72},{48,80},{56,88},{64,... | collective-permute-start | bytes 786440 | tf_op jit(solution)/shard_map/ppermute | solution.py:341
  39.3 10.6 %collective-permute-start.18 = (bf16[512,256]{1,0:T(8,128)(2,1)S(1)}, bf16[512,256]{1,0:T(8,128)(2,1)S(1)}, u32[]{:S(2)}, u32[]{:S(2)}) collective-permute-start(bf16[512,256]{1,0:T(8,128)(2,1)S(1)} %keyval_rotate.1.own), channel_id=1, source_target_pairs={{0,24},{8,16},{16,8},{24,0},{32,56},{40,48},{48,40},{56,32},{64,88... | collective-permute-start | bytes 786440 | tf_op jit(solution)/shard_map/ppermute | solution.py:341
  42.1 10.5 %collective-permute-start.12 = (bf16[512,256]{1,0:T(8,128)(2,1)S(1)}, bf16[512,256]{1,0:T(8,128)(2,1)S(1)}, u32[]{:S(2)}, u32[]{:S(2)}) collective-permute-start(bf16[512,256]{1,0:T(8,128)(2,1)S(1)} %bitcast.22), channel_id=1, source_target_pairs={{0,4},{2,6},{4,0},{6,2},{1,5},{3,7},{5,1},{7,3},{8,12},{10,14},{12... | collective-permute-start | bytes 786440 | tf_op jit(solution)/shard_map/ppermute | solution.py:371
  44.7 10.6 %collective-permute-start.13 = (bf16[512,256]{1,0:T(8,128)(2,1)S(1)}, bf16[512,256]{1,0:T(8,128)(2,1)S(1)}, u32[]{:S(2)}, u32[]{:S(2)}) collective-permute-start(bf16[512,256]{1,0:T(8,128)(2,1)S(1)} %bitcast.21), channel_id=1, source_target_pairs={{0,2},{2,4},{4,6},{6,0},{1,3},{3,5},{5,7},{7,1},{8,10},{10,12},{12... | collective-permute-start | bytes 786440 | tf_op jit(solution)/shard_map/ppermute | solution.py:371
  45.9 9.4 %collective-permute-start.14 = (bf16[512,256]{1,0:T(8,128)(2,1)S(1)}, bf16[512,256]{1,0:T(8,128)(2,1)S(1)}, u32[]{:S(2)}, u32[]{:S(2)}) collective-permute-start(bf16[512,256]{1,0:T(8,128)(2,1)S(1)} %bitcast.20), channel_id=1, source_target_pairs={{0,6},{2,0},{4,2},{6,4},{1,7},{3,1},{5,3},{7,5},{8,14},{10,8},{12,... | collective-permute-start | bytes 786440 | tf_op jit(solution)/shard_map/ppermute | solution.py:371
  48.0 9.4 %collective-permute-start.16 = (bf16[512,256]{1,0:T(8,128)(2,1)S(1)}, bf16[512,256]{1,0:T(8,128)(2,1)S(1)}, u32[]{:S(2)}, u32[]{:S(2)}) collective-permute-start(bf16[512,256]{1,0:T(8,128)(2,1)S(1)} %collective-permute-done.15.back1), channel_id=1, source_target_pairs={{0,32},{8,40},{16,48},{24,56},{32,64},{40,72},{48,80},{56,88},{64,... | collective-permute-start | bytes 786440 | tf_op jit(solution)/shard_map/ppermute | solution.py:341
  49.9 10.5 %collective-permute-start.19 = (bf16[512,256]{1,0:T(8,128)(2,1)S(1)}, bf16[512,256]{1,0:T(8,128)(2,1)}, u32[]{:S(2)}, u32[]{:S(2)}) collective-permute-start(bf16[512,256]{1,0:T(8,128)(2,1)S(1)} %collective-permute-done.18), channel_id=1, source_target_pairs={{0,32},{8,40},{32,64},{40,72},{64,96},{72,104},{128,160},{136,168}... | collective-permute-start | bytes 786440 | tf_op jit(solution)/shard_map/ppermute | solution.py:341
  52.6 10.4 %collective-permute-start.20 = (bf16[512,256]{1,0:T(8,128)(2,1)S(1)}, bf16[512,256]{1,0:T(8,128)(2,1)S(1)}, u32[]{:S(2)}, u32[]{:S(2)}) collective-permute-start(bf16[512,256]{1,0:T(8,128)(2,1)S(1)} %collective-permute-done.15.back1), channel_id=1, source_target_pairs={{0,24},{8,16},{16,40},{24,32},{32,56},{40,48},{48,72},{56,64},{64,... | collective-permute-start | bytes 786440 | tf_op jit(solution)/shard_map/ppermute | solution.py:341
  58.1 6.5 %collective-permute-start.17 = (bf16[512,256]{1,0:T(8,128)(2,1)S(1)}, bf16[512,256]{1,0:T(8,128)(2,1)S(1)}, u32[]{:S(2)}, u32[]{:S(2)}) collective-permute-start(bf16[512,256]{1,0:T(8,128)(2,1)S(1)} %query_rotate.1.query), channel_id=1, source_target_pairs={{0,8},{8,0},{16,24},{24,16},{32,40},{40,32},{48,56},{56,48},{64,72... | collective-permute-start | bytes 786440 | tf_op jit(solution)/shard_map/ppermute | solution.py:341

commit v8 on v7

--- a/solution.py
+++ b/solution.py
@@ -227,20 +227,22 @@
 
 
 def late_body(
-    ids, query, pair, own, back1, mirror1, back2, chosen, before, out, sums, pair_sums, keys, values
+    ids, query, pair, own, back1, back2, raised, opposite, across, before, out, sums, pair_sums, keys, values
 ):
     shard, _, _ = scalars(ids)
     side = shard & 1
     partner = shard + 1 - 2 * side
     own_shard, back1_shard, mirror1_shard, back2_shard, chosen_shard = key_shards(shard)
     first = (shard >> 4) << 4
+    lower = (shard & 2) == 0
     used = 0
     listed = (
         (own, own_shard, side == 0),
         (back2, back2_shard, side == 1),
         (back1, back1_shard, True),
-        (mirror1, mirror1_shard, True),
-        (chosen, chosen_shard, True),
+        (raised, mirror1_shard, lower),
+        (opposite, chosen_shard, jnp.logical_not(lower)),
+        (across, jnp.where(lower, chosen_shard, mirror1_shard), True),
     )
     for place, (keyval, key_shard, seen) in enumerate(listed):
         if place == 3:
@@ -444,10 +446,7 @@
     back2 = hop(back1)
     across = turned(back1)
     opposite = mirrored(own)
-    lower = lax.axis_index("xh") == 0
     raised = hop(opposite, (0, 1))
-    mirror1 = jnp.where(lower, raised, across)
-    chosen = jnp.where(lower, across, opposite)
 
     query_sums, back2 = lax.optimization_barrier((query_sums, back2))
     query = local(
@@ -467,7 +466,7 @@
     )
     pieces = local(
         late_body,
-        (ids, query, pair, own, back1, mirror1, back2, chosen, before),
+        (ids, query, pair, own, back1, back2, raised, opposite, across, before),
         sds((2 * ROWS, PIECE, 2 * HEAD), bf16),
         "attend_late",
         scratch=[

time: 82.2 us -> 84 us (1.022)
  the two profiles are of different devices: /device:TPU:64 before, /device:TPU:32 now
where the time goes in v8:
time: 84 us; the launch traced here: 82.7 us
  starting transfers between devices  36.1 us (43%)
  waiting for transfers between devices  14.2 us (17%)
  Pallas kernels  13.2 us (16%)
  blocking collectives  12.9 us (15%)
  local copies, waits for them, and re-layouts  4.01 us (5%)
  other arithmetic  1.94 us (2%)
    ppermute x10, starting transfers between devices, onward(): lax.ppermute(value, 'row', [(row, (row + step) % ROWS) for row in range(R...  18.4 us
    ppermute x6, starting transfers between devices, along_seq(): return lax.ppermute(value, SEQ, pairs)  17.1 us
    pallas_call x10, Pallas kernels, local(): pl.pallas_call(body, out_shape=out_shapes, in_specs=[SMEM] + [VMEM] * (le...  13.2 us
    all_to_all x1, blocking collectives, on_device(): returned = lax.all_to_all(pieces, ('xl', 'row'), 0, 0)  12.9 us
    ppermute x10, waiting for transfers between devices, onward(): lax.ppermute(value, 'row', [(row, (row + step) % ROWS) for row in range(R...  9.44 us
    ppermute x6, waiting for transfers between devices, along_seq(): return lax.ppermute(value, SEQ, pairs)  4.53 us
    unnamed x3, local copies, waits for them, and re-layouts  2.29 us
  transfers between devices with their start and end apart: 21, of which 7 were waited for; matrix products, arithmetic and copies ran while one was open for 7% of the time, Pallas kernels for 8%

profile of v8, /device:TPU:32, one launch (start us, length us, event | category | flops | bytes accessed | tf_op | source)
XLA Modules:
  0.0 82.7 jit_solution(3391781588911268717)
XLA Ops:
  1.5 1.0 %constant_dynamic-slice_fusion.own = bf16[64,2304]{1,0:T(8,128)(2,1)S(1)} fusion(bf16[128,2304]{1,0:T(8,128)(2,1)} %param.5, s32[]{:T(128)S(6)} %select_n.10), kind=kLoop, calls=%fused_computation.8 | loop fusion | bytes 589828 | tf_op jit(solution)/shard_map/dynamic_slice | solution.py:388
  2.5 0.9 %norm.1 = (bf16[64,1152]{1,0:T(8,128)(2,1)S(1)}, bf16[64,1152]{1,0:T(8,128)(2,1)S(1)}, bf16[64,1152]{1,0:T(8,128)(2,1)S(1)}, bf16[64,1152]{1,0:T(8,128)(2,1)S(1)}) custom-call(s32[35]{0:T(128)S(1)} %pad_add_fusion.ids, bf16[64,2304]{1,0:T(8,128)(2,1)S(1)} %constant_dynamic-slice_fusion.own, bf16[128,2304]{1,0:T(8,128)(2,1)S(1)} %collective-permute-done.received, ...), custom_call_target="tpu_custom_call" | custom-call | bytes 1048576 | tf_op jit(solution)/shard_map/norm/pallas_call | solution.py:41
  3.4 1.7 %collective-permute-start.1 = (bf16[64,1152]{1,0:T(8,128)(2,1)S(1)}, bf16[64,1152]{1,0:T(8,128)(2,1)S(1)}, u32[]{:S(2)}, u32[]{:S(2)}) collective-permute-start(bf16[64,1152]{1,0:T(8,128)(2,1)S(1)} %get-tuple-element.67), channel_id=1, source_target_pairs={{0,2},{2,4},{4,6},{6,0},{1,3},{3,5},{5,7},{7,1},{8,10},{10,12},{12... | collective-permute-start | bytes 442376 | tf_op jit(solution)/shard_map/ppermute | solution.py:373
  5.0 2.9 %collective-permute-start.2 = (bf16[64,1152]{1,0:T(8,128)(2,1)S(1)}, bf16[64,1152]{1,0:T(8,128)(2,1)S(1)}, u32[]{:S(2)}, u32[]{:S(2)}) collective-permute-start(bf16[64,1152]{1,0:T(8,128)(2,1)S(1)} %get-tuple-element.68), channel_id=1, source_target_pairs={{0,4},{2,6},{4,0},{6,2},{1,5},{3,7},{5,1},{7,3},{8,12},{10,14},{12... | collective-permute-start | bytes 442376 | tf_op jit(solution)/shard_map/ppermute | solution.py:373
  7.9 1.3 %collective-permute-start.3 = (bf16[64,1152]{1,0:T(8,128)(2,1)S(1)}, bf16[64,1152]{1,0:T(8,128)(2,1)S(1)}, u32[]{:S(2)}, u32[]{:S(2)}) collective-permute-start(bf16[64,1152]{1,0:T(8,128)(2,1)S(1)} %get-tuple-element.69), channel_id=1, source_target_pairs={{0,6},{2,0},{4,2},{6,4},{1,7},{3,1},{5,3},{7,5},{8,14},{10,8},{12,... | collective-permute-start | bytes 442376 | tf_op jit(solution)/shard_map/ppermute | solution.py:373
  9.3 2.3 %copy.6 = bf16[144,8,2,512]{3,1,2,0:T(8,128)(2,1)S(1)} copy(bf16[144,8,2,512]{3,2,1,0:T(2,128)(2,1)} %bitcast.25) | data formatting | bytes 4718592
  11.7 3.6 %collective-permute-done.2.refs_2_ = bf16[64,1152]{1,0:T(8,128)(2,1)S(1)} collective-permute-done((bf16[64,1152]{1,0:T(8,128)(2,1)S(1)}, bf16[64,1152]{1,0:T(8,128)(2,1)S(1)}, u32[]{:S(2)}, u32[]{:S(2)}) %collective-permute-start.2) | collective-permute-done | bytes 147488 | tf_op jit(solution)/shard_map/ppermute | solution.py:373
  15.9 1.0 %fusion = (f32[512,64]{1,0:T(8,128)S(1)}, f32[512,64]{1,0:T(8,128)S(1)}, f32[512,64]{1,0:T(8,128)S(1)}) fusion(f32[64]{0:T(128)S(1)} %multiply_power_fusion, f32[512]{0:T(512)S(1)} %add_convert_fusion), kind=kLoop, calls=%fused_computation.4 | loop fusion | flops 65536 | bytes 395520 | tf_op jit(solution)/shard_map/neg | solution.py:409
  17.2 1.1 %keyval_far.1 = (bf16[4,2,64,128]{3,2,1,0:T(8,128)(2,1)S(1)}, bf16[4,2,64,128]{3,2,1,0:T(8,128)(2,1)S(1)}) custom-call(s32[35]{0:T(128)S(1)} %pad_add_fusion.ids, bf16[64,1152]{1,0:T(8,128)(2,1)S(1)} %get-tuple-element.100.refs_0_, bf16[64,1152]{1,0:T(8,128)(2,1)S(1)} %collective-permute-done.1.refs_1_, bf16[64,1152]{1,0:T(8,128)(2,1)S(1)} %collective-permute-done.2.refs_2_, ...), custom_call_target="tpu_custom_call" | custom-call | flops 301989888 | bytes 1048576 | tf_op jit(solution)/shard_map/keyval_far/pallas_call | solution.py:41
  18.3 1.3 %collective-permute-start.8 = (bf16[512,128]{1,0:T(8,128)(2,1)S(1)}, bf16[512,128]{1,0:T(8,128)(2,1)S(1)}, u32[]{:S(2)}, u32[]{:S(2)}) collective-permute-start(bf16[512,128]{1,0:T(8,128)(2,1)S(1)} %bitcast.24), channel_id=1, source_target_pairs={{0,2},{2,4},{4,6},{6,0},{1,3},{3,5},{5,7},{7,1},{8,10},{10,12},{12... | collective-permute-start | bytes 393224 | tf_op jit(solution)/shard_map/ppermute | solution.py:373
  19.6 2.0 %collective-permute-start.9 = (bf16[512,128]{1,0:T(8,128)(2,1)S(1)}, bf16[512,128]{1,0:T(8,128)(2,1)S(1)}, u32[]{:S(2)}, u32[]{:S(2)}) collective-permute-start(bf16[512,128]{1,0:T(8,128)(2,1)S(1)} %bitcast.23), channel_id=1, source_target_pairs={{0,6},{2,0},{4,2},{6,4},{1,7},{3,1},{5,3},{7,5},{8,14},{10,8},{12,... | collective-permute-start | bytes 393224 | tf_op jit(solution)/shard_map/ppermute | solution.py:373
  21.8 1.8 %keyval_near.1 = (f32[4,2,64,256]{3,2,1,0:T(8,128)S(1)}, f32[4,2,64,256]{3,2,1,0:T(8,128)S(1)}, f32[4,2,64,256]{3,2,1,0:T(8,128)S(1)}) custom-call(s32[35]{0:T(128)S(1)} %pad_add_fusion.ids, bf16[64,1152]{1,0:T(8,128)(2,1)S(1)} %get-tuple-element.100.refs_0_, bf16[64,1152]{1,0:T(8,128)(2,1)S(1)} %collective-permute-done.1.refs_1_, ...), custom_call_target="tpu_custom_call" | custom-call | flops 905969664 | bytes 1048576 | tf_op jit(solution)/shard_map/keyval_near/pallas_call | solution.py:41
  23.7 1.5 %collective-permute-done.8.first = bf16[512,128]{1,0:T(8,128)(2,1)S(1)} collective-permute-done((bf16[512,128]{1,0:T(8,128)(2,1)S(1)}, bf16[512,128]{1,0:T(8,128)(2,1)S(1)}, u32[]{:S(2)}, u32[]{:S(2)}) %collective-permute-start.8) | collective-permute-done | bytes 131104 | tf_op jit(solution)/shard_map/ppermute | solution.py:373
  25.8 1.1 %collective-permute-start.10 = (bf16[512,256]{1,0:T(8,128)(2,1)S(1)}, bf16[512,256]{1,0:T(8,128)(2,1)S(1)}, u32[]{:S(2)}, u32[]{:S(2)}) collective-permute-start(bf16[512,256]{1,0:T(8,128)(2,1)S(1)} %get-tuple-element.113), channel_id=1, source_target_pairs={{0,2},{2,4},{4,6},{6,0},{1,3},{3,5},{5,7},{7,1},{8,10},{10,12},{12... | collective-permute-start | bytes 786440 | tf_op jit(solution)/shard_map/ppermute | solution.py:373
  27.0 2.2 %collective-permute-start.11 = (bf16[512,256]{1,0:T(8,128)(2,1)S(1)}, bf16[512,256]{1,0:T(8,128)(2,1)S(1)}, u32[]{:S(2)}, u32[]{:S(2)}) collective-permute-start(bf16[512,256]{1,0:T(8,128)(2,1)S(1)} %get-tuple-element.114), channel_id=1, source_target_pairs={{0,6},{2,0},{4,2},{6,4},{1,7},{3,1},{5,3},{7,5},{8,14},{10,8},{12,... | collective-permute-start | bytes 786440 | tf_op jit(solution)/shard_map/ppermute | solution.py:373
  29.2 2.1 %query_partial.1 = (bf16[4,2,64,256]{3,2,1,0:T(8,128)(2,1)S(1)}, bf16[4,2,64,256]{3,2,1,0:T(8,128)(2,1)S(1)}, bf16[4,2,64,256]{3,2,1,0:T(8,128)(2,1)S(1)}, bf16[4,2,64,256]{3,2,1,0:T(8,128)(2,1)S(1)}) custom-call(s32[35]{0:T(128)S(1)} %pad_add_fusion.ids, bf16[64,1152]{1,0:T(8,128)(2,1)S(1)} %get-tuple-element.100.refs_0_, ...), custom_call_target="tpu_custom_call" | custom-call | flops 1207959552 | bytes 1048576 | tf_op jit(solution)/shard_map/query_partial/pallas_call | solution.py:41
  31.3 3.4 %collective-permute-done.10.refs_1_ = bf16[512,256]{1,0:T(8,128)(2,1)S(1)} collective-permute-done((bf16[512,256]{1,0:T(8,128)(2,1)S(1)}, bf16[512,256]{1,0:T(8,128)(2,1)S(1)}, u32[]{:S(2)}, u32[]{:S(2)}) %collective-permute-start.10) | collective-permute-done | bytes 262176 | tf_op jit(solution)/shard_map/ppermute | solution.py:373
  35.4 3.8 %collective-permute-start.15 = (bf16[512,256]{1,0:T(8,128)(2,1)S(1)}, bf16[512,256]{1,0:T(8,128)(2,1)S(1)}, u32[]{:S(2)}, u32[]{:S(2)}) collective-permute-start(bf16[512,256]{1,0:T(8,128)(2,1)S(1)} %keyval_rotate.1.own), channel_id=1, source_target_pairs={{0,32},{8,40},{16,48},{24,56},{32,64},{40,72},{48,80},{56,88},{64,... | collective-permute-start | bytes 786440 | tf_op jit(solution)/shard_map/ppermute | solution.py:343
  39.3 2.8 %collective-permute-start.18 = (bf16[512,256]{1,0:T(8,128)(2,1)S(1)}, bf16[512,256]{1,0:T(8,128)(2,1)S(1)}, u32[]{:S(2)}, u32[]{:S(2)}) collective-permute-start(bf16[512,256]{1,0:T(8,128)(2,1)S(1)} %keyval_rotate.1.own), channel_id=1, source_target_pairs={{0,24},{8,16},{16,8},{24,0},{32,56},{40,48},{48,40},{56,32},{64,88... | collective-permute-start | bytes 786440 | tf_op jit(solution)/shard_map/ppermute | solution.py:343
  42.1 2.6 %collective-permute-start.12 = (bf16[512,256]{1,0:T(8,128)(2,1)S(1)}, bf16[512,256]{1,0:T(8,128)(2,1)S(1)}, u32[]{:S(2)}, u32[]{:S(2)}) collective-permute-start(bf16[512,256]{1,0:T(8,128)(2,1)S(1)} %bitcast.22), channel_id=1, source_target_pairs={{0,4},{2,6},{4,0},{6,2},{1,5},{3,7},{5,1},{7,3},{8,12},{10,14},{12... | collective-permute-start | bytes 786440 | tf_op jit(solution)/shard_map/ppermute | solution.py:373
  44.7 1.2 %collective-permute-start.13 = (bf16[512,256]{1,0:T(8,128)(2,1)S(1)}, bf16[512,256]{1,0:T(8,128)(2,1)S(1)}, u32[]{:S(2)}, u32[]{:S(2)}) collective-permute-start(bf16[512,256]{1,0:T(8,128)(2,1)S(1)} %bitcast.21), channel_id=1, source_target_pairs={{0,2},{2,4},{4,6},{6,0},{1,3},{3,5},{5,7},{7,1},{8,10},{10,12},{12... | collective-permute-start | bytes 786440 | tf_op jit(solution)/shard_map/ppermute | solution.py:373
  45.9 2.0 %collective-permute-start.14 = (bf16[512,256]{1,0:T(8,128)(2,1)S(1)}, bf16[512,256]{1,0:T(8,128)(2,1)S(1)}, u32[]{:S(2)}, u32[]{:S(2)}) collective-permute-start(bf16[512,256]{1,0:T(8,128)(2,1)S(1)} %bitcast.20), channel_id=1, source_target_pairs={{0,6},{2,0},{4,2},{6,4},{1,7},{3,1},{5,3},{7,5},{8,14},{10,8},{12,... | collective-permute-start | bytes 786440 | tf_op jit(solution)/shard_map/ppermute | solution.py:373
  48.0 3.8 %collective-permute-start.16 = (bf16[512,256]{1,0:T(8,128)(2,1)S(1)}, bf16[512,256]{1,0:T(8,128)(2,1)S(1)}, u32[]{:S(2)}, u32[]{:S(2)}) collective-permute-start(bf16[512,256]{1,0:T(8,128)(2,1)S(1)} %collective-permute-done.15.back1), channel_id=1, source_target_pairs={{0,32},{8,40},{16,48},{24,56},{32,64},{40,72},{48,80},{56,88},{64,... | collective-permute-start | bytes 786440 | tf_op jit(solution)/shard_map/ppermute | solution.py:343
  51.8 0.8 collective-permute-done.12.refs_0_
  52.6 2.4 %collective-permute-start.20 = (bf16[512,256]{1,0:T(8,128)(2,1)S(1)}, bf16[512,256]{1,0:T(8,128)(2,1)S(1)}, u32[]{:S(2)}, u32[]{:S(2)}) collective-permute-start(bf16[512,256]{1,0:T(8,128)(2,1)S(1)} %collective-permute-done.15.back1), channel_id=1, source_target_pairs={{0,24},{8,16},{16,40},{24,32},{32,56},{40,48},{48,72},{56,64},{64,... | collective-permute-start | bytes 786440 | tf_op jit(solution)/shard_map/ppermute | solution.py:343
  55.0 3.8 %collective-permute-start.19 = (bf16[512,256]{1,0:T(8,128)(2,1)S(1)}, bf16[512,256]{1,0:T(8,128)(2,1)S(1)}, u32[]{:S(2)}, u32[]{:S(2)}) collective-permute-start(bf16[512,256]{1,0:T(8,128)(2,1)S(1)} %collective-permute-done.18.opposite), channel_id=1, source_target_pairs={{0,32},{8,40},{32,64},{40,72},{64,96},{72,104},{128,160},{136,168}... | collective-permute-start | bytes 786440 | tf_op jit(solution)/shard_map/ppermute | solution.py:343
  60.0 1.6 %attend_early.1.before = f32[2,512,256]{2,1,0:T(8,128)S(1)} custom-call(s32[35]{0:T(128)S(1)} %pad_add_fusion.ids, bf16[512,256]{1,0:T(8,128)(2,1)S(1)} %query_rotate.1.query, bf16[512,256]{1,0:T(8,128)(2,1)S(1)} %keyval_rotate.1.own, bf16[512,256]{1,0:T(8,128)(2,1)S(1)} %collective-permute-done.15.back1, bf16[512,256]{1,0:T(8,128)(2,1)S(1)} %collective-permute-done.16.back2), custom_call_target="tpu_custom_call" | custom-call | flops 2147483648 | bytes 1048576 | tf_op jit(solution)/shard_map/attend_early/pallas_call | solution.py:41
  61.6 1.7 %collective-permute-done.19.raised = bf16[512,256]{1,0:T(8,128)(2,1)S(1)} collective-permute-done((bf16[512,256]{1,0:T(8,128)(2,1)S(1)}, bf16[512,256]{1,0:T(8,128)(2,1)S(1)}, u32[]{:S(2)}, u32[]{:S(2)}) %collective-permute-start.19) | collective-permute-done | bytes 262176 | tf_op jit(solution)/shard_map/ppermute | solution.py:343
  63.2 2.8 %collective-permute-done.17.pair = bf16[512,256]{1,0:T(8,128)(2,1)S(1)} collective-permute-done((bf16[512,256]{1,0:T(8,128)(2,1)S(1)}, bf16[512,256]{1,0:T(8,128)(2,1)S(1)}, u32[]{:S(2)}, u32[]{:S(2)}) %collective-permute-start.17) | collective-permute-done | bytes 262176 | tf_op jit(solution)/shard_map/ppermute | solution.py:343
  66.1 2.2 %attend_late.1 = bf16[8,144,256]{2,1,0:T(8,128)(2,1)S(1)} custom-call(s32[35]{0:T(128)S(1)} %pad_add_fusion.ids, bf16[512,256]{1,0:T(8,128)(2,1)S(1)} %query_rotate.1.query, bf16[512,256]{1,0:T(8,128)(2,1)S(1)} %collective-permute-done.17.pair, bf16[512,256]{1,0:T(8,128)(2,1)S(1)} %keyval_rotate.1.own, bf16[512,256]{1,0:T(8,128)(2,1)S(1)} %collective-permute-done.15.back1, ...), custom_call_target="tpu_custom_call" | custom-call | flops 2147483648 | bytes 1048576 | tf_op jit(solution)/shard_map/attend_late/pallas_call | solution.py:41
  68.3 12.9 %all_to_all.5.pieces = bf16[8,144,256]{2,1,0:T(8,128)(2,1)S(1)} all-to-all(bf16[8,144,256]{2,1,0:T(8,128)(2,1)S(1)} %attend_late.1), channel_id=1, replica_groups=mesh['z'=8,'xh'=2,'xl'=2,'row'=4,'col'=2] {'xl','row'}, dimensions={0} | all-to-all | bytes 1179648 | tf_op jit(solution)/shard_map/all_to_all | solution.py:481
  81.2 1.5 %finish.1 = bf16[128,1024]{1,0:T(8,128)(2,1)} custom-call(s32[35]{0:T(128)S(1)} %pad_add_fusion.ids, bf16[8,144,256]{2,1,0:T(8,128)(2,1)S(1)} %all_to_all.5.pieces), custom_call_target="tpu_custom_call" | custom-call | bytes 1048576 | tf_op jit(solution)/shard_map/finish/pallas_call | solution.py:41
  (31 shorter events, 5.2 us)
Async XLA Ops:
  0.0 2.5 %collective-permute-start = (bf16[128,2304]{1,0:T(8,128)(2,1)}, bf16[128,2304]{1,0:T(8,128)(2,1)S(1)}, u32[]{:S(2)}, u32[]{:S(2)}) collective-permute-start(bf16[128,2304]{1,0:T(8,128)(2,1)} %param.5), channel_id=1, source_target_pairs={{0,1},{1,0},{2,3},{3,2},{4,5},{5,4},{6,7},{7,6},{8,9},{9,8},{10,11... | collective-permute-start | bytes 1769480 | tf_op jit(solution)/shard_map/ppermute | solution.py:377
  3.4 8.3 %collective-permute-start.1 = (bf16[64,1152]{1,0:T(8,128)(2,1)S(1)}, bf16[64,1152]{1,0:T(8,128)(2,1)S(1)}, u32[]{:S(2)}, u32[]{:S(2)}) collective-permute-start(bf16[64,1152]{1,0:T(8,128)(2,1)S(1)} %get-tuple-element.67), channel_id=1, source_target_pairs={{0,2},{2,4},{4,6},{6,0},{1,3},{3,5},{5,7},{7,1},{8,10},{10,12},{12... | collective-permute-start | bytes 442376 | tf_op jit(solution)/shard_map/ppermute | solution.py:373
  5.0 10.3 %collective-permute-start.2 = (bf16[64,1152]{1,0:T(8,128)(2,1)S(1)}, bf16[64,1152]{1,0:T(8,128)(2,1)S(1)}, u32[]{:S(2)}, u32[]{:S(2)}) collective-permute-start(bf16[64,1152]{1,0:T(8,128)(2,1)S(1)} %get-tuple-element.68), channel_id=1, source_target_pairs={{0,4},{2,6},{4,0},{6,2},{1,5},{3,7},{5,1},{7,3},{8,12},{10,14},{12... | collective-permute-start | bytes 442376 | tf_op jit(solution)/shard_map/ppermute | solution.py:373
  7.9 7.4 %collective-permute-start.3 = (bf16[64,1152]{1,0:T(8,128)(2,1)S(1)}, bf16[64,1152]{1,0:T(8,128)(2,1)S(1)}, u32[]{:S(2)}, u32[]{:S(2)}) collective-permute-start(bf16[64,1152]{1,0:T(8,128)(2,1)S(1)} %get-tuple-element.69), channel_id=1, source_target_pairs={{0,6},{2,0},{4,2},{6,4},{1,7},{3,1},{5,3},{7,5},{8,14},{10,8},{12,... | collective-permute-start | bytes 442376 | tf_op jit(solution)/shard_map/ppermute | solution.py:373
  11.6 5.4 %collective-permute-start.4 = (bf16[64,1152]{1,0:T(8,128)(2,1)S(1)}, bf16[64,1152]{1,0:T(8,128)(2,1)S(1)}, u32[]{:S(2)}, u32[]{:S(2)}) collective-permute-start(bf16[64,1152]{1,0:T(8,128)(2,1)S(1)} %get-tuple-element.100.refs_0_), channel_id=1, source_target_pairs={{0,1},{1,0},{2,3},{3,2},{4,5},{5,4},{6,7},{7,6},{8,9},{9,8},{10,11... | collective-permute-start | bytes 442376 | tf_op jit(solution)/shard_map/ppermute | solution.py:377
  15.3 1.6 %collective-permute-start.5 = (bf16[64,1152]{1,0:T(8,128)(2,1)S(1)}, bf16[64,1152]{1,0:T(8,128)(2,1)S(1)}, u32[]{:S(2)}, u32[]{:S(2)}) collective-permute-start(bf16[64,1152]{1,0:T(8,128)(2,1)S(1)} %collective-permute-done.1.refs_1_), channel_id=1, source_target_pairs={{0,1},{1,0},{2,3},{3,2},{4,5},{5,4},{6,7},{7,6},{8,9},{9,8},{10,11... | collective-permute-start | bytes 442376 | tf_op jit(solution)/shard_map/ppermute | solution.py:377
  15.3 1.6 %collective-permute-start.6 = (bf16[64,1152]{1,0:T(8,128)(2,1)S(1)}, bf16[64,1152]{1,0:T(8,128)(2,1)S(1)}, u32[]{:S(2)}, u32[]{:S(2)}) collective-permute-start(bf16[64,1152]{1,0:T(8,128)(2,1)S(1)} %collective-permute-done.2.refs_2_), channel_id=1, source_target_pairs={{0,1},{1,0},{2,3},{3,2},{4,5},{5,4},{6,7},{7,6},{8,9},{9,8},{10,11... | collective-permute-start | bytes 442376 | tf_op jit(solution)/shard_map/ppermute | solution.py:377
  15.8 1.4 %collective-permute-start.7 = (bf16[64,1152]{1,0:T(8,128)(2,1)S(1)}, bf16[64,1152]{1,0:T(8,128)(2,1)S(1)}, u32[]{:S(2)}, u32[]{:S(2)}) collective-permute-start(bf16[64,1152]{1,0:T(8,128)(2,1)S(1)} %collective-permute-done.3.refs_3_), channel_id=1, source_target_pairs={{0,1},{1,0},{2,3},{3,2},{4,5},{5,4},{6,7},{7,6},{8,9},{9,8},{10,11... | collective-permute-start | bytes 442376 | tf_op jit(solution)/shard_map/ppermute | solution.py:377
  18.3 6.9 %collective-permute-start.8 = (bf16[512,128]{1,0:T(8,128)(2,1)S(1)}, bf16[512,128]{1,0:T(8,128)(2,1)S(1)}, u32[]{:S(2)}, u32[]{:S(2)}) collective-permute-start(bf16[512,128]{1,0:T(8,128)(2,1)S(1)} %bitcast.24), channel_id=1, source_target_pairs={{0,2},{2,4},{4,6},{6,0},{1,3},{3,5},{5,7},{7,1},{8,10},{10,12},{12... | collective-permute-start | bytes 393224 | tf_op jit(solution)/shard_map/ppermute | solution.py:373
  19.6 5.6 %collective-permute-start.9 = (bf16[512,128]{1,0:T(8,128)(2,1)S(1)}, bf16[512,128]{1,0:T(8,128)(2,1)S(1)}, u32[]{:S(2)}, u32[]{:S(2)}) collective-permute-start(bf16[512,128]{1,0:T(8,128)(2,1)S(1)} %bitcast.23), channel_id=1, source_target_pairs={{0,6},{2,0},{4,2},{6,4},{1,7},{3,1},{5,3},{7,5},{8,14},{10,8},{12,... | collective-permute-start | bytes 393224 | tf_op jit(solution)/shard_map/ppermute | solution.py:373
  21.8 7.3 %copy-start = (bf16[1152,1024]{1,0:T(8,128)(2,1)S(1)}, bf16[1152,1024]{1,0:T(8,128)(2,1)}, u32[]{:S(2)}) copy-start(bf16[1152,1024]{1,0:T(8,128)(2,1)} %refs_8_.1) | copy-start | bytes 7077892
  25.8 8.9 %collective-permute-start.10 = (bf16[512,256]{1,0:T(8,128)(2,1)S(1)}, bf16[512,256]{1,0:T(8,128)(2,1)S(1)}, u32[]{:S(2)}, u32[]{:S(2)}) collective-permute-start(bf16[512,256]{1,0:T(8,128)(2,1)S(1)} %get-tuple-element.113), channel_id=1, source_target_pairs={{0,2},{2,4},{4,6},{6,0},{1,3},{3,5},{5,7},{7,1},{8,10},{10,12},{12... | collective-permute-start | bytes 786440 | tf_op jit(solution)/shard_map/ppermute | solution.py:373
  27.0 7.8 %collective-permute-start.11 = (bf16[512,256]{1,0:T(8,128)(2,1)S(1)}, bf16[512,256]{1,0:T(8,128)(2,1)S(1)}, u32[]{:S(2)}, u32[]{:S(2)}) collective-permute-start(bf16[512,256]{1,0:T(8,128)(2,1)S(1)} %get-tuple-element.114), channel_id=1, source_target_pairs={{0,6},{2,0},{4,2},{6,4},{1,7},{3,1},{5,3},{7,5},{8,14},{10,8},{12,... | collective-permute-start | bytes 786440 | tf_op jit(solution)/shard_map/ppermute | solution.py:373
  35.4 12.5 %collective-permute-start.15 = (bf16[512,256]{1,0:T(8,128)(2,1)S(1)}, bf16[512,256]{1,0:T(8,128)(2,1)S(1)}, u32[]{:S(2)}, u32[]{:S(2)}) collective-permute-start(bf16[512,256]{1,0:T(8,128)(2,1)S(1)} %keyval_rotate.1.own), channel_id=1, source_target_pairs={{0,32},{8,40},{16,48},{24,56},{32,64},{40,72},{48,80},{56,88},{64,... | collective-permute-start | bytes 786440 | tf_op jit(solution)/shard_map/ppermute | solution.py:343
  39.3 15.7 %collective-permute-start.18 = (bf16[512,256]{1,0:T(8,128)(2,1)S(1)}, bf16[512,256]{1,0:T(8,128)(2,1)S(1)}, u32[]{:S(2)}, u32[]{:S(2)}) collective-permute-start(bf16[512,256]{1,0:T(8,128)(2,1)S(1)} %keyval_rotate.1.own), channel_id=1, source_target_pairs={{0,24},{8,16},{16,8},{24,0},{32,56},{40,48},{48,40},{56,32},{64,88... | collective-permute-start | bytes 786440 | tf_op jit(solution)/shard_map/ppermute | solution.py:343
  42.1 10.5 %collective-permute-start.12 = (bf16[512,256]{1,0:T(8,128)(2,1)S(1)}, bf16[512,256]{1,0:T(8,128)(2,1)S(1)}, u32[]{:S(2)}, u32[]{:S(2)}) collective-permute-start(bf16[512,256]{1,0:T(8,128)(2,1)S(1)} %bitcast.22), channel_id=1, source_target_pairs={{0,4},{2,6},{4,0},{6,2},{1,5},{3,7},{5,1},{7,3},{8,12},{10,14},{12... | collective-permute-start | bytes 786440 | tf_op jit(solution)/shard_map/ppermute | solution.py:373
  44.7 14.1 %collective-permute-start.13 = (bf16[512,256]{1,0:T(8,128)(2,1)S(1)}, bf16[512,256]{1,0:T(8,128)(2,1)S(1)}, u32[]{:S(2)}, u32[]{:S(2)}) collective-permute-start(bf16[512,256]{1,0:T(8,128)(2,1)S(1)} %bitcast.21), channel_id=1, source_target_pairs={{0,2},{2,4},{4,6},{6,0},{1,3},{3,5},{5,7},{7,1},{8,10},{10,12},{12... | collective-permute-start | bytes 786440 | tf_op jit(solution)/shard_map/ppermute | solution.py:373
  45.9 12.9 %collective-permute-start.14 = (bf16[512,256]{1,0:T(8,128)(2,1)S(1)}, bf16[512,256]{1,0:T(8,128)(2,1)S(1)}, u32[]{:S(2)}, u32[]{:S(2)}) collective-permute-start(bf16[512,256]{1,0:T(8,128)(2,1)S(1)} %bitcast.20), channel_id=1, source_target_pairs={{0,6},{2,0},{4,2},{6,4},{1,7},{3,1},{5,3},{7,5},{8,14},{10,8},{12,... | collective-permute-start | bytes 786440 | tf_op jit(solution)/shard_map/ppermute | solution.py:373
  48.0 10.9 %collective-permute-start.16 = (bf16[512,256]{1,0:T(8,128)(2,1)S(1)}, bf16[512,256]{1,0:T(8,128)(2,1)S(1)}, u32[]{:S(2)}, u32[]{:S(2)}) collective-permute-start(bf16[512,256]{1,0:T(8,128)(2,1)S(1)} %collective-permute-done.15.back1), channel_id=1, source_target_pairs={{0,32},{8,40},{16,48},{24,56},{32,64},{40,72},{48,80},{56,88},{64,... | collective-permute-start | bytes 786440 | tf_op jit(solution)/shard_map/ppermute | solution.py:343
  52.6 10.7 %collective-permute-start.20 = (bf16[512,256]{1,0:T(8,128)(2,1)S(1)}, bf16[512,256]{1,0:T(8,128)(2,1)S(1)}, u32[]{:S(2)}, u32[]{:S(2)}) collective-permute-start(bf16[512,256]{1,0:T(8,128)(2,1)S(1)} %collective-permute-done.15.back1), channel_id=1, source_target_pairs={{0,24},{8,16},{16,40},{24,32},{32,56},{40,48},{48,72},{56,64},{64,... | collective-permute-start | bytes 786440 | tf_op jit(solution)/shard_map/ppermute | solution.py:343
  55.0 8.3 %collective-permute-start.19 = (bf16[512,256]{1,0:T(8,128)(2,1)S(1)}, bf16[512,256]{1,0:T(8,128)(2,1)S(1)}, u32[]{:S(2)}, u32[]{:S(2)}) collective-permute-start(bf16[512,256]{1,0:T(8,128)(2,1)S(1)} %collective-permute-done.18.opposite), channel_id=1, source_target_pairs={{0,32},{8,40},{32,64},{40,72},{64,96},{72,104},{128,160},{136,168}... | collective-permute-start | bytes 786440 | tf_op jit(solution)/shard_map/ppermute | solution.py:343
  59.6 6.5 %collective-permute-start.17 = (bf16[512,256]{1,0:T(8,128)(2,1)S(1)}, bf16[512,256]{1,0:T(8,128)(2,1)S(1)}, u32[]{:S(2)}, u32[]{:S(2)}) collective-permute-start(bf16[512,256]{1,0:T(8,128)(2,1)S(1)} %query_rotate.1.query), channel_id=1, source_target_pairs={{0,8},{8,0},{16,24},{24,16},{32,40},{40,32},{48,56},{56,48},{64,72... | collective-permute-start | bytes 786440 | tf_op jit(solution)/shard_map/ppermute | solution.py:343
